TPU v7x, 32 devices: a whole 2x2x4 slice. The times are simulated.
32 devices in a mesh: rep: 4 (over z), fsdp: 8 (over y, x, core).
Axes of the slice: x: 2, y: 2, z: 4, core: 2. Of those that a mesh axis runs over, the one named last changes fastest.
Arguments:
- tokens: bfloat16 [4, 8, 2048, 1024], P('rep', None, 'fsdp'), may hold values from -6 to 6
- cotangent: bfloat16 [4, 8, 2048, 1024], P('rep', None, 'fsdp'), may hold values from -6 to 6
- lengths: int32 [4, 8], P('rep'), may hold values from 1 to 2048, 8192 in all within a row
- dealing: int32 [4, 8], P('rep'), may hold values from 0 to 7, each once within a row
- norm_gain: bfloat16 [1024], P('fsdp'), may hold values from 0.5 to 1.5
- in_weight: bfloat16 [1024, 4384], P('fsdp'), may hold values from -0.1875 to 0.1875
- conv_weight: bfloat16 [4, 2304], P(None, 'fsdp'), may hold values from -3 to 3
- conv_bias: bfloat16 [2304], P('fsdp'), may hold values from -3 to 3
- dt_bias: float32 [32], replicated, may hold values from -5 to -1
- a_log: float32 [32], replicated, may hold values from -3 to 1
- skip_gain: float32 [32], replicated, may hold values from 0.5 to 2
- out_gain: bfloat16 [2048], P('fsdp'), may hold values from 0.5 to 1.5
- out_weight: bfloat16 [2048, 1024], P('fsdp'), may hold values from -0.125 to 0.125
Outputs:
- output: bfloat16 [4, 8, 2048, 1024], P('rep', None, 'fsdp')
- token_grad: bfloat16 [4, 8, 2048, 1024], P('rep', None, 'fsdp')
- norm_gain_grad: float32 [1024], P('fsdp')
- in_weight_grad: float32 [1024, 4384], P('fsdp')
- conv_weight_grad: float32 [4, 2304], P(None, 'fsdp')
- conv_bias_grad: float32 [2304], P('fsdp')
- dt_bias_grad: float32 [32], replicated
- a_log_grad: float32 [32], replicated
- skip_gain_grad: float32 [32], replicated
- out_gain_grad: float32 [2048], P('fsdp')
- out_weight_grad: float32 [2048, 1024], P('fsdp')
Inputs may be any that keep to these rules, and one draw needn't show every extreme that they name: Each group's lengths sum to 8192 and one of them is exactly 2048. `dealing`: each group's row is a permutation of the dealt positions.
All inputs are finite; a program needn't handle non-finite values.
Results may differ from a plain program's by a relative error of at most 0.007.
Values may be sent and summed in bfloat16 or wider, within the bound.
A program may use at most 448 MiB of HBM per device.

v0:
```python
import jax
import jax.numpy as jnp
from jax import lax
from jax.sharding import PartitionSpec as P

STATE = 128
HEADS = 32
HEADDIM = 64
CONV = 4
SPAN = 256
INNER = 2048


epsilon = 1e-05
largest_value = lax.Precision.HIGHEST


def front_norm(hidden, gain):
    return hidden * lax.rsqrt(jnp.mean(hidden * hidden, axis=-1, keepdims=True) + epsilon) * gain


def block_step(state, block):
    values, state_in, state_out, step_sizes, log_decay = block
    width = values.shape[0]
    summed = jnp.cumsum(log_decay, axis=1)
    causal = (jnp.arange(width)[:, None] >= jnp.arange(width)[None, :])[None]
    gaps = summed[:, :, None] - summed[:, None, :]
    decay = jnp.where(causal, jnp.exp(jnp.where(causal, gaps, 0.0)), 0.0)
    intersection = jnp.dot(state_out, state_in.T, precision=largest_value)
    weights = intersection[None] * decay * step_sizes[:, None, :]
    by_head = values.reshape(width, HEADS, HEADDIM)
    inside = jnp.einsum("hts,shp->thp", weights, by_head, precision=largest_value)
    carried = jnp.exp(summed).T[:, :, None] * jnp.einsum(
        "tn,hpn->thp", state_out, state, precision=largest_value
    )
    last_sum = summed[:, -1]
    tail = jnp.exp(last_sum[:, None] - summed) * step_sizes
    update = jnp.einsum(
        "shp,sn->hpn", tail.T[:, :, None] * by_head, state_in, precision=largest_value
    )
    fresh = jnp.exp(last_sum)[:, None, None] * state + update
    return (fresh, (inside + carried).reshape(width, HEADS * HEADDIM))


def scan_blocks(values, state_in, state_out, step_sizes, log_decay):
    length = values.shape[0]
    count = length // SPAN
    blocks = (
        values.reshape(count, SPAN, INNER),
        state_in.reshape(count, SPAN, STATE),
        state_out.reshape(count, SPAN, STATE),
        step_sizes.reshape(HEADS, count, SPAN).transpose(1, 0, 2),
        log_decay.reshape(HEADS, count, SPAN).transpose(1, 0, 2),
    )
    start = jnp.zeros((HEADS, HEADDIM, STATE), jnp.float32)
    final, outputs = lax.scan(jax.checkpoint(block_step), start, blocks)
    return outputs.reshape(length, INNER)


def middle_part(main_proj, raw_steps, conv_w, conv_b, step_bias, decay_log, direct, gated_gain):
    length = main_proj.shape[0]
    channels = INNER + 2 * STATE
    gate = main_proj[:, :INNER]
    conv_in = main_proj[:, INNER : INNER + channels]
    padded = jnp.concatenate([jnp.zeros((CONV - 1, channels), jnp.float32), conv_in], axis=0)
    mixed = jnp.zeros((length, channels), jnp.float32) + conv_b
    for offset in range(CONV):
        mixed = mixed + conv_w[offset] * padded[offset : offset + length]
    mixed = jax.nn.silu(mixed)
    values = mixed[:, :INNER]
    state_in = mixed[:, INNER : INNER + STATE]
    state_out = mixed[:, INNER + STATE :]
    step_sizes = jax.nn.softplus(raw_steps + step_bias[:, None])
    log_decay = -step_sizes * jnp.exp(decay_log)[:, None]
    direct_wide = jnp.repeat(direct, HEADDIM)
    result = (
        scan_blocks(values, state_in, state_out, step_sizes, log_decay)
        + direct_wide[None, :] * values
    )
    result = result * jax.nn.silu(gate)
    return front_norm(result, gated_gain)


def middle_all(main_proj, raw_steps, conv_w, conv_b, step_bias, decay_log, direct, gated_gain):
    return jax.vmap(middle_part, in_axes=(0, 0, None, None, None, None, None, None))(
        main_proj, raw_steps, conv_w, conv_b, step_bias, decay_log, direct, gated_gain
    )


def body(
    tokens,
    cotangent,
    lengths,
    dealing,
    norm_gain,
    in_weight,
    conv_weight,
    conv_bias,
    dt_bias,
    a_log,
    skip_gain,
    out_gain,
    out_weight,
):
    local_tokens = tokens[0]
    local_grad = cotangent[0]
    order = dealing[0]
    count = order.shape[0]
    slots = jnp.arange(count, dtype=jnp.int32)
    inverse = jnp.sum(jnp.where(order[None, :] == slots[:, None], slots[None, :], 0), axis=1)
    sent_tokens = jnp.take(local_tokens, inverse, axis=0)
    sent_grad = jnp.take(local_grad, inverse, axis=0)
    dealt_tokens, dealt_grad = (
        lax.all_to_all(sent_tokens, "fsdp", split_axis=0, concat_axis=1, tiled=True),
        lax.all_to_all(sent_grad, "fsdp", split_axis=0, concat_axis=1, tiled=True),
    )
    per_device = dealt_tokens.shape[0]
    length = dealt_tokens.shape[1]
    width = dealt_tokens.shape[2]
    first = lax.axis_index("fsdp") * per_device
    own_lengths = lax.dynamic_slice_in_dim(lengths[0], first, per_device)
    keep = (jnp.arange(length, dtype=jnp.int32)[None, :] < own_lengths[:, None]).reshape(-1, 1)
    main_cols = in_weight.shape[1] - HEADS
    in_main_shard = in_weight[:, :main_cols]
    in_step_shard = in_weight[:, main_cols:]
    gathered = (
        lax.all_gather(norm_gain, "fsdp", axis=0, tiled=True),
        lax.all_gather(in_main_shard, "fsdp", axis=0, tiled=True),
        lax.all_gather(in_step_shard, "fsdp", axis=0, tiled=True),
        lax.all_gather(conv_weight, "fsdp", axis=1, tiled=True),
        lax.all_gather(conv_bias, "fsdp", axis=0, tiled=True),
        lax.all_gather(out_gain, "fsdp", axis=0, tiled=True),
        lax.all_gather(out_weight, "fsdp", axis=0, tiled=True),
    )
    first_gain, weight_main, weight_stride, conv_w, conv_b, gated_gain, weight_out = gathered
    hidden = dealt_tokens.reshape(-1, width).astype(jnp.float32)
    normed_full, front_back = jax.vjp(front_norm, hidden, first_gain.astype(jnp.float32))
    normalized_rows = normed_full.astype(jnp.bfloat16)
    normalized_sequence = normalized_rows.reshape(per_device, length, width)
    main_proj = jnp.dot(normalized_rows, weight_main, preferred_element_type=jnp.float32)
    raw_steps = jnp.einsum(
        "ew,yme->ywm", weight_stride, normalized_sequence, preferred_element_type=jnp.float32
    )
    mixed_full, middle_back = jax.vjp(
        middle_all,
        main_proj.reshape(per_device, length, main_cols),
        raw_steps,
        conv_w.astype(jnp.float32),
        conv_b.astype(jnp.float32),
        dt_bias,
        a_log,
        skip_gain,
        gated_gain.astype(jnp.float32),
    )
    mixed = mixed_full.reshape(-1, INNER).astype(jnp.bfloat16)
    branch = (
        jnp.dot(mixed, weight_out, preferred_element_type=jnp.float32) * keep.astype(jnp.float32)
    ).astype(jnp.bfloat16)
    back_main, backward_stride, back_out = (
        lax.all_gather(in_main_shard, "fsdp", axis=0, tiled=True),
        lax.all_gather(in_step_shard, "fsdp", axis=0, tiled=True),
        lax.all_gather(out_weight, "fsdp", axis=0, tiled=True),
    )
    grad_branch = dealt_grad.reshape(-1, width) * keep.astype(jnp.bfloat16)
    grad_out_weight = jnp.einsum(
        "rk,rd->kd", mixed, grad_branch, preferred_element_type=jnp.float32
    )
    grad_mixed = jnp.einsum("rd,kd->rk", grad_branch, back_out, preferred_element_type=jnp.float32)
    middle_grads = middle_back(grad_mixed.reshape(per_device, length, INNER))
    grad_main = middle_grads[0].reshape(-1, main_cols).astype(jnp.bfloat16)
    gradient_stride_list = middle_grads[1].astype(jnp.bfloat16)
    grad_in_main = jnp.einsum(
        "rd,rp->dp", normalized_rows, grad_main, preferred_element_type=jnp.float32
    )
    grad_in_step = jnp.einsum(
        "yct,yjc->tj", normalized_sequence, gradient_stride_list, preferred_element_type=jnp.float32
    )
    grad_normed = jnp.einsum("rp,dp->rd", grad_main, back_main, preferred_element_type=jnp.float32)
    grad_normed = grad_normed + jnp.einsum(
        "uze,wz->uew", gradient_stride_list, backward_stride, preferred_element_type=jnp.float32
    ).reshape(-1, width)
    grad_hidden, grad_first_gain = front_back(grad_normed)
    returned_branch, returned_grad = (
        lax.all_to_all(
            branch.reshape(per_device, length, width),
            "fsdp",
            split_axis=1,
            concat_axis=0,
            tiled=True,
        ),
        lax.all_to_all(
            grad_hidden.astype(jnp.bfloat16).reshape(per_device, length, width),
            "fsdp",
            split_axis=1,
            concat_axis=0,
            tiled=True,
        ),
    )
    restored_branch = jnp.take(returned_branch, order, axis=0)
    restored_grad = jnp.take(returned_grad, order, axis=0)
    output = (local_tokens.astype(jnp.float32) + restored_branch.astype(jnp.float32)).astype(
        jnp.bfloat16
    )[None]
    token_grad = (local_grad.astype(jnp.float32) + restored_grad.astype(jnp.float32)).astype(
        jnp.bfloat16
    )[None]
    shards = (
        lax.psum_scatter(grad_first_gain, "fsdp", scatter_dimension=0, tiled=True),
        lax.psum_scatter(grad_in_main, "fsdp", scatter_dimension=0, tiled=True),
        lax.psum_scatter(grad_in_step, "fsdp", scatter_dimension=0, tiled=True),
        lax.psum_scatter(middle_grads[2], "fsdp", scatter_dimension=1, tiled=True),
        lax.psum_scatter(middle_grads[3], "fsdp", scatter_dimension=0, tiled=True),
        lax.psum_scatter(middle_grads[7], "fsdp", scatter_dimension=0, tiled=True),
        lax.psum_scatter(grad_out_weight, "fsdp", scatter_dimension=0, tiled=True),
    )
    summed = lax.psum(
        (shards[0], shards[1], shards[2], shards[3], shards[4], shards[5], shards[6]), "rep"
    )
    small = lax.psum((middle_grads[4], middle_grads[5], middle_grads[6]), ("rep", "fsdp"))
    in_grad = jnp.concatenate([summed[1], summed[2]], axis=1)
    return (
        output,
        token_grad,
        summed[0],
        in_grad,
        summed[3],
        summed[4],
        small[0],
        small[1],
        small[2],
        summed[5],
        summed[6],
    )


def solution(mesh):
    in_specs = (
        P("rep", None, "fsdp", None),
        P("rep", None, "fsdp", None),
        P("rep", None),
        P("rep", None),
        P("fsdp"),
        P("fsdp", None),
        P(None, "fsdp"),
        P("fsdp"),
        P(),
        P(),
        P(),
        P("fsdp"),
        P("fsdp", None),
    )
    out_specs = (
        P("rep", None, "fsdp", None),
        P("rep", None, "fsdp", None),
        P("fsdp"),
        P("fsdp", None),
        P(None, "fsdp"),
        P("fsdp"),
        P(),
        P(),
        P(),
        P("fsdp"),
        P("fsdp", None),
    )
    return jax.shard_map(body, mesh=mesh, in_specs=in_specs, out_specs=out_specs, check_vma=False)
```

profile of v0, /device:TPU:0, one launch (start us, length us, event | category | flops | bytes accessed | tf_op | source)
XLA Modules:
  0.0 2188.5 jit_solution(4783930592136174851)
XLA Ops:
  27.2 78.3 %all_to_all.42 = bf16[8,256,1024]{2,1,0:T(8,128)(2,1)} all-to-all(bf16[8,256,1024]{2,1,0:T(8,128)(2,1)S(1)} %get-tuple-element.938), channel_id=1, replica_groups=mesh['rep'=4,'fsdp'=8] {'fsdp'}, dimensions={0} | all-to-all | bytes 8388608 | tf_op jit(solution)/shard_map/all_to_all | solution.py:114
  111.0 66.4 %all-gather = bf16[8,1,128]{2,1,0:T(2,128)(2,1)S(1)} all-gather(bf16[1,1,128]{2,1,0:T(2,128)(2,1)S(1)} %bitcast.661), channel_id=1, replica_groups=mesh['rep'=4,'fsdp'=8] {'fsdp'}, dimensions={0}, use_global_device_ids=true | all-gather | bytes 2304 | tf_op jit(solution)/shard_map/all_gather | solution.py:127
  187.7 13.4 all-reduce.15
  245.9 26.6 %convolution_bitcast_fusion.5 = f32[1,2048,4352]{2,1,0:T(8,128)} fusion(bf16[2048,1024]{1,0:T(8,128)(2,1)} %copy-done.11, bf16[1024,4352]{0,1:T(8,128)(2,1)} %all-gather.6.cloned.1.call-done), kind=kOutput, calls=%fused_computation.140 | convolution fusion | flops 18253611008 | bytes 48758784 | tf_op jit(solution)/shard_map/dot_general | solution.py:140
  272.5 14.4 slice.142
  286.9 32.5 %fusion.83 = (f32[1,2048,2304]{2,1,0:T(8,128)S(1)}, f32[1,2048,2304]{2,1,0:T(8,128)}) fusion(f32[1,2048,2304]{2,1,0:T(8,128)} %slice.142, f32[2304]{0:T(1024)S(1)} %get-tuple-element.836, f32[2304]{0:T(1024)S(1)} %get-tuple-element.837, f32[2304]{0:T(1024)S(1)} %get-tuple-element.838, f32[2304]{0:T(1024)S(1)} %get-tuple-element.835, ...), kind=kLoop, calls=%fused_computation.151 | loop fusion | flops 56623104 | bytes 56669184 | tf_op jit(solution)/shard_map/jvp(vmap(jit(silu)))/mul | solution.py:69
  331.3 16.4 copy.270
  355.6 251.9 %while.44 = (s32[]{:T(128)}, f32[1,32,64,128]{3,2,1,0:T(8,128)S(1)}, f32[8,1,256,2048]{3,2,0,1:T(8,128)}, f32[8,1,32,64,128]{4,3,2,1,0:T(8,128)}, f32[8,1,32,256...) while((s32[]{:T(128)}, ...), condition=%wide.region_5.7_spmd.clone.clone, body=%wide.region_2.0_spmd.clone.clone.sunk | while | flops 3336331264 | bytes 36804896 | solution.py:56
  367.8 11.1 bitcast_add_fusion.18
  399.3 11.1 bitcast_add_fusion.18
  430.7 11.1 bitcast_add_fusion.18
  462.2 11.1 bitcast_add_fusion.18
  493.7 11.1 bitcast_add_fusion.18
  525.2 11.1 bitcast_add_fusion.18
  556.6 11.1 bitcast_add_fusion.18
  588.1 11.1 bitcast_add_fusion.18
  607.5 23.7 %multiply_reduce_fusion.9 = (f32[2048]{0:T(1024)S(1)}, f32[1,2048,2048]{2,1,0:T(8,128)}) fusion(f32[1,2048,4352]{2,1,0:T(8,128)} %convolution_bitcast_fusion.5, f32[1,2048,2304]{2,1,0:T(8,128)} %copy-done.5, f32[2048]{0:T(1024)S(1)} %copy-done.25, f32[8,1,256,2048]{3,2,0,1:T(8,128)} %get-tuple-element.422), kind=kLoop, calls=%fused_computation.166 | loop fusion | flops 37746688 | bytes 67125248 | tf_op jit(solution)/shard_map/jvp(vmap())/reduce_sum | solution.py:19
  631.3 19.4 fusion.87
  650.7 40.6 %multiply_reduce_fusion.8 = (f32[2048]{0:T(1024)}, f32[1,2048,2048]{2,1,0:T(8,128)}, f32[1,2048,2048]{2,1,0:T(8,128)}) fusion(f32[1,2048,2304]{2,1,0:T(8,128)} %copy-done.5, f32[1,2048,4352]{2,1,0:T(8,128)} %convolution_bitcast_fusion.5, f32[1,2048,2048]{2,1,0:T(8,128)} %get-tuple-element.912, f32[2048]{0:T(1024)S(1)} %multiply_multiply_fusion.1, ...), kind=kLoop, calls=%fused_computation.164 | loop fusion | flops 88078336 | bytes 117481472 | tf_op jit(solution)/shard_map/transpose(jvp(vmap()))/reduce_sum | solution.py:78
  703.2 879.3 %while.43 = (s32[]{:T(128)}, f32[1,32,64,128]{3,2,1,0:T(8,128)}, f32[8,1,256,2048]{3,2,0,1:T(8,128)}, f32[8,1,256,128]{3,2,0,1:T(8,128)}, f32[8,1,256,128]{3,2,1...) while((s32[]{:T(128)}, f32[1,32,64,128]{3,2,1,0:T(8,128)}, ...), condition=%wide.region_21.23_spmd.clone, body=%wide.region_8.22_spmd.clone.sunk | while | flops 7599472640 | bytes 94608200 | solution.py:56
  727.8 16.5 fusion.224
  786.9 10.2 bitcast_add_fusion.16
  837.9 16.5 fusion.224
  896.9 10.2 bitcast_add_fusion.16
  947.9 16.5 fusion.224
  1057.8 16.5 fusion.224
  1167.8 16.5 fusion.224
  1226.8 10.2 bitcast_add_fusion.16
  1277.8 16.5 fusion.224
  1387.8 16.5 fusion.224
  1497.8 16.5 fusion.224
  1582.5 18.3 bitcast_add_fusion.6
  1605.3 12.1 fusion.127
  1618.9 49.7 %multiply_reduce_fusion.6 = (f32[2304]{0:T(1024)}, f32[2304]{0:T(1024)}, f32[2304]{0:T(1024)}, f32[2304]{0:T(1024)}, f32[2304]{0:T(1024)}, /*index=5*/f32[1,2048,2304]{2,1,0:T(8,128)}) fusion(f32[1,2048,2304]{2,1,0:T(8,128)} %slice.142, f32[1,2048,4352]{2,1,0:T(8,128)} %convolution_bitcast_fusion.5, f32[1,2048,2304]{2,1,0:T(8,128)} %get-tuple-element.914, ...), kind=kLoop, calls=%fused_computation.148 | loop fusion | flops 94360320 | bytes 94417920 | tf_op jit(solution)/shard_map/transpose(jvp(vmap()))/reduce_sum | solution.py:68
  1668.7 30.9 %broadcast_multiply_fusion = (f32[1,2048,2304]{2,1,0:T(8,128)}, f32[1,2048,2304]{2,1,0:T(8,128)}, f32[1,2048,2304]{2,1,0:T(8,128)}, f32[1,2048,2304]{2,1,0:T(8,128)}) fusion(f32[1,2048,2304]{2,1,0:T(8,128)} %get-tuple-element.910, f32[2304]{0:T(1024)S(1)} %copy-done.30, f32[2304]{0:T(1024)S(1)} %copy-done.28, f32[2304]{0:T(1024)S(1)} %copy-done.34, ...), kind=kLoop, calls=%fused_computation.170 | loop fusion | flops 18874368 | bytes 94408704 | tf_op jit(solution)/shard_map/transpose(jvp(vmap()))/mul | solution.py:68
  1699.6 31.6 %pad_add_fusion = f32[1,2048,2304]{2,1,0:T(8,128)} fusion(f32[1,2048,2304]{2,1,0:T(8,128)} %get-tuple-element.923, f32[1,2048,2304]{2,1,0:T(8,128)} %get-tuple-element.924, f32[1,2048,2304]{2,1,0:T(8,128)} %get-tuple-element.925, f32[1,2048,2304]{2,1,0:T(8,128)} %get-tuple-element.922), kind=kLoop, calls=%fused_computation.143 | loop fusion | flops 14155776 | bytes 94371840 | tf_op jit(solution)/shard_map/transpose(jvp(vmap()))/add_any | solution.py:68
  1731.2 29.8 %fusion.105 = f32[1024,4352]{1,0:T(8,128)} fusion(bf16[2048,1024]{1,0:T(8,128)(2,1)S(1)} %bitcast.629, f32[1,2048,2048]{2,1,0:T(8,128)} %get-tuple-element.921, f32[1,2048,2304]{2,1,0:T(8,128)} %pad_add_fusion), kind=kOutput, calls=%fused_computation.201 | convolution fusion | flops 18271436800 | bytes 57671680 | tf_op jit(solution)/shard_map/rd,rp->dp/dot_general | solution.py:172
  1762.6 14.6 fusion.104
  1777.3 28.7 %copy.354 = bf16[1,2048,1024]{2,0,1:T(2,128)(2,1)} copy(bf16[1,2048,1024]{2,1,0:T(8,128)(2,1)S(1)} %fusion.104) | data formatting | bytes 8388608 | tf_op jit(solution)/shard_map/reshape | solution.py:185
  1806.5 26.0 %reduce.93 = bf16[2048,1024]{1,0:T(8,128)(2,1)} reduce(bf16[2048,1,1024]{2,1,0:T(2,128)(2,1)} %bitcast.611, bf16[]{:T(256)} %broadcast.591), dimensions={1}, to_apply=%bitcast.393.reduce_sub_computation | reduce | bytes 8388610
  1850.4 29.8 %fusion.95 = (f32[1024]{0:T(1024)S(1)}, f32[2048]{0:T(1024)S(1)}, f32[2048,1024]{1,0:T(8,128)}) fusion(bf16[8,256,1024]{2,1,0:T(8,128)(2,1)} %all_to_all.42, f32[2048]{0:T(1024)S(1)} %copy-done.36, f32[1024]{0:T(1024)S(1)} %bitcast.654, f32[2048,1024]{1,0:T(8,128)} %fusion.115, bf16[1024,4352]{0,1:T(8,128)(2,1)} %all-gather.6.cloned.1.call-done, ...), kind=kOutput, calls=%fused_computation.184 | convolution fusion | flops 18288211968 | bytes 65560576 | tf_op jit(solution)/shard_map/rp,dp->rd/dot_general | solution.py:178
  1885.8 28.7 %copy.353 = bf16[1,2048,1024]{2,0,1:T(2,128)(2,1)} copy(bf16[1,2048,1024]{2,1,0:T(8,128)(2,1)S(1)} %bitcast.617) | data formatting | bytes 8388608 | tf_op jit(solution)/shard_map/reshape | solution.py:192
  1914.5 26.0 %reduce.92 = bf16[2048,1024]{1,0:T(8,128)(2,1)} reduce(bf16[2048,1,1024]{2,1,0:T(2,128)(2,1)} %bitcast.612, bf16[]{:T(256)} %broadcast.591), dimensions={1}, to_apply=%bitcast.392.reduce_sub_computation | reduce | bytes 8388610
  1962.4 76.4 %all-reduce.19 = (f32[32]{0:T(128)}, f32[32]{0:T(128)}, f32[32]{0:T(128)}) all-reduce(f32[32]{0:T(128)S(1)} %get-tuple-element.908, f32[32]{0:T(128)S(1)} %exponential_multiply_fusion, f32[32]{0:T(128)S(1)} %reduce_sum.249), channel_id=1, replica_groups=mesh['rep'=4,'fsdp'=8] {'rep','fsdp'}, use_global_device_ids=true, to_apply=%region_40.42 | all-reduce | flops 96 | bytes 768 | tf_op jit(solution)/shard_map/psum | solution.py:219
  2038.8 23.8 %all-reduce.20 = (f32[1024]{0:T(1024)S(1)}, f32[2304]{0:T(1024)S(1)}, f32[2048]{0:T(1024)S(1)}) all-reduce(f32[1024]{0:T(1024)S(1)} %get-tuple-element.833, f32[2304]{0:T(1024)S(1)} %copy-done.41, f32[2048]{0:T(1024)S(1)} %copy-done.51), channel_id=2, replica_groups=mesh['rep'=4,'fsdp'=8] {'fsdp'}, use_global_device_ids=true, to_apply=%region_24.26.clone | all-reduce | flops 5376 | bytes 43008
  2063.8 22.1 %all-reduce.21 = (f32[128]{0:T(128)}, f32[128,32]{1,0:T(8,128)S(1)}, f32[4,288]{1,0:T(4,128)}, f32[288]{0:T(512)}, f32[256]{0:T(256)}) all-reduce(f32[128]{0:T(128)S(1)} %dynamic-slice.3, f32[128,32]{1,0:T(8,128)} %reduce-scatter.9.cloned.1.call-done, f32[4,288]{1,0:T(4,128)S(1)} %copy.293, ...), channel_id=1, replica_groups=mesh['rep'=4,'fsdp'=8] {'rep'}, use_global_device_ids=true, to_apply=%region_25.27 | all-reduce | flops 5920 | bytes 47360 | tf_op jit(solution)/shard_map/psum | solution.py:216
  2127.7 10.7 fusion.103
  2138.4 38.2 %all-reduce.25.cloned.1.call-done = (f32[128,4352]{1,0:T(8,128)}, f32[256,1024]{1,0:T(8,128)}) async-done(((f32[128,4352]{1,0:T(8,128)}, f32[256,1024]{1,0:T(8,128)}), (f32[128,4352]{1,0:T(8,128)}, f32[256,1024]{1,0:T(8,128)})) %all-reduce.25.cloned.1.call-update) | async-done | bytes 3276816 | tf_op jit(solution)/shard_map/psum | solution.py:216
  (1066 shorter events, 1087.7 us)
Async XLA Ops:
  7.2 203.6 %copy-start = (s32[1,8]{1,0:T(1,128)S(1)}, s32[1,8]{1,0:T(1,128)}, u32[]{:S(2)}) copy-start(s32[1,8]{1,0:T(1,128)} %param.21) | copy-start | bytes 100
  7.2 238.7 %all-gather.6.cloned.1.call-start = ((), (), s32[]{:S(2)}) async-start(), calls=%async_computation.8 | async-start | bytes 10027008 | tf_op jit(solution)/shard_map/all_gather | solution.py:128
  27.2 83.8 %copy-start.58 = (bf16[128]{0:T(256)(128)(2,1)S(1)}, bf16[128]{0:T(256)(128)(2,1)}, u32[]{:S(2)}) copy-start(bf16[128]{0:T(256)(128)(2,1)} %param.23) | copy-start | bytes 772
  27.2 150.2 %copy-start.54 = (bf16[4,288]{1,0:T(4,128)(2,1)S(1)}, bf16[4,288]{1,0:T(4,128)(2,1)}, u32[]{:S(2)}) copy-start(bf16[4,288]{1,0:T(4,128)(2,1)} %param.25) | copy-start | bytes 6916
  27.2 159.0 %copy-start.56 = (u32[32]{0:T(128)S(1)}, u32[32]{0:T(128)}, u32[]{:S(2)}) copy-start(u32[32]{0:T(128)} %constant.185) | copy-start | bytes 388
  27.2 160.3 %copy-start.57 = (bf16[288]{0:T(512)(128)(2,1)S(1)}, bf16[288]{0:T(512)(128)(2,1)}, u32[]{:S(2)}) copy-start(bf16[288]{0:T(512)(128)(2,1)} %param.26) | copy-start | bytes 1732
  27.2 174.0 %copy-start.62 = (f32[32]{0:T(128)S(1)}, f32[32]{0:T(128)}, u32[]{:S(2)}) copy-start(f32[32]{0:T(128)} %param.28) | copy-start | bytes 388
  27.2 174.0 %copy-start.59 = (f32[32]{0:T(128)S(1)}, f32[32]{0:T(128)}, u32[]{:S(2)}) copy-start(f32[32]{0:T(128)} %param.29) | copy-start | bytes 388
  27.2 174.7 %copy-start.60 = (bf16[256]{0:T(256)(128)(2,1)S(1)}, bf16[256]{0:T(256)(128)(2,1)}, u32[]{:S(2)}) copy-start(bf16[256]{0:T(256)(128)(2,1)} %param.30) | copy-start | bytes 1540
  27.2 184.2 %slice-start = ((bf16[128,4384]{0,1:T(8,128)(2,1)}), bf16[128,32]{0,1:T(8,128)(2,1)S(1)}, s32[]{:S(2)}) async-start(bf16[128,4384]{0,1:T(8,128)(2,1)} %param.24), calls=%async_computation.15 | async-start | bytes 16384 | tf_op jit(solution)/shard_map/slice | solution.py:125
  105.5 131.3 %all-to-all-start.2 = ((bf16[8,256,1024]{2,1,0:T(8,128)(2,1)}), bf16[8,256,1024]{2,1,0:T(8,128)(2,1)}, u32[]{:S(2)}, u32[]{:S(2)}) async-start(bf16[8,256,1024]{2,1,0:T(8,128)(2,1)} %get-tuple-element.937), calls=%async_computation.2 | async-start | bytes 8388608 | tf_op jit(solution)/shard_map/all_to_all | solution.py:115
  110.1 120.5 %copy-start.55 = (f32[32]{0:T(128)S(1)}, f32[32]{0:T(128)}, u32[]{:S(2)}) copy-start(f32[32]{0:T(128)} %param.27) | copy-start | bytes 388
  110.1 521.1 %all-gather.8.cloned.1.call-start = ((), (), s32[]{:S(2)}) async-start(), calls=%async_computation.9 | async-start | bytes 4718592 | tf_op jit(solution)/shard_map/all_gather | solution.py:133
  110.9 1848.6 %reduce-scatter.11.cloned.1.call-start = ((), (), s32[]{:S(2)}) async-start(), calls=%async_computation.12 | async-start | bytes 9437184 | tf_op jit(solution)/shard_map/reduce_scatter | solution.py:214
  177.4 56.9 %copy-start.39 = (f32[8,1,128]{2,1,0:T(1,128)}, f32[8,1,128]{2,1,0:T(1,128)S(1)}, u32[]{:S(2)}) copy-start(f32[8,1,128]{2,1,0:T(1,128)S(1)} %convert_element_type.129) | copy-start | bytes 12292
  201.2 31.6 %copy-start.52 = (f32[32]{0:T(128)}, f32[32]{0:T(128)S(1)}, u32[]{:S(2)}) copy-start(f32[32]{0:T(128)S(1)} %exp.141) | copy-start | bytes 388
  221.4 65.5 %copy-start.27 = (f32[2304]{0:T(1024)}, f32[2304]{0:T(1024)S(1)}, u32[]{:S(2)}) copy-start(f32[2304]{0:T(1024)S(1)} %get-tuple-element.835) | copy-start | bytes 27652
  221.4 65.5 %copy-start.29 = (f32[2304]{0:T(1024)}, f32[2304]{0:T(1024)S(1)}, u32[]{:S(2)}) copy-start(f32[2304]{0:T(1024)S(1)} %get-tuple-element.836) | copy-start | bytes 27652
  221.4 65.5 %copy-start.31 = (f32[2304]{0:T(1024)}, f32[2304]{0:T(1024)S(1)}, u32[]{:S(2)}) copy-start(f32[2304]{0:T(1024)S(1)} %get-tuple-element.837) | copy-start | bytes 27652
  221.4 65.5 %copy-start.33 = (f32[2304]{0:T(1024)}, f32[2304]{0:T(1024)S(1)}, u32[]{:S(2)}) copy-start(f32[2304]{0:T(1024)S(1)} %get-tuple-element.838) | copy-start | bytes 27652
  355.6 251.9 %copy-start.25 = (f32[2048]{0:T(1024)S(1)}, f32[2048]{0:T(1024)}, u32[]{:S(2)}) copy-start(f32[2048]{0:T(1024)} %mul.744) | copy-start | bytes 24580
  607.5 23.8 %copy-start.47 = (f32[8,1,256]{2,1,0:T(1,128)S(1)}, f32[8,1,256]{2,1,0:T(1,128)}, u32[]{:S(2)}) copy-start(f32[8,1,256]{2,1,0:T(1,128)} %convert_element_type.131) | copy-start | bytes 24580
  703.2 879.3 %copy-start.26 = (f32[2048]{0:T(1024)S(1)}, f32[2048]{0:T(1024)}, u32[]{:S(2)}) copy-start(f32[2048]{0:T(1024)} %mul.744) | copy-start | bytes 24580
  704.4 41.5 %copy-start.10 = (f32[1,256,128]{2,1,0:T(8,128)}, f32[1,256,128]{2,1,0:T(8,128)S(1)}, u32[]{:S(2)}) copy-start(f32[1,256,128]{2,1,0:T(8,128)S(1)} %get-tuple-element.1114) | copy-start | bytes 393220 | tf_op jit(solution)/shard_map/transpose(jvp(vmap()))/while
  813.2 42.7 %copy-start.10 = (f32[1,256,128]{2,1,0:T(8,128)}, f32[1,256,128]{2,1,0:T(8,128)S(1)}, u32[]{:S(2)}) copy-start(f32[1,256,128]{2,1,0:T(8,128)S(1)} %get-tuple-element.1114) | copy-start | bytes 393220 | tf_op jit(solution)/shard_map/transpose(jvp(vmap()))/while
  923.2 42.7 %copy-start.10 = (f32[1,256,128]{2,1,0:T(8,128)}, f32[1,256,128]{2,1,0:T(8,128)S(1)}, u32[]{:S(2)}) copy-start(f32[1,256,128]{2,1,0:T(8,128)S(1)} %get-tuple-element.1114) | copy-start | bytes 393220 | tf_op jit(solution)/shard_map/transpose(jvp(vmap()))/while
  1033.1 42.7 %copy-start.10 = (f32[1,256,128]{2,1,0:T(8,128)}, f32[1,256,128]{2,1,0:T(8,128)S(1)}, u32[]{:S(2)}) copy-start(f32[1,256,128]{2,1,0:T(8,128)S(1)} %get-tuple-element.1114) | copy-start | bytes 393220 | tf_op jit(solution)/shard_map/transpose(jvp(vmap()))/while
  1143.1 42.7 %copy-start.10 = (f32[1,256,128]{2,1,0:T(8,128)}, f32[1,256,128]{2,1,0:T(8,128)S(1)}, u32[]{:S(2)}) copy-start(f32[1,256,128]{2,1,0:T(8,128)S(1)} %get-tuple-element.1114) | copy-start | bytes 393220 | tf_op jit(solution)/shard_map/transpose(jvp(vmap()))/while
  1253.1 42.7 %copy-start.10 = (f32[1,256,128]{2,1,0:T(8,128)}, f32[1,256,128]{2,1,0:T(8,128)S(1)}, u32[]{:S(2)}) copy-start(f32[1,256,128]{2,1,0:T(8,128)S(1)} %get-tuple-element.1114) | copy-start | bytes 393220 | tf_op jit(solution)/shard_map/transpose(jvp(vmap()))/while
  1363.1 42.7 %copy-start.10 = (f32[1,256,128]{2,1,0:T(8,128)}, f32[1,256,128]{2,1,0:T(8,128)S(1)}, u32[]{:S(2)}) copy-start(f32[1,256,128]{2,1,0:T(8,128)S(1)} %get-tuple-element.1114) | copy-start | bytes 393220 | tf_op jit(solution)/shard_map/transpose(jvp(vmap()))/while
  1473.1 42.7 %copy-start.10 = (f32[1,256,128]{2,1,0:T(8,128)}, f32[1,256,128]{2,1,0:T(8,128)S(1)}, u32[]{:S(2)}) copy-start(f32[1,256,128]{2,1,0:T(8,128)S(1)} %get-tuple-element.1114) | copy-start | bytes 393220 | tf_op jit(solution)/shard_map/transpose(jvp(vmap()))/while
  1582.5 22.8 %copy-start.17 = (bf16[8,256,1024]{2,1,0:T(8,128)(2,1)S(1)}, bf16[8,256,1024]{2,1,0:T(8,128)(2,1)}, u32[]{:S(2)}) copy-start(bf16[8,256,1024]{2,1,0:T(8,128)(2,1)} %broadcast_multiply_fusion.4) | copy-start | bytes 12582916
  1582.5 22.8 %copy-start.48 = (f32[8,1,256]{2,1,0:T(1,128)S(1)}, f32[8,1,256]{2,1,0:T(1,128)}, u32[]{:S(2)}) copy-start(f32[8,1,256]{2,1,0:T(1,128)} %convert_element_type.131) | copy-start | bytes 24580
  1617.4 342.1 %reduce-scatter.7.cloned.1.call-start = ((), (), s32[]{:S(2)}) async-start(), calls=%async_computation.10 | async-start | bytes 20054016 | tf_op jit(solution)/shard_map/reduce_scatter | solution.py:209
  1618.9 49.7 %copy-start.28 = (f32[2304]{0:T(1024)S(1)}, f32[2304]{0:T(1024)}, u32[]{:S(2)}) copy-start(f32[2304]{0:T(1024)} %copy-done.27) | copy-start | bytes 27652
  1618.9 49.7 %copy-start.30 = (f32[2304]{0:T(1024)S(1)}, f32[2304]{0:T(1024)}, u32[]{:S(2)}) copy-start(f32[2304]{0:T(1024)} %copy-done.29) | copy-start | bytes 27652
  1618.9 49.7 %copy-start.32 = (f32[2304]{0:T(1024)S(1)}, f32[2304]{0:T(1024)}, u32[]{:S(2)}) copy-start(f32[2304]{0:T(1024)} %copy-done.31) | copy-start | bytes 27652
  1618.9 49.7 %copy-start.34 = (f32[2304]{0:T(1024)S(1)}, f32[2304]{0:T(1024)}, u32[]{:S(2)}) copy-start(f32[2304]{0:T(1024)} %copy-done.33) | copy-start | bytes 27652
  1699.6 31.6 %copy-start.16 = (bf16[8,256,1024]{2,1,0:T(8,128)(2,1)S(1)}, bf16[8,256,1024]{2,1,0:T(8,128)(2,1)}, u32[]{:S(2)}) copy-start(bf16[8,256,1024]{2,1,0:T(8,128)(2,1)} %fusion.98) | copy-start | bytes 12582916
  1840.5 107.9 %all-to-all-start.1 = ((bf16[8,2,131072]{2,1,0:T(2,128)(2,1)}), bf16[8,2,131072]{2,1,0:T(2,128)(2,1)}, u32[]{:S(2)}, u32[]{:S(2)}) async-start(bf16[8,2,131072]{2,1,0:T(2,128)(2,1)} %reshape.1444), calls=%async_computation.1 | async-start | bytes 8388608 | tf_op jit(solution)/shard_map/all_to_all | solution.py:184
  1850.4 29.8 %copy-start.38 = (f32[1,2,8,128]{3,1,2,0:T(2,128)S(1)}, f32[1,2,8,128]{3,1,2,0:T(2,128)}, u32[]{:S(2)}) copy-start(f32[1,2,8,128]{3,1,2,0:T(2,128)} %copy-done.37) | copy-start | bytes 24580
  1948.4 90.4 %copy-start.41 = (f32[2304]{0:T(1024)S(1)}, f32[2304]{0:T(1024)}, u32[]{:S(2)}) copy-start(f32[2304]{0:T(1024)} %get-tuple-element.831) | copy-start | bytes 27652
  1948.4 90.4 %copy-start.51 = (f32[2048]{0:T(1024)S(1)}, f32[2048]{0:T(1024)}, u32[]{:S(2)}) copy-start(f32[2048]{0:T(1024)} %get-tuple-element.829) | copy-start | bytes 24580
  1948.4 153.3 %all-to-all-start.3 = ((bf16[8,2,131072]{2,1,0:T(2,128)(2,1)}), bf16[8,2,131072]{2,1,0:T(2,128)(2,1)}, u32[]{:S(2)}, u32[]{:S(2)}) async-start(bf16[8,2,131072]{2,1,0:T(2,128)(2,1)} %reshape.1446), calls=%async_computation.3 | async-start | bytes 8388608 | tf_op jit(solution)/shard_map/all_to_all | solution.py:191
  1953.3 109.5 %reduce-scatter.13.cloned.1.call-start = ((), (), s32[]{:S(2)}) async-start(), calls=%async_computation.13 | async-start | bytes 1327104
  1954.9 108.9 %reduce-scatter.9.cloned.1.call-start = ((), (), s32[]{:S(2)}) async-start(), calls=%async_computation.11 | async-start | bytes 589824 | tf_op jit(solution)/shard_map/reduce_scatter | solution.py:210
  1959.4 217.2 %all-reduce.25.cloned.1.call-start = ((), (), s32[]{:S(2)}) async-start(), calls=%async_computation.14 | async-start | bytes 6553600 | tf_op jit(solution)/shard_map/psum | solution.py:216
  2127.7 53.7 %copy-start.1 = (s32[1,8]{1,0:T(1,128)S(1)}, s32[1,8]{1,0:T(1,128)}, u32[]{:S(2)}) copy-start(s32[1,8]{1,0:T(1,128)} %param.21) | copy-start | bytes 100
  (83 other events, 731.1 us)
Sparse Core Ops, SparseCore 0:
  10.5 97.6 all-gather.5
  112.8 64.7 all-gather.7
  1617.5 71.2 reduce-scatter.10
  1761.2 146.3 reduce-scatter.6
  1957.9 50.5 reduce-scatter.12
  2012.0 33.7 reduce-scatter.8
  2048.4 128.1 all-reduce.24
where the time goes:
time: 2210 us; the launch traced here: 2190 us
  matrix products  696 us (31%)
  local copies, waits for them, and re-layouts  613 us (28%)
  other arithmetic  498 us (23%)
  blocking collectives  306 us (14%)
  waiting for transfers between devices  39.7 us (2%)
    dot_general x24, matrix products, block_step(): jnp.einsum('hts,shp->thp', weights, by_head, precision=largest_value)  302 us
    dot_general x32, matrix products, block_step(): jnp.einsum('tn,hpn->thp', state_out, state, precision=largest_value)  111 us
    dynamic_update_slice x56, local copies, waits for them, and re-layouts, scan_blocks(): final, outputs = lax.scan(jax.checkpoint(block_step), start, blocks)  104 us
    dot_general x24, matrix products, block_step(): jnp.einsum('shp,sn->hpn', tail.T[:, :, None] * by_head, state_in, precisi...  93.9 us
    another operation x174, local copies, waits for them, and re-layouts  86.1 us
    unnamed x133, local copies, waits for them, and re-layouts  82.7 us
    all_to_all x1, blocking collectives, body(): lax.all_to_all(sent_tokens, 'fsdp', split_axis=0, concat_axis=1, tiled=True)  78.3 us
    psum x1, blocking collectives, body(): lax.psum((middle_grads[4], middle_grads[5], middle_grads[6]), ('rep', 'fs...  76.4 us
  transfers between devices with their start and end apart: 10, of which 1 were waited for; matrix products, arithmetic and copies ran while one was open for 37% of the time, Pallas kernels for 0%

commit v1 on v0

v1 whole, which is shorter than its diff:
```python
import functools
import jax
import jax.numpy as jnp
from jax import lax
from jax.experimental import pallas as pl
from jax.experimental.pallas import tpu as pltpu
from jax.sharding import PartitionSpec as P

STATE = 128
HEADDIM = 64
HEADS = 32
INNER = 2048
CONV = 4
BLOCK = 256
CHUNK = 128
LANES = 128
MESH = pl.DeviceIdType.MESH
EPS = 1e-05
F32 = jnp.float32
BF16 = jnp.bfloat16
FAR = -1e9
NT = (((1,), (1,)), ((), ()))
TN = (((0,), (0,)), ((), ()))


def mm(a, b, dims=(((1,), (0,)), ((), ()))):
    return lax.dot_general(a, b, dims, preferred_element_type=F32)


def two_parts(v):
    high = v.astype(BF16)
    return high, (v - high.astype(F32)).astype(BF16)


def spread(v, expand):
    high, low = two_parts(v)
    return mm(jnp.concatenate([high, low], axis=1), expand)


def gather_heads(v, collect):
    high, low = two_parts(v)
    return mm(high, collect) + mm(low, collect)


def sigmoid(v):
    return 0.5 + 0.5 * jnp.tanh(0.5 * v)


def mm_state(rows, state):
    return mm(jnp.concatenate([rows, rows], axis=1), jnp.concatenate(two_parts(state), axis=0))


def softplus(v):
    return jnp.maximum(v, 0.0) + jnp.log1p(jnp.exp(-jnp.abs(v)))


def causal_sum(log_decay):
    rows = lax.broadcasted_iota(jnp.int32, (CHUNK, CHUNK), 0)
    cols = lax.broadcasted_iota(jnp.int32, (CHUNK, CHUNK), 1)
    tri = (rows >= cols).astype(F32)
    return lax.dot_general(
        tri, log_decay, (((1,), (0,)), ((), ())),
        precision=lax.Precision.HIGHEST, preferred_element_type=F32,
    )


def reverse_sum(v):
    rows = lax.broadcasted_iota(jnp.int32, (CHUNK, CHUNK), 0)
    cols = lax.broadcasted_iota(jnp.int32, (CHUNK, CHUNK), 1)
    tri = (cols >= rows).astype(F32)
    return lax.dot_general(
        tri, v, (((1,), (0,)), ((), ())),
        precision=lax.Precision.HIGHEST, preferred_element_type=F32,
    )


def convolve(cbuf, cw_ref, cb_ref, cols):
    total = cb_ref[0:1, cols] + cw_ref[3:4, cols] * cbuf[8 : 8 + BLOCK, cols]
    for k in range(CONV - 1):
        total = total + cw_ref[k : k + 1, cols] * cbuf[5 + k : 5 + k + BLOCK, cols]
    return total


def normalize(tok_ref, gain_ref):
    hidden = tok_ref[0].astype(F32)
    scale = lax.rsqrt(jnp.mean(hidden * hidden, axis=1, keepdims=True) + EPS)
    return (hidden * scale * gain_ref[0:1, :]).astype(BF16)


def fwd_kernel(
    inner, heads,
    nb_ref, tok_ref, gain_ref, win_ref, cw_ref, cb_ref, hp_ref, dwide_ref, og_ref, expand_ref,
    gate_ref, cin_ref, raw_ref, y_ref, s_ref, ss_ref, sc_ref,
    cbuf, xbuf, state,
):
    seq, blk = pl.program_id(0), pl.program_id(1)
    chan = inner + 2 * STATE

    @pl.when(blk < nb_ref[seq])
    def _():
        @pl.when(blk == 0)
        def _():
            cbuf[0:8, :] = jnp.zeros((8, chan), F32)
            state[...] = jnp.zeros_like(state)

        @pl.when(blk > 0)
        def _():
            cbuf[0:8, :] = cbuf[BLOCK : BLOCK + 8, :]

        normed = normalize(tok_ref, gain_ref)
        for j in range(0, inner, 256):
            gate_ref[0, :, j : j + 256] = mm(normed, win_ref[:, j : j + 256])
        for j in range(0, chan, 256):
            part = mm(normed, win_ref[:, inner + j : inner + j + 256])
            cin_ref[0, :, j : j + 256] = part
            cbuf[8 : 8 + BLOCK, j : j + 256] = part
        raw = mm(normed, win_ref[:, inner + chan :])
        raw_ref[0] = raw
        for j in range(0, chan, 256):
            u = convolve(cbuf, cw_ref, cb_ref, slice(j, j + 256))
            xbuf[:, j : j + 256] = u * sigmoid(u)
        step = softplus(raw + hp_ref[0:1, :])
        log_decay = -step * hp_ref[1:2, :]
        rows = lax.broadcasted_iota(jnp.int32, (CHUNK, CHUNK), 0)
        cols = lax.broadcasted_iota(jnp.int32, (CHUNK, CHUNK), 1)
        causal = rows >= cols
        left = cols < HEADDIM
        for c in range(BLOCK // CHUNK):
            at = slice(c * CHUNK, (c + 1) * CHUNK)
            dt = step[at]
            cum = causal_sum(log_decay[at])
            cum_t = cum.T
            last = cum[CHUNK - 1 : CHUNK]
            three = jnp.concatenate([jnp.exp(cum), dt, jnp.exp(last - cum) * dt], axis=0)
            wide = spread(three, expand_ref[...])
            e_wide, dt_wide, w_wide = wide[:CHUNK], wide[CHUNK : 2 * CHUNK], wide[2 * CHUNK :]
            s_in = xbuf[at, inner : inner + STATE].astype(BF16)
            s_out = xbuf[at, inner + STATE :].astype(BF16)
            cross = mm(s_out, s_in, NT)
            x = xbuf[at, :inner]
            xd = (x * dt_wide).astype(BF16)
            xw = (x * w_wide).astype(BF16)
            held = state[...]
            s_ref[0, c] = held
            carried = e_wide * mm_state(s_out, held)
            for p in range(heads // 2):
                lanes = slice(p * 128, (p + 1) * 128)
                pair = xd[:, lanes]
                zero = jnp.zeros_like(pair)
                both = jnp.concatenate([jnp.where(left, pair, zero), jnp.where(left, zero, pair)], axis=0)
                parts = []
                for h in (2 * p, 2 * p + 1):
                    gap = cum[:, h : h + 1] - cum_t[h : h + 1, :]
                    parts.append((cross * jnp.exp(jnp.where(causal, gap, FAR))).astype(BF16))
                y_ref[0, at, lanes] = carried[:, lanes] + mm(jnp.concatenate(parts, axis=1), both)
            state[...] = e_wide[CHUNK - 1 : CHUNK] * held + mm(s_in, xw, TN)
        total = jnp.zeros((BLOCK, 1), F32)
        for j in range(0, inner, 256):
            at = slice(j, j + 256)
            gate = gate_ref[0, :, at]
            gated = (y_ref[0, :, at] + dwide_ref[0:1, at] * xbuf[:, at]) * (gate * sigmoid(gate))
            total = total + jnp.sum(gated * gated, axis=1, keepdims=True)
            sc_ref[0, :, at] = gated * og_ref[0:1, at]
        ss_ref[...] = jnp.broadcast_to(total, (BLOCK, LANES)).T[0:8]


def fixed(shape):
    return pl.BlockSpec(shape, lambda *_: (0,) * len(shape), pipeline_mode=pl.Buffered(1))


def fwd_call(nb, tok, gain, win, cw, cb, hp, dwide, og, expand):
    nseq, length, width = tok.shape
    inner = dwide.shape[1]
    heads = inner // HEADDIM
    chan = inner + 2 * STATE
    blocks = length // BLOCK

    def rows(s, b, nb):
        return (s, jnp.maximum(jnp.minimum(b, nb[s] - 1), 0), 0)

    def srows(s, b, nb):
        return (s, jnp.maximum(jnp.minimum(b, nb[s] - 1), 0), 0, 0)

    def ssrows(s, b, nb):
        return (s * blocks + jnp.maximum(jnp.minimum(b, nb[s] - 1), 0), 0)

    grid_spec = pltpu.PrefetchScalarGridSpec(
        num_scalar_prefetch=1,
        grid=(nseq, blocks),
        in_specs=[
            pl.BlockSpec((1, BLOCK, width), rows),
            fixed(gain.shape), fixed(win.shape), fixed(cw.shape), fixed(cb.shape),
            fixed(hp.shape), fixed(dwide.shape), fixed(og.shape), fixed(expand.shape),
        ],
        out_specs=[
            pl.BlockSpec((1, BLOCK, inner), rows),
            pl.BlockSpec((1, BLOCK, chan), rows),
            pl.BlockSpec((1, BLOCK, LANES), rows),
            pl.BlockSpec((1, BLOCK, inner), rows),
            pl.BlockSpec((1, BLOCK // CHUNK, STATE, inner), srows),
            pl.BlockSpec((8, BLOCK), ssrows),
            pl.BlockSpec((1, BLOCK, inner), rows),
        ],
        scratch_shapes=[
            pltpu.VMEM((BLOCK + 8, chan), F32),
            pltpu.VMEM((BLOCK, chan), F32),
            pltpu.VMEM((STATE, inner), F32),
        ],
    )
    shapes = [
        jax.ShapeDtypeStruct((nseq, length, inner), F32),
        jax.ShapeDtypeStruct((nseq, length, chan), F32),
        jax.ShapeDtypeStruct((nseq, length, LANES), F32),
        jax.ShapeDtypeStruct((nseq, length, inner), F32),
        jax.ShapeDtypeStruct((nseq, length // CHUNK, STATE, inner), F32),
        jax.ShapeDtypeStruct((nseq * blocks * 8, BLOCK), F32),
        jax.ShapeDtypeStruct((nseq, length, inner), F32),
    ]
    return pl.pallas_call(
        functools.partial(fwd_kernel, inner, heads),
        grid_spec=grid_spec,
        out_shape=shapes,
        compiler_params=pltpu.CompilerParams(
            dimension_semantics=("arbitrary", "arbitrary"), vmem_limit_bytes=60 * 1024 * 1024
        ),
        cost_estimate=pl.CostEstimate(
            flops=nseq * length * width * (3 * inner + 400), bytes_accessed=60 << 20, transcendentals=0
        ),
        name="layer_forward",
    )(nb, tok, gain, win, cw, cb, hp, dwide, og, expand)


def mid_kernel(nb_ref, len_ref, cot_ref, sc_ref, wout_ref, gm_ref, v_ref, bp_ref):
    seq, blk = pl.program_id(0), pl.program_id(1)

    @pl.when(blk < nb_ref[seq])
    def _():
        cot = cot_ref[0]
        position = blk * BLOCK + lax.broadcasted_iota(jnp.int32, cot.shape, 0)
        gb = jnp.where(position < len_ref[seq], cot, jnp.zeros_like(cot))
        total = jnp.zeros((BLOCK, 1), F32)
        for j in range(0, sc_ref.shape[2], 256):
            at = slice(j, j + 256)
            gm = mm(gb, wout_ref[at, :], NT)
            gm_ref[0, :, at] = gm
            total = total + jnp.sum(gm * sc_ref[0, :, at], axis=1, keepdims=True)
        v_ref[...] = jnp.broadcast_to(total, (BLOCK, LANES)).T[0:8]
        scaled = sc_ref[0].astype(BF16)
        for j in range(0, cot.shape[1], 256):
            bp_ref[0, :, j : j + 256] = mm(scaled, wout_ref[:, j : j + 256]).astype(BF16)


def mid_call(nb, lens, cot, scaled, wout):
    nseq, length, width = cot.shape
    inner = wout.shape[0]
    blocks = length // BLOCK

    def place(s, b, nb):
        return jnp.maximum(jnp.minimum(b, nb[s] - 1), 0)

    def rows(s, b, nb, lens):
        return (s, place(s, b, nb), 0)

    def vrows(s, b, nb, lens):
        return (s * blocks + place(s, b, nb), 0)

    return pl.pallas_call(
        mid_kernel,
        grid_spec=pltpu.PrefetchScalarGridSpec(
            num_scalar_prefetch=2,
            grid=(nseq, blocks),
            in_specs=[pl.BlockSpec((1, BLOCK, width), rows), pl.BlockSpec((1, BLOCK, inner), rows), fixed(wout.shape)],
            out_specs=[
                pl.BlockSpec((1, BLOCK, inner), rows), pl.BlockSpec((8, BLOCK), vrows),
                pl.BlockSpec((1, BLOCK, width), rows),
            ],
        ),
        out_shape=[
            jax.ShapeDtypeStruct((nseq, length, inner), F32),
            jax.ShapeDtypeStruct((nseq * blocks * 8, BLOCK), F32),
            jax.ShapeDtypeStruct((nseq, length, width), BF16),
        ],
        compiler_params=pltpu.CompilerParams(
            dimension_semantics=("arbitrary", "arbitrary"), vmem_limit_bytes=40 * 1024 * 1024
        ),
        cost_estimate=pl.CostEstimate(flops=10**10, bytes_accessed=30 << 20, transcendentals=0),
        name="layer_middle",
    )(nb, lens, cot, scaled, wout)


def bwd_kernel(
    inner, heads, blocks,
    nb_ref, len_ref,
    tok_ref, cot_ref, gain_ref, win_ref, gm_ref, cw_ref, cb_ref, hp_ref, dwide_ref, og_ref, expand_ref,
    collect_ref, gate_ref, cin_ref, halo_ref, raw_ref, y_ref, s_ref, rv_ref,
    gn_ref, win_out, wout_out, dcw_ref, dhp_ref, dog_ref, ddw_ref,
    cbuf, ubuf, dbuf, xbuf, dybuf, dproj, dstate, later, dwin_ref, dwout_ref,
):
    seq, step_id = pl.program_id(0), pl.program_id(1)
    chan = inner + 2 * STATE
    width = tok_ref.shape[2]
    nb = nb_ref[seq]
    blk = nb - 1 - step_id

    @pl.when((seq == 0) & (step_id == 0))
    def _():
        dwin_ref[...] = jnp.zeros_like(dwin_ref)
        dwout_ref[...] = jnp.zeros_like(dwout_ref)
        dcw_ref[...] = jnp.zeros_like(dcw_ref)
        dhp_ref[...] = jnp.zeros_like(dhp_ref)
        dog_ref[...] = jnp.zeros_like(dog_ref)
        ddw_ref[...] = jnp.zeros_like(ddw_ref)

    @pl.when(blk >= 0)
    def _():
        @pl.when(step_id == 0)
        def _():
            dbuf[BLOCK : BLOCK + 8, :] = jnp.zeros((8, chan), F32)
            dstate[...] = jnp.zeros_like(dstate)
            later[...] = jnp.zeros_like(later)

        @pl.when(step_id > 0)
        def _():
            dbuf[BLOCK : BLOCK + 8, :] = dbuf[0:8, :]

        @pl.when(blk == 0)
        def _():
            cbuf[0:8, :] = jnp.zeros((8, chan), F32)

        @pl.when(blk > 0)
        def _():
            cbuf[0:8, :] = halo_ref[0]

        cbuf[8 : 8 + BLOCK, :] = cin_ref[0]
        position = blk * BLOCK + lax.broadcasted_iota(jnp.int32, (BLOCK, width), 0)
        cot = cot_ref[0]
        gb = jnp.where(position < len_ref[seq], cot, jnp.zeros_like(cot))
        rv = jnp.concatenate([rv_ref[...], jnp.zeros((LANES - 8, BLOCK), F32)], axis=0).T
        scale, coef = rv[:, 0:1], rv[:, 1:2]
        for j in range(0, chan, 256):
            at = slice(j, j + 256)
            u = convolve(cbuf, cw_ref, cb_ref, at)
            sig = sigmoid(u)
            xbuf[:, at] = u * sig
            ubuf[:, at] = sig * (1.0 + u * (1.0 - sig))
        for j in range(0, inner, 256):
            at = slice(j, j + 256)
            gm = gm_ref[0, :, at]
            gate = gate_ref[0, :, at]
            sig = sigmoid(gate)
            x = xbuf[:, at]
            ysum = y_ref[0, :, at] + dwide_ref[0:1, at] * x
            gated = ysum * (gate * sig)
            normal = gated * scale
            mixed = (normal * og_ref[0:1, at]).astype(BF16)
            dwout_ref[at, :] += mm(mixed, gb, TN)
            dog_ref[0:1, at] += jnp.sum(gm * normal, axis=0, keepdims=True)
            dgated = scale * (gm * og_ref[0:1, at]) - gated * coef
            dproj[:, at] = (dgated * ysum * (sig * (1.0 + gate * (1.0 - sig)))).astype(BF16)
            dy = dgated * (gate * sig)
            ddw_ref[0:1, at] += jnp.sum(dy * x, axis=0, keepdims=True)
            dybuf[:, at] = dy
        raw = raw_ref[0] + hp_ref[0:1, :]
        step = softplus(raw)
        log_decay = -step * hp_ref[1:2, :]
        rows = lax.broadcasted_iota(jnp.int32, (CHUNK, CHUNK), 0)
        cols = lax.broadcasted_iota(jnp.int32, (CHUNK, CHUNK), 1)
        causal = cols >= rows
        left = cols < HEADDIM
        for c in reversed(range(BLOCK // CHUNK)):
            at = slice(c * CHUNK, (c + 1) * CHUNK)
            dt = step[at]
            cum = causal_sum(log_decay[at])
            cum_t = cum.T
            last = cum[CHUNK - 1 : CHUNK]
            tail = jnp.exp(last - cum)
            four = jnp.concatenate([jnp.exp(cum), dt, tail], axis=0)
            wide = spread(four, expand_ref[...])
            e_wide, dt_wide, t_wide = wide[:CHUNK], wide[CHUNK : 2 * CHUNK], wide[2 * CHUNK :]
            s_in = xbuf[at, inner : inner + STATE].astype(BF16)
            s_out = xbuf[at, inner + STATE :].astype(BF16)
            cross = mm(s_in, s_out, NT)
            x = xbuf[at, :inner]
            dy = dybuf[at, :]
            dy16 = dy.astype(BF16)
            xd32 = x * dt_wide
            xd = xd32.astype(BF16)
            xw = (xd32 * t_wide).astype(BF16)
            held32 = s_ref[0, c]
            held = held32.astype(BF16)
            dheld = dstate[...]
            dheld16 = dheld.astype(BF16)
            edy = (e_wide * dy).astype(BF16)
            back = mm_state(s_in, dheld)
            reach = mm_state(s_out, held32)
            dcross = jnp.zeros((CHUNK, CHUNK), F32)
            dxd_parts = []
            for p in range(heads // 2):
                lanes = slice(p * 128, (p + 1) * 128)
                pair = xd[:, lanes]
                dpair = dy16[:, lanes]
                zero = jnp.zeros_like(pair)
                both = jnp.concatenate([jnp.where(left, dpair, zero), jnp.where(left, zero, dpair)], axis=0)
                dweights = mm(pair, both, NT)
                parts = []
                for i, h in enumerate((2 * p, 2 * p + 1)):
                    gap = cum_t[h : h + 1, :] - cum[:, h : h + 1]
                    decay = jnp.exp(jnp.where(causal, gap, FAR))
                    parts.append((cross * decay).astype(BF16))
                    dcross = dcross + dweights[:, i * CHUNK : (i + 1) * CHUNK] * decay
                dxd_parts.append(mm(jnp.concatenate(parts, axis=1), both))
            inside = jnp.concatenate(dxd_parts, axis=1)
            dxd = inside + t_wide * back
            fold = jnp.sum(dheld * later[...], axis=0, keepdims=True)
            direct = x * dxd
            scanned = (y_ref[0, at, :] - e_wide * reach) * dy16.astype(F32) + edy.astype(F32) * reach
            scanned = scanned - xd.astype(F32) * inside - xw.astype(F32) * back
            stacked = jnp.concatenate([direct, scanned, jnp.broadcast_to(fold, (8, inner))], axis=0)
            small = gather_heads(stacked, collect_ref[...])
            ddirect, dcum = small[:CHUNK], small[CHUNK : 2 * CHUNK]
            dlog = reverse_sum(dcum) + small[2 * CHUNK : 2 * CHUNK + 1]
            dstep = ddirect - dlog * hp_ref[1:2, :]
            draw = dstep * sigmoid(raw[at])
            dhp_ref[0:1, :] += jnp.sum(draw, axis=0, keepdims=True)
            dhp_ref[1:2, :] += jnp.sum(dlog * log_decay[at], axis=0, keepdims=True)
            dproj[at, inner + chan :] = draw.astype(BF16)
            dybuf[at, :] = dt_wide * dxd + dwide_ref[0:1, :] * dy
            dcross16 = dcross.astype(BF16)
            ds_in = mm(dcross16, s_out) + mm(xw, dheld16, NT)
            ds_out = mm(dcross16, s_in, TN) + mm(edy, held, NT)
            dbuf[at, inner : inner + STATE] = ds_in
            dbuf[at, inner + STATE :] = ds_out
            later[...] = held32
            dstate[...] = e_wide[CHUNK - 1 : CHUNK] * dheld + mm(s_out, edy, TN)
        for j in range(0, chan, 256):
            at = slice(j, j + 256)
            grad = dybuf[:, at] if j < inner else dbuf[0:BLOCK, at]
            du = grad * ubuf[:, at]
            dbuf[0:BLOCK, at] = du
            dcw_ref[CONV : CONV + 1, at] += jnp.sum(du, axis=0, keepdims=True)
            for k in range(CONV):
                dcw_ref[k : k + 1, at] += jnp.sum(du * cbuf[5 + k : 5 + k + BLOCK, at], axis=0, keepdims=True)
            dcin = cw_ref[CONV - 1 : CONV, at] * du
            for k in range(CONV - 1):
                dcin = dcin + cw_ref[k : k + 1, at] * dbuf[3 - k : 3 - k + BLOCK, at]
            dproj[:, inner + j : inner + j + 256] = dcin.astype(BF16)
        normed = normalize(tok_ref, gain_ref)
        count = dproj.shape[1]
        for j in range(0, count, 256):
            at = slice(j, min(j + 256, count))
            dwin_ref[:, at] += mm(normed, dproj[:, at], TN)
        for j in range(0, width, 256):
            gn_ref[0, :, j : j + 256] = mm(dproj[...], win_ref[j : j + 256, :], NT).astype(BF16)

    @pl.when((seq == pl.num_programs(0) - 1) & (step_id == blocks - 1))
    def _():
        win_out[...] = dwin_ref[...].astype(BF16)
        wout_out[...] = dwout_ref[...].astype(BF16)


def bwd_call(nb, lens, tok, cot, gain, win, gm, cw, cb, hp, dwide, og, expand, collect, gate, cin, raw, y, s, rv):
    nseq, length, width = tok.shape
    inner = gm.shape[2]
    heads = inner // HEADDIM
    chan = inner + 2 * STATE
    blocks = length // BLOCK

    def place(s, b, nb):
        return jnp.maximum(nb[s] - 1 - b, 0)

    def rows(s, b, nb, lens):
        return (s, place(s, b, nb), 0)

    def srows(s, b, nb, lens):
        return (s, place(s, b, nb), 0, 0)

    def halo(s, b, nb, lens):
        return (s, jnp.maximum(place(s, b, nb) * (BLOCK // 8) - 1, 0), 0)

    def rvrows(s, b, nb, lens):
        return (s * blocks + place(s, b, nb), 0)

    def whole(shape):
        return pl.BlockSpec(shape, lambda *_: (0,) * len(shape), pipeline_mode=pl.Buffered(1))

    grid_spec = pltpu.PrefetchScalarGridSpec(
        num_scalar_prefetch=2,
        grid=(nseq, blocks),
        in_specs=[
            pl.BlockSpec((1, BLOCK, width), rows),
            pl.BlockSpec((1, BLOCK, width), rows),
            fixed(gain.shape), fixed(win.shape), pl.BlockSpec((1, BLOCK, inner), rows), fixed(cw.shape), fixed(cb.shape),
            fixed(hp.shape), fixed(dwide.shape), fixed(og.shape), fixed(expand.shape), fixed(collect.shape),
            pl.BlockSpec((1, BLOCK, inner), rows),
            pl.BlockSpec((1, BLOCK, chan), rows),
            pl.BlockSpec((1, 8, chan), halo),
            pl.BlockSpec((1, BLOCK, LANES), rows),
            pl.BlockSpec((1, BLOCK, inner), rows),
            pl.BlockSpec((1, BLOCK // CHUNK, STATE, inner), srows),
            pl.BlockSpec((8, BLOCK), rvrows),
        ],
        out_specs=[
            pl.BlockSpec((1, BLOCK, width), rows),
            whole(win.shape), whole((inner, width)), whole((8, chan)), whole((8, LANES)), whole((8, inner)),
            whole((8, inner)),
        ],
        scratch_shapes=[
            pltpu.VMEM((BLOCK + 8, chan), F32),
            pltpu.VMEM((BLOCK, chan), F32),
            pltpu.VMEM((BLOCK + 8, chan), F32),
            pltpu.VMEM((BLOCK, chan), F32),
            pltpu.VMEM((BLOCK, inner), F32),
            pltpu.VMEM((BLOCK, win.shape[1]), BF16),
            pltpu.VMEM((STATE, inner), F32),
            pltpu.VMEM((STATE, inner), F32),
            pltpu.VMEM(win.shape, F32),
            pltpu.VMEM((inner, width), F32),
        ],
    )
    shapes = [
        jax.ShapeDtypeStruct((nseq, length, width), BF16),
        jax.ShapeDtypeStruct(win.shape, BF16),
        jax.ShapeDtypeStruct((inner, width), BF16),
        jax.ShapeDtypeStruct((8, chan), F32),
        jax.ShapeDtypeStruct((8, LANES), F32),
        jax.ShapeDtypeStruct((8, inner), F32),
        jax.ShapeDtypeStruct((8, inner), F32),
    ]
    return pl.pallas_call(
        functools.partial(bwd_kernel, inner, heads, blocks),
        grid_spec=grid_spec,
        out_shape=shapes,
        compiler_params=pltpu.CompilerParams(
            dimension_semantics=("arbitrary", "arbitrary"), vmem_limit_bytes=63 * 1024 * 1024
        ),
        cost_estimate=pl.CostEstimate(
            flops=2 * nseq * length * width * (3 * inner + 400), bytes_accessed=100 << 20, transcendentals=0
        ),
        name="layer_backward",
    )(nb, lens, tok, cot, gain, win, gm, cw, cb, hp, dwide, og, expand, collect, gate, cin, cin, raw, y, s, rv)


def matrices(inner):
    heads = inner // HEADDIM
    owner = jnp.arange(inner, dtype=jnp.int32) // HEADDIM
    head = jnp.arange(LANES, dtype=jnp.int32)
    one = (head[:, None] == owner[None, :]).astype(BF16)
    return jnp.concatenate([one, one], axis=0), one.T


def combine_kernel(place_ref, count_ref, base_ref, part_ref, out_ref):
    kept = count_ref[pl.program_id(0)]
    base = base_ref[0]
    row = lax.broadcasted_iota(jnp.int32, base.shape, 0)
    part = jnp.where(row < kept, part_ref[0].astype(F32), 0.0)
    out_ref[0] = (base.astype(F32) + part).astype(BF16)


def combine_call(place, kept, base, part):
    count, span, width = base.shape
    block = (1, span, width)
    return pl.pallas_call(
        combine_kernel,
        grid_spec=pltpu.PrefetchScalarGridSpec(
            num_scalar_prefetch=2,
            grid=(count,),
            in_specs=[
                pl.BlockSpec(block, lambda s, place, kept: (s, 0, 0)),
                pl.BlockSpec(block, lambda s, place, kept: (place[s], 0, 0)),
            ],
            out_specs=pl.BlockSpec(block, lambda s, place, kept: (s, 0, 0)),
        ),
        out_shape=jax.ShapeDtypeStruct(base.shape, BF16),
        name="combine",
    )(place, kept, base, part)


def peers_of(n):
    return [(away, turn) for away in range(n // 2) for turn in range(2) if away or turn]


def enter(n, me):
    barrier = pltpu.get_barrier_semaphore()
    for away, turn in peers_of(n):
        pl.semaphore_signal(barrier, inc=1, device_id={"fsdp": peer_at(n, me, away, turn)}, device_id_type=MESH)
    pl.semaphore_wait(barrier, n - 1)


def peer_at(n, me, away, turn):
    chip = lax.rem(lax.div(me, 2) + away, n // 2)
    return 2 * chip + lax.rem(lax.rem(me, 2) + turn, 2)


def sender_at(n, me, away, turn):
    chip = lax.rem(lax.div(me, 2) + n // 2 - away, n // 2)
    return 2 * chip + lax.rem(lax.rem(me, 2) + turn, 2)


def rows_at(index, size):
    return pl.ds(pl.multiple_of(index * size, size), size)


def start_kernel(
    n, sent, shards, small, tok, win, smalls, here, w_send, w_recv, t_send, t_recv, f_send, f_recv, s_send, s_recv
):
    me = lax.axis_index("fsdp")
    core = lax.rem(me, 2)
    chip = lax.div(me, 2)
    partner = 2 * chip + 1 - core
    span, rows = sent.shape[1], shards.shape[1]
    enter(n, me)
    pending = []
    for index, (away, turn) in enumerate(peers_of(n)):
        peer = peer_at(n, me, away, turn)
        theirs = lax.rem(core + turn, 2)

        def push(src, dst, send, recv):
            copy = pltpu.make_async_remote_copy(
                src_ref=src, dst_ref=dst, send_sem=send, recv_sem=recv, device_id={"fsdp": peer}, device_id_type=MESH
            )
            copy.start()
            pending.append(copy)

        push(sent.at[peer], tok.at[theirs, rows_at(me, span)], t_send.at[index], t_recv.at[index])
        push(shards.at[theirs], win.at[rows_at(me, rows)], w_send.at[index], w_recv.at[index])
        push(small, smalls.at[me], s_send.at[index], s_recv.at[index])
    local = [
        pltpu.make_async_copy(sent.at[me], tok.at[core, rows_at(me, span)], here.at[0]),
        pltpu.make_async_copy(sent.at[partner], tok.at[1 - core, rows_at(me, span)], here.at[1]),
        pltpu.make_async_copy(shards.at[core], win.at[rows_at(me, rows)], here.at[2]),
        pltpu.make_async_copy(small, smalls.at[me], here.at[3]),
    ]
    for copy in local:
        copy.start()

    def forward(index, src, owner):
        copy = pltpu.make_async_remote_copy(
            src_ref=src, dst_ref=tok.at[core, rows_at(owner, span)], send_sem=f_send.at[index],
            recv_sem=f_recv.at[index], device_id={"fsdp": partner}, device_id_type=MESH,
        )
        copy.start()
        return copy

    passed = [forward(0, sent.at[me], me)]
    for index, (away, turn) in enumerate(peers_of(n)):
        owner = sender_at(n, me, away, turn)
        block = tok.at[core, rows_at(owner, span)]
        pltpu.make_async_remote_copy(
            src_ref=block, dst_ref=block, send_sem=t_send.at[index], recv_sem=t_recv.at[index],
            device_id={"fsdp": partner}, device_id_type=MESH,
        ).wait_recv()
        if away:
            passed.append(forward(index, block, owner))
    for copy in passed:
        copy.wait()
    for copy in pending:
        copy.wait_send()
    for index, (away, turn) in enumerate(peers_of(n)):
        owner = sender_at(n, me, away, turn)
        checks = [(win.at[rows_at(owner, rows)], w_send, w_recv), (smalls.at[owner], s_send, s_recv)]
        for block, send, recv in checks:
            pltpu.make_async_remote_copy(
                src_ref=block, dst_ref=block, send_sem=send.at[index], recv_sem=recv.at[index],
                device_id={"fsdp": partner}, device_id_type=MESH,
            ).wait_recv()
    for copy in local:
        copy.wait()


def start_call(n, sent, shards, small):
    span, width = sent.shape[1:]
    _, rows, wide = shards.shape
    count = n - 1
    anywhere = pl.BlockSpec(memory_space=pl.ANY)
    return pl.pallas_call(
        functools.partial(start_kernel, n),
        out_shape=[
            jax.ShapeDtypeStruct((2, n * span, width), BF16),
            jax.ShapeDtypeStruct((n * rows, wide), BF16),
            jax.ShapeDtypeStruct((n,) + small.shape, BF16),
        ],
        in_specs=[anywhere] * 3,
        out_specs=[anywhere] * 3,
        scratch_shapes=[pltpu.SemaphoreType.DMA((4,))] + [pltpu.SemaphoreType.DMA((count,))] * 8,
        compiler_params=pltpu.CompilerParams(collective_id=0, has_side_effects=True),
        name="start",
    )(sent, shards, small)


def exchange_kernel(
    bp, ss_ref, v_ref, branch, rv_ref, mine, theirs, ss_in, v_in, here, put, b_send, b_recv, s_send, s_recv
):
    me = lax.axis_index("fsdp")
    core = lax.rem(me, 2)
    partner = 2 * lax.div(me, 2) + 1 - core
    length, width = mine.shape
    blocks = length // BLOCK
    barrier = pltpu.get_barrier_semaphore()
    pl.semaphore_signal(barrier, inc=1, device_id={"fsdp": partner}, device_id_type=MESH)
    pl.semaphore_wait(barrier, 1)

    def remote(src, dst, send, recv):
        return pltpu.make_async_remote_copy(
            src_ref=src, dst_ref=dst, send_sem=send, recv_sem=recv, device_id={"fsdp": partner}, device_id_type=MESH
        )

    load = pltpu.make_async_copy(bp.at[core], mine, here.at[0])
    load.start()
    copies = [
        remote(ss_ref, ss_in, s_send.at[0], s_recv.at[0]),
        remote(v_ref, v_in, s_send.at[1], s_recv.at[1]),
    ]
    for b in range(blocks):
        at = pl.ds(b * BLOCK, BLOCK)
        copies.append(remote(bp.at[1 - core, at], theirs.at[at], b_send.at[b], b_recv.at[b]))
    for copy in copies:
        copy.start()
    for copy in copies[:2]:
        copy.wait_recv()
    scale = lax.rsqrt((ss_ref[...] + ss_in[...]) * (1.0 / INNER) + EPS)
    coef = scale * scale * scale * (v_ref[...] + v_in[...]) * (1.0 / INNER)
    sub = lax.rem(lax.broadcasted_iota(jnp.int32, scale.shape, 0), 8)
    rv_ref[...] = jnp.where(sub == 0, scale, coef)
    load.wait()
    puts = []
    for b in range(blocks):
        at = pl.ds(b * BLOCK, BLOCK)
        copies[2 + b].wait_recv()
        rows = rv_ref[pl.ds(pl.multiple_of((core * blocks + b) * 8, 8), 8), :]
        column = jnp.concatenate([rows, jnp.zeros((LANES - 8, BLOCK), F32)], axis=0).T[:, 0:1]
        mine[at, :] = ((mine[at, :].astype(F32) + theirs[at, :].astype(F32)) * column).astype(BF16)
        copy = pltpu.make_async_copy(mine.at[at], branch.at[at], put.at[b])
        copy.start()
        puts.append(copy)
    for copy in copies:
        copy.wait_send()
    for copy in puts:
        copy.wait()


def exchange_call(bp, ss, v):
    _, length, width = bp.shape
    blocks = length // BLOCK
    vmem = pl.BlockSpec(memory_space=pltpu.VMEM)
    anywhere = pl.BlockSpec(memory_space=pl.ANY)
    dma = pltpu.SemaphoreType.DMA
    return pl.pallas_call(
        exchange_kernel,
        out_shape=[jax.ShapeDtypeStruct((length, width), BF16), jax.ShapeDtypeStruct(ss.shape, F32)],
        in_specs=[anywhere, vmem, vmem],
        out_specs=[anywhere, vmem],
        scratch_shapes=[
            pltpu.VMEM((length, width), BF16), pltpu.VMEM((length, width), BF16),
            pltpu.VMEM(ss.shape, F32), pltpu.VMEM(ss.shape, F32),
            dma((1,)), dma((blocks,)), dma((blocks,)), dma((blocks,)), dma((2,)), dma((2,)),
        ],
        compiler_params=pltpu.CompilerParams(
            collective_id=2, has_side_effects=True, vmem_limit_bytes=30 * 1024 * 1024
        ),
        name="exchange",
    )(bp, ss, v)


def finish_kernel(
    n, planes, cuts, groups, length_ref, gn, tok, gain_ref, dwin, dwout, sums,
    back, w_ref, o_ref, sums_ref,
    gn_mine, gn_theirs, hidden, grad, dgain, w_own, w_in, o_own, o_in, w_give, w_pair, w_chip, z_in, oz_in, z_out,
    oz_out, w_all, o_all, s_own, s_in, d_in, s_tot, s_up,
    here, g_send, g_recv, b_send, b_recv, w_send, w_recv, o_send, o_recv, p_send, p_recv,
    z_send, z_recv, oz_send, oz_recv, y_send, y_recv, oy_send, oy_recv, s_send, s_recv, d_send, d_recv,
    u_send, u_recv,
):
    me = lax.axis_index("fsdp")
    level = lax.axis_index("rep")
    core = lax.rem(me, 2)
    chip = lax.div(me, 2)
    partner = 2 * chip + 1 - core
    span = back.shape[1]
    chip_rows = w_own.shape[0]
    rows = chip_rows // 2
    outs = o_own.shape[0]
    part, opart = rows // planes, outs // planes
    others = n // 2 - 1
    tile = 16
    barrier = pltpu.get_barrier_semaphore()
    for away, turn in peers_of(n):
        pl.semaphore_signal(barrier, inc=1, device_id={"fsdp": peer_at(n, me, away, turn)}, device_id_type=MESH)
    for up in range(1, planes):
        pl.semaphore_signal(barrier, inc=1, device_id={"rep": lax.rem(level + up, planes)}, device_id_type=MESH)
    pl.semaphore_wait(barrier, n - 1 + planes - 1)

    def remote(src, dst, send, recv, where):
        return pltpu.make_async_remote_copy(
            src_ref=src, dst_ref=dst, send_sem=send, recv_sem=recv, device_id=where, device_id_type=MESH
        )

    def arrived(block, send, recv):
        remote(block, block, send, recv, {"fsdp": partner}).wait_recv()

    pending = []

    def push(src, dst, send, recv, where):
        copy = remote(src, dst, send, recv, where)
        copy.start()
        pending.append(copy)

    def above(up):
        return lax.rem(level + up, planes)

    loads = [
        pltpu.make_async_copy(dwin.at[rows_at(chip, chip_rows)], w_own, here.at[0]),
        pltpu.make_async_copy(dwout.at[rows_at(chip, outs)], o_own, here.at[1]),
        pltpu.make_async_copy(gn.at[core], gn_mine, here.at[2]),
        pltpu.make_async_copy(tok.at[core], hidden, here.at[3]),
        pltpu.make_async_copy(sums.at[me], s_own, here.at[4]),
    ]
    for copy in loads:
        copy.start()
    everyone = [(0, 0)] + peers_of(n)
    for index, (away, turn) in enumerate(everyone):
        block = rows_at(peer_at(n, me, away, turn), span)
        push(gn.at[1 - core, block], gn_theirs.at[block], g_send.at[index], g_recv.at[index], {"fsdp": partner})
    for c, cols in enumerate(cuts):
        for i in range(others):
            target = {"fsdp": peer_at(n, me, i + 1, 0)}
            other = lax.rem(chip + i + 1, n // 2)
            k = c * others + i
            push(
                dwin.at[rows_at(other, chip_rows), cols], w_in.at[i, :, cols], w_send.at[k], w_recv.at[k], target
            )
    for i in range(others):
        target = {"fsdp": peer_at(n, me, i + 1, 0)}
        other = lax.rem(chip + i + 1, n // 2)
        push(dwout.at[rows_at(other, outs)], o_in.at[i], o_send.at[i], o_recv.at[i], target)
    for index, (away, turn) in enumerate(everyone):
        if index:
            peer = peer_at(n, me, away, turn)
            push(sums.at[peer], s_in.at[index - 1], s_send.at[index], s_recv.at[index], {"fsdp": peer})
    for copy in loads[2:]:
        copy.wait()
    dgain[...] = jnp.zeros_like(dgain)
    step = 64

    def norm_back(index):
        away, turn = everyone[index]
        target = peer_at(n, me, away, turn)
        block = rows_at(target, span)
        sender_index = everyone.index((away, 1 - turn))
        arrived(gn_theirs.at[block], g_send.at[sender_index], g_recv.at[sender_index])
        first = target * span

        @pl.loop(0, span // step)
        def _(i):
            at = pl.ds(pl.multiple_of(first + i * step, step), step)
            position = first + i * step + lax.broadcasted_iota(jnp.int32, (step, gn_mine.shape[1]), 0)
            total = gn_mine[at, :].astype(F32) + gn_theirs[at, :].astype(F32)
            total = jnp.where(position < length_ref[0], total, 0.0)
            h = hidden[at, :].astype(F32)
            inv = lax.rsqrt(jnp.mean(h * h, axis=1, keepdims=True) + EPS)
            normal = h * inv
            dgain[0:1, :] += jnp.sum(total * normal, axis=0, keepdims=True)
            scaled = total * gain_ref[0:1, :]
            mean = jnp.mean(scaled * normal, axis=1, keepdims=True)
            grad[at, :] = (inv * (scaled - normal * mean)).astype(BF16)

    for index in range(n):
        norm_back(index)
    seg = dgain.shape[1] // n
    for index, (away, turn) in enumerate(everyone):
        if index:
            peer = peer_at(n, me, away, turn)
            cols = pl.ds(pl.multiple_of(peer * seg, seg), seg)
            push(dgain.at[:, cols], d_in.at[index - 1], d_send.at[index], d_recv.at[index], {"fsdp": peer})

    own_block = pltpu.make_async_copy(grad.at[rows_at(me, span)], back.at[me], here.at[5])
    own_block.start()
    waiting = list(range(1, n))

    def give_back(count):
        for index in waiting[:count]:
            away, turn = everyone[index]
            peer = peer_at(n, me, away, turn)
            push(grad.at[rows_at(peer, span)], back.at[me], b_send.at[index], b_recv.at[index], {"fsdp": peer})
        del waiting[:count]

    def add_up(own, pieces, at, cols):
        total = own[at, cols].astype(F32)
        for i in range(pieces.shape[0]):
            total = total + pieces[i, at, cols].astype(F32)
        return total.astype(BF16)

    def stage_sum(c):
        cols = cuts[c]
        for i in range(others):
            k = c * others + i
            arrived(w_in.at[i, :, cols], w_send.at[k], w_recv.at[k])

        @pl.loop(0, rows // tile)
        def _(i):
            at = pl.ds(pl.multiple_of((1 - core) * rows + i * tile, tile), tile)
            w_give[pl.ds(pl.multiple_of(i * tile, tile), tile), cols] = add_up(w_own, w_in, at, cols)

        push(w_give.at[:, cols], w_pair.at[:, cols], p_send.at[c], p_recv.at[c], {"fsdp": partner})

        @pl.loop(0, rows // tile)
        def _(i):
            at = pl.ds(pl.multiple_of(core * rows + i * tile, tile), tile)
            w_chip[core, pl.ds(pl.multiple_of(i * tile, tile), tile), cols] = add_up(w_own, w_in, at, cols)

    def stage_up(c):
        cols = cuts[c]
        arrived(w_pair.at[:, cols], p_send.at[c], p_recv.at[c])
        w_chip[1 - core, :, cols] = w_pair[:, cols]
        for up in range(1, planes):
            k = c * (planes - 1) + up - 1
            push(
                w_chip.at[:, rows_at(above(up), part), cols], z_in.at[up - 1, :, :, cols],
                z_send.at[k], z_recv.at[k], {"rep": above(up)},
            )

    def stage_total(c):
        cols = cuts[c]
        for up in range(1, planes):
            k = c * (planes - 1) + up - 1
            arrived(z_in.at[up - 1, :, :, cols], z_send.at[k], z_recv.at[k])
        at = rows_at(level, part)
        for q in range(2):
            total = w_chip[q, at, cols].astype(F32)
            for k in range(planes - 1):
                total = total + z_in[k, q, :, cols].astype(F32)
            z_out[q, :, cols] = total.astype(BF16)
            w_all[q, at, cols] = total.astype(BF16)
        for up in range(1, planes):
            k = c * (planes - 1) + up - 1
            push(z_out.at[:, :, cols], w_all.at[:, at, cols], y_send.at[k], y_recv.at[k], {"rep": above(up)})

    for copy in loads[:2]:
        copy.wait()
    count = len(cuts)
    for c in range(count + 2):
        if c < count:
            stage_sum(c)
            give_back(2)
        if c == count:
            give_back(n)
            for i in range(others):
                arrived(o_in.at[i], o_send.at[i], o_recv.at[i])

            @pl.loop(0, outs // tile)
            def _(i):
                at = pl.ds(pl.multiple_of(i * tile, tile), tile)
                o_own[at, :] = add_up(o_own, o_in, at, slice(None))

            for up in range(1, planes):
                push(
                    o_own.at[rows_at(above(up), opart)], oz_in.at[up - 1], oz_send.at[up - 1], oz_recv.at[up - 1],
                    {"rep": above(up)},
                )
        if 1 <= c <= count:
            stage_up(c - 1)
        if c >= 2:
            stage_total(c - 2)

    total = s_own[...]
    for index, (away, turn) in enumerate(everyone):
        if index:
            arrived(s_in.at[index - 1], s_send.at[index], s_recv.at[index])
            arrived(d_in.at[index - 1], d_send.at[index], d_recv.at[index])
            total = total + s_in[index - 1]
    heads = s_own.shape[0]
    s_tot[0:heads, :] = total
    mine = dgain[:, pl.ds(pl.multiple_of(me * seg, seg), seg)]
    for index in range(n - 1):
        mine = mine + d_in[index]
    s_tot[heads : heads + 8, :] = mine
    for up in range(1, planes):
        push(s_tot, s_up.at[up - 1], u_send.at[up - 1], u_recv.at[up - 1], {"rep": above(up)})
    for i in range(planes - 1):
        arrived(oz_in.at[i], oz_send.at[i], oz_recv.at[i])
    at = rows_at(level, opart)
    total = o_own[at, :].astype(F32)
    for k in range(planes - 1):
        total = total + oz_in[k].astype(F32)
    oz_out[...] = total.astype(BF16)
    o_all[at, :] = total.astype(BF16)
    for up in range(1, planes):
        push(oz_out, o_all.at[at], oy_send.at[up - 1], oy_recv.at[up - 1], {"rep": above(up)})
    for i in range(planes - 1):
        arrived(s_up.at[i], u_send.at[i], u_recv.at[i])
    total = s_tot[...]
    for k in range(planes - 1):
        total = total + s_up[k]
    sums_ref[...] = total
    for c, cols in enumerate(cuts):
        for up in range(1, planes):
            below = lax.rem(level + planes - up, planes)
            k = c * (planes - 1) + up - 1
            arrived(w_all.at[:, rows_at(below, part), cols], y_send.at[k], y_recv.at[k])
    inner, group, heads = groups
    for g in range(2 * inner // group):
        q, at = g % 2, g // 2 * group
        w_ref[:, g * group : (g + 1) * group] = w_all[q, :, at : at + group].astype(F32)
        w_ref[:, 2 * inner + g * group : 2 * inner + (g + 1) * group] = (
            w_all[q, :, inner + at : inner + at + group].astype(F32)
        )
    both = w_all[0, :, 2 * inner : 2 * inner + 2 * STATE].astype(F32)
    both = both + w_all[1, :, 2 * inner : 2 * inner + 2 * STATE].astype(F32)
    w_ref[:, 4 * inner : 4 * inner + 2 * STATE] = both
    first = 2 * inner + 2 * STATE
    tails = [w_all[q, :, first : first + LANES].astype(F32) for q in range(2)]
    size = group // HEADDIM
    pieces = [tails[g % 2][:, g // 2 * size : (g // 2 + 1) * size] for g in range(2 * inner // group)]
    w_ref[:, 4 * inner + 2 * STATE :] = jnp.concatenate(pieces, axis=1)
    for up in range(1, planes):
        below = lax.rem(level + planes - up, planes)
        arrived(o_all.at[rows_at(below, opart)], oy_send.at[up - 1], oy_recv.at[up - 1])
    o_ref[...] = o_all[...].astype(F32)
    for index, (away, turn) in enumerate(everyone):
        if index:
            owner = sender_at(n, me, away, turn)
            arrived(back.at[owner], b_send.at[index], b_recv.at[index])
    for copy in pending:
        copy.wait_send()
    own_block.wait()


def finish_call(n, planes, group, length, gn, tok, gain, dwin, dwout, sums):
    _, total, width = gn.shape
    span = total // n
    wide = dwin.shape[1]
    inner = dwout.shape[0]
    heads = inner // HEADDIM
    chip_rows, outs = dwin.shape[0] // (n // 2), inner // (n // 2)
    rows = chip_rows // 2
    others = n // 2 - 1
    lane_tiles = wide // LANES
    pieces = 4
    bounds = [(lane_tiles * i + pieces - 1) // pieces * LANES for i in range(pieces + 1)]
    cuts = [pl.ds(bounds[i], bounds[i + 1] - bounds[i]) for i in range(pieces)]
    anywhere = pl.BlockSpec(memory_space=pl.ANY)
    vmem = pl.BlockSpec(memory_space=pltpu.VMEM)
    dma = pltpu.SemaphoreType.DMA
    up = planes - 1
    held = sums.shape[1]
    return pl.pallas_call(
        functools.partial(finish_kernel, n, planes, cuts, (inner, group, heads)),
        out_shape=[
            jax.ShapeDtypeStruct((n, span, width), BF16),
            jax.ShapeDtypeStruct((rows, 4 * inner + 2 * STATE + 2 * heads), F32),
            jax.ShapeDtypeStruct((outs, width), F32),
            jax.ShapeDtypeStruct((held + 8, LANES), F32),
        ],
        in_specs=[pl.BlockSpec(memory_space=pltpu.SMEM), anywhere, anywhere, vmem, anywhere, anywhere, anywhere],
        out_specs=[anywhere, vmem, vmem, vmem],
        scratch_shapes=[
            pltpu.VMEM((total, width), BF16), pltpu.VMEM((total, width), BF16), pltpu.VMEM((total, width), BF16),
            pltpu.VMEM((total, width), BF16), pltpu.VMEM((8, width), F32),
            pltpu.VMEM((chip_rows, wide), BF16), pltpu.VMEM((others, chip_rows, wide), BF16),
            pltpu.VMEM((outs, width), BF16), pltpu.VMEM((others, outs, width), BF16),
            pltpu.VMEM((rows, wide), BF16), pltpu.VMEM((rows, wide), BF16), pltpu.VMEM((2, rows, wide), BF16),
            pltpu.VMEM((up, 2, rows // planes, wide), BF16), pltpu.VMEM((up, outs // planes, width), BF16),
            pltpu.VMEM((2, rows // planes, wide), BF16), pltpu.VMEM((outs // planes, width), BF16),
            pltpu.VMEM((2, rows, wide), BF16), pltpu.VMEM((outs, width), BF16),
            pltpu.VMEM((held, LANES), F32), pltpu.VMEM((n - 1, held, LANES), F32),
            pltpu.VMEM((n - 1, 8, LANES), F32), pltpu.VMEM((held + 8, LANES), F32),
            pltpu.VMEM((up, held + 8, LANES), F32),
            dma((6,)), dma((n,)), dma((n,)), dma((n,)), dma((n,)),
            dma((pieces * others,)), dma((pieces * others,)), dma((others,)), dma((others,)),
            dma((pieces,)), dma((pieces,)), dma((pieces * up,)), dma((pieces * up,)), dma((up,)), dma((up,)),
            dma((pieces * up,)), dma((pieces * up,)), dma((up,)), dma((up,)),
            dma((n,)), dma((n,)), dma((n,)), dma((n,)), dma((up,)), dma((up,)),
        ],
        compiler_params=pltpu.CompilerParams(
            collective_id=1, has_side_effects=True, vmem_limit_bytes=60 * 1024 * 1024
        ),
        name="finish",
    )(length, gn, tok, gain, dwin, dwout, sums)


def pairs_of(n):
    return [[2 * c, 2 * c + 1] for c in range(n // 2)]


def columns_of(n):
    return [list(range(q, n, 2)) for q in range(2)]


def halves(array, axis, group):
    shape = array.shape
    view = array.reshape(shape[:axis] + (shape[axis] // (2 * group), 2, group) + shape[axis + 1 :])
    out = []
    for q in range(2):
        part = lax.index_in_dim(view, q, axis + 1, keepdims=False)
        out.append(part.reshape(shape[:axis] + (shape[axis] // 2,) + shape[axis + 1 :]))
    return out


def interleave(first, second, axis, group):
    shape = first.shape
    views = [
        part.reshape(shape[:axis] + (shape[axis] // group, 1, group) + shape[axis + 1 :]) for part in (first, second)
    ]
    return jnp.concatenate(views, axis=axis + 1).reshape(shape[:axis] + (2 * shape[axis],) + shape[axis + 1 :])


def body(
    tokens, cotangent, lengths, dealing, norm_gain, in_weight, conv_weight, conv_bias, dt_bias, a_log, skip_gain,
    out_gain, out_weight,
):
    n = lax.axis_size("fsdp")
    me = lax.axis_index("fsdp")
    core = lax.rem(me, 2)
    pairs, columns = pairs_of(n), columns_of(n)
    local_tokens, local_grad = tokens[0], cotangent[0]
    count, span, width = local_tokens.shape
    length = span * n
    inner = INNER // 2
    heads = HEADS // 2
    group = max(HEADDIM, INNER // n)
    blocks = length // BLOCK
    rows = in_weight.shape[0]

    slots = jnp.arange(count, dtype=jnp.int32)
    own = jnp.sum(jnp.where(dealing[0][:, None] == slots[None, :], lengths[0][None, :], 0), axis=1)
    ahead = (own[None, :] > own[:, None]) | ((own[None, :] == own[:, None]) & (slots[None, :] < slots[:, None]))
    rank = jnp.sum(ahead.astype(jnp.int32), axis=1)
    place = jnp.where(rank < count // 2, 2 * rank, 2 * (count - 1 - rank) + 1)
    source = jnp.sum(jnp.where(place[None, :] == slots[:, None], slots[None, :], 0), axis=1)
    placed = jnp.sum(jnp.where(place[None, :] == slots[:, None], own[None, :], 0), axis=1)
    chip_lens = lax.dynamic_slice_in_dim(placed, me - core, 2)
    chip_blocks = (chip_lens + BLOCK - 1) // BLOCK

    main = INNER + INNER + 2 * STATE
    gates = halves(in_weight[:, :INNER], 1, group)
    vals = halves(in_weight[:, INNER : 2 * INNER], 1, group)
    both = in_weight[:, 2 * INNER : main]
    steps = halves(in_weight[:, main:], 1, group // HEADDIM)
    pad = jnp.zeros((rows, LANES - heads), BF16)
    shards = jnp.stack([jnp.concatenate([gates[q], vals[q], both, steps[q], pad], axis=1) for q in range(2)])
    aligned = INNER // n >= HEADDIM
    small = jnp.concatenate([norm_gain, conv_weight.reshape(-1), conv_bias, out_gain])
    room = -(-small.shape[0] // (16 * LANES)) * 16
    small = jnp.pad(small, (0, room * LANES - small.shape[0])).reshape(room, LANES)
    sent_grad = jnp.take(local_grad, source, axis=0)
    tok, win, smalls = start_call(n, jnp.take(local_tokens, source, axis=0), shards, small)
    tok, sent_grad, out_weight = lax.optimization_barrier((tok, sent_grad, out_weight))
    smalls = smalls.reshape(n, -1).astype(F32)
    own_grad = lax.all_to_all(sent_grad, "fsdp", split_axis=0, concat_axis=0, tiled=True)
    cot = lax.all_gather(own_grad.reshape(1, length, width), "fsdp", axis=0, tiled=True, axis_index_groups=pairs)
    if aligned:
        wout = lax.all_gather(out_weight, "fsdp", axis=0, tiled=True, axis_index_groups=columns)
    else:
        whole = lax.all_gather(out_weight, "fsdp", axis=0, tiled=True)
        wout = lax.dynamic_index_in_dim(jnp.stack(halves(whole, 0, group)), core, 0, keepdims=False)
    cuts = [norm_gain.shape[0], conv_weight.size, conv_bias.shape[0], out_gain.shape[0]]
    ends = [sum(cuts[: i + 1]) for i in range(4)]
    first_gain = smalls[:, : ends[0]].reshape(-1)
    conv_w = smalls[:, ends[0] : ends[1]].reshape(n, CONV, -1).transpose(1, 0, 2).reshape(CONV, -1)
    conv_b = smalls[:, ends[1] : ends[2]].reshape(1, -1)
    gated_gain = smalls[:, ends[2] : ends[3]].reshape(1, -1)

    def half_of(array, axis, size):
        return lax.dynamic_index_in_dim(jnp.stack(halves(array, axis, size)), core, 0, keepdims=False)

    conv_all = jnp.concatenate([conv_w, conv_b, jnp.zeros((3, conv_w.shape[1]), F32)], axis=0)
    conv_all = jnp.concatenate([half_of(conv_all[:, :INNER], 1, group), conv_all[:, INNER:]], axis=1)
    head_rows = jnp.stack([dt_bias, jnp.exp(a_log), skip_gain] + [jnp.zeros_like(dt_bias)] * 5)
    head_rows = half_of(head_rows, 1, group // HEADDIM)
    dwide = jnp.broadcast_to(jnp.repeat(head_rows[2:3], HEADDIM, axis=1), (8, inner))
    hp = jnp.concatenate([head_rows, jnp.zeros((8, LANES - heads), F32)], axis=1)
    og = jnp.broadcast_to(half_of(gated_gain, 1, group), (8, inner))
    gain = jnp.broadcast_to(first_gain[None, :], (8, width))
    cb = jnp.broadcast_to(conv_all[CONV : CONV + 1], conv_all.shape)
    expand, collect = matrices(inner)
    args = (gain, win, conv_all, cb, hp, dwide, og, expand)
    gate, cin, raw, y, states, ss, mixing = fwd_call(chip_blocks, tok, *args)

    gm, v, bp = mid_call(chip_blocks, chip_lens, cot, mixing, wout)
    branch, rv = exchange_call(bp, ss, v)

    def restore(part):
        return lax.all_to_all(part.reshape(n, span, width), "fsdp", split_axis=0, concat_axis=0, tiled=True)

    kept = jnp.clip(own - me * span, 0, span)
    output = combine_call(place, kept, local_tokens, restore(branch))[None]
    gn, dwin, dwout, dcw, dhp, dog, ddw = bwd_call(
        chip_blocks, chip_lens, tok, cot, gain, win, gm, *args[2:], collect, gate, cin, raw, y, states, rv
    )
    def widen(half, axis, size):
        zero = jnp.zeros_like(half)
        return interleave(jnp.where(core == 0, half, zero), jnp.where(core == 1, half, zero), axis, size)

    own_len = lax.dynamic_slice_in_dim(chip_lens, core, 1)
    dconv = jnp.concatenate([widen(dcw[: CONV + 1, :inner], 1, group), dcw[: CONV + 1, inner:]], axis=1)
    dskip = jnp.sum(ddw[0].reshape(heads, HEADDIM), axis=1)
    dheads = widen(jnp.concatenate([dhp[:2, :heads], dskip[None]], axis=0), 1, group // HEADDIM)
    dog = widen(dog[0], 0, group)
    planes = lax.axis_size("rep")
    if aligned and rows % (16 * planes) == 0 and out_weight.shape[0] % (16 * planes) == 0:
        sums = jnp.concatenate(
            [
                dconv.reshape(CONV + 1, n, -1).transpose(1, 0, 2).reshape(n, -1),
                dog.reshape(n, -1),
                jnp.broadcast_to(dheads.reshape(1, -1), (n, dheads.size)),
            ],
            axis=1,
        )
        room = -(-sums.shape[1] // (8 * LANES)) * 8
        sums = jnp.pad(sums, ((0, 0), (0, room * LANES - sums.shape[1]))).reshape(n, room, LANES)
        back, dwin, dwout, sums = finish_call(n, planes, group, own_len, gn, tok, gain, dwin, dwout, sums)
        flat = sums.reshape(-1)
        c0 = dconv.size // n
        c1 = c0 + dog.size // n
        dheads = flat[c1 : c1 + dheads.size].reshape(dheads.shape)
        dog, dgain = flat[c0:c1], sums[room, : width // n]
        dconv = flat[:c0].reshape(CONV + 1, -1)
    else:
        other = lax.dynamic_index_in_dim(gn, 1 - core, 0, keepdims=False)
        other = lax.ppermute(other, "fsdp", [(2 * c + q, 2 * c + 1 - q) for c in range(n // 2) for q in range(2)])
        mine = lax.dynamic_index_in_dim(gn, core, 0, keepdims=False)
        hidden = lax.dynamic_index_in_dim(tok, core, 0, keepdims=False).astype(F32)
        inv = lax.rsqrt(jnp.mean(hidden * hidden, axis=-1, keepdims=True) + EPS)
        position = jnp.arange(length, dtype=jnp.int32)[:, None]
        grad_normed = jnp.where(position < own_len[0], mine.astype(F32) + other.astype(F32), 0.0)
        dgain = jnp.sum(grad_normed * hidden * inv, axis=0)
        scaled = grad_normed * first_gain[None, :]
        grad_hidden = inv * scaled - hidden * (inv * inv * inv) * jnp.mean(scaled * hidden, axis=-1, keepdims=True)
        back = restore(grad_hidden.astype(BF16))
        dwin = lax.psum_scatter(
            dwin.astype(F32), "fsdp", scatter_dimension=0, tiled=True, axis_index_groups=columns
        )
        dwin = lax.psum(dwin, "rep").reshape(2, rows, -1)
        dwin = lax.all_to_all(dwin, "fsdp", split_axis=0, concat_axis=0, tiled=True, axis_index_groups=pairs)
        if aligned:
            dwout = lax.psum_scatter(
                dwout.astype(F32), "fsdp", scatter_dimension=0, tiled=True, axis_index_groups=columns
            )
        else:
            wide_grad = widen(dwout.astype(F32), 0, group)
            dwout = lax.psum_scatter(wide_grad, "fsdp", scatter_dimension=0, tiled=True)
        dwout = lax.psum(dwout, "rep")
        c0, c1, c2 = inner, 2 * inner, 2 * inner + 2 * STATE
        dwin = jnp.concatenate(
            [
                interleave(dwin[0, :, :c0], dwin[1, :, :c0], 1, group),
                interleave(dwin[0, :, c0:c1], dwin[1, :, c0:c1], 1, group),
                dwin[0, :, c1:c2] + dwin[1, :, c1:c2],
                interleave(dwin[0, :, c2 : c2 + heads], dwin[1, :, c2 : c2 + heads], 1, group // HEADDIM),
            ],
            axis=1,
        )
        dconv, dheads, dog, dgain = lax.psum((dconv, dheads, dog, dgain), ("rep", "fsdp"))

        def shard(array):
            size = array.shape[-1] // n
            return lax.dynamic_slice_in_dim(array, me * size, size, axis=array.ndim - 1)

        dconv, dog, dgain = shard(dconv), shard(dog), shard(dgain)
    token_grad = combine_call(place, kept, local_grad, back)[None]
    return (
        output, token_grad, dgain, dwin, dconv[:CONV], dconv[CONV], dheads[0], dheads[1], dheads[2], dog, dwout,
    )


def solution(mesh):
    row = P("rep", None, "fsdp", None)
    per = P("rep", None)
    in_specs = (
        row, row, per, per, P("fsdp"), P("fsdp", None), P(None, "fsdp"), P("fsdp"), P(), P(), P(), P("fsdp"),
        P("fsdp", None),
    )
    out_specs = (
        row, row, P("fsdp"), P("fsdp", None), P(None, "fsdp"), P("fsdp"), P(), P(), P(), P("fsdp"), P("fsdp", None),
    )
    return jax.shard_map(body, mesh=mesh, in_specs=in_specs, out_specs=out_specs, check_vma=False)
```

time: 2210 us -> 606 us (0.27)
  matrix products: 696 us -> 0 us
  local copies, waits for them, and re-layouts: 613 us -> 36.6 us
  other arithmetic: 498 us -> 15.5 us
  Pallas kernels: 0 us -> 462 us
  blocking collectives: 306 us -> 0 us
  waiting for transfers between devices: 39.7 us -> 64.2 us
    dot_general x121 -> x0, matrix products: 696 us -> none  [the longest x24 302 us: block_step(): jnp.einsum('hts,shp->thp', weights, by_head, precision=largest_value)]
    pallas_call x0 -> x8, Pallas kernels: none -> 462 us  [the longest x1 149 us: finish_call(): pl.pallas_call(functools.partial(finish_kernel, n, planes, cuts, (inner,...]
    mul x37 -> x0, other arithmetic: 135 us -> none  [the longest x16 41.9 us: block_step(): tail.T[:, :, None] * by_head]
    reduce_sum x23 -> x4, other arithmetic: 122 us -> 1.3 us  [the longest x1 0.85 us: body(): jnp.sum(jnp.where(dealing[0][:, None] == slots[None, :], lengths[0][None,...]
    dynamic_update_slice x56 -> x0, local copies, waits for them, and re-layouts: 104 us -> none  [scan_blocks(): final, outputs = lax.scan(jax.checkpoint(block_step), start, blocks)]
    psum x2 -> x0, blocking collectives: 98.5 us -> none  [the longest x1 76.4 us: body(): lax.psum((middle_grads[4], middle_grads[5], middle_grads[6]), ('rep', 'fs...]
    all_gather x4 -> x0, blocking collectives: 91.9 us -> none  [the longest x1 66.4 us: body(): lax.all_gather(norm_gain, 'fsdp', axis=0, tiled=True)]
    another operation x174 -> x18, local copies, waits for them, and re-layouts: 86.1 us -> 1.74 us  [the longest x6 0.84 us: halves(): part.reshape(shape[:axis] + (shape[axis] // 2,) + shape[axis + 1:])]
  transfers between devices with their start and end apart: 10 -> 4, of which waited for: 1 -> 1; matrix products, arithmetic and copies ran while one was open for 37% -> 4% of each run, Pallas kernels for 0% -> 54%
where the time goes in v1:
time: 606 us; the launch traced here: 602 us
  Pallas kernels  462 us (76%)
  waiting for transfers between devices  64.2 us (11%)
  local copies, waits for them, and re-layouts  36.6 us (6%)
  other arithmetic  15.5 us (3%)
  between operations  14.6 us (2%)
  starting transfers between devices  9.4 us (2%)
    pallas_call x1, Pallas kernels, finish_call(): pl.pallas_call(functools.partial(finish_kernel, n, planes, cuts, (inner,...  149 us
    pallas_call x1, Pallas kernels, bwd_call(): pl.pallas_call(functools.partial(bwd_kernel, inner, heads, blocks), grid_...  116 us
    pallas_call x1, Pallas kernels, start_call(): pl.pallas_call(functools.partial(start_kernel, n), out_shape=[jax.ShapeDt...  105 us
    all_to_all x1, waiting for transfers between devices, body(): lax.all_to_all(sent_grad, 'fsdp', split_axis=0, concat_axis=0, tiled=True)  63.5 us
    pallas_call x1, Pallas kernels, fwd_call(): pl.pallas_call(functools.partial(fwd_kernel, inner, heads), grid_spec=gri...  48 us
    pallas_call x2, Pallas kernels, combine_call(): pl.pallas_call(combine_kernel, grid_spec=pltpu.PrefetchScalarGridSpec(num...  17.4 us
    pallas_call x1, Pallas kernels, mid_call(): pl.pallas_call(mid_kernel, grid_spec=pltpu.PrefetchScalarGridSpec(num_sca...  17.4 us
  transfers between devices with their start and end apart: 4, of which 1 were waited for; matrix products, arithmetic and copies ran while one was open for 4% of the time, Pallas kernels for 54%

profile of v1, /device:TPU:0, one launch (start us, length us, event | category | flops | bytes accessed | tf_op | source)
XLA Modules:
  0.0 602.2 jit_solution(14443889861582275572)
XLA Ops:
  7.2 0.9 select_reduce_fusion.2
  8.4 1.3 fusion.16
  9.7 5.0 gather_fusion.1
  14.7 5.0 gather_fusion
  21.1 0.6 pad_bitcast_fusion.1.small
  21.7 0.3 concatenate.61
  22.0 0.3 concatenate.60
  22.2 1.2 pad_maximum_fusion.shards
  23.4 7.7 %broadcast_select_fusion = (bf16[8,256,1024]{2,1,0:T(8,128)(2,1)}, bf16[8,256,1024]{2,1,0:T(8,128)(2,1)}) fusion(bf16[8,256,1024]{2,1,0:T(8,128)(2,1)} %gather_fusion.1, pred[8]{0:T(512)(128)(4,1)S(1)} %compare_and_fusion, bf16[8,256,1024]{2,1,0:T(8,128)(2,1)} %gather_fusion), kind=kLoop, calls=%fused_computation.2 | loop fusion | flops 4194304 | bytes 16777224 | tf_op jit(solution)/shard_map/jit(_take)/select_n | solution.py:1144
  31.1 104.9 %start.1 = (bf16[2,2048,1024]{2,1,0:T(8,128)(2,1)}, bf16[1024,2432]{1,0:T(8,128)(2,1)}, bf16[8,16,128]{2,1,0:T(8,128)(2,1)}) custom-call(bf16[8,256,1024]{2,1,0:T(8,128)(2,1)} %get-tuple-element.142.sent, bf16[2,128,2432]{2,1,0:T(8,128)(2,1)} %pad_maximum_fusion.shards, bf16[16,128]{1,0:T(8,128)(2,1)} %pad_bitcast_fusion.1.small), custom_call_target="tpu_custom_call" | custom-call | tf_op jit(solution)/shard_map/start/pallas_call | solution.py:675
  136.0 4.6 all-to-all-start
  140.6 0.7 all-gather.5.cloned.1.call-update
  141.6 63.5 %all-to-all-done = bf16[8,256,1024]{2,1,0:T(8,128)(2,1)} async-done(((bf16[8,256,1024]{2,1,0:T(8,128)(2,1)}), bf16[8,256,1024]{2,1,0:T(8,128)(2,1)}, u32[]{:S(2)}, u32[]{:S(2)}) %all-to-all-start) | async-done | bytes 4194336 | tf_op jit(solution)/shard_map/all_to_all | solution.py:1148
  206.7 0.6 concatenate.65.hp_ref
  207.6 0.6 dynamic_slice.25.length_ref
  208.3 0.6 and_select_fusion
  209.0 0.9 add_convert_fusion.expand_ref
  209.8 0.5 subtract_clamp_fusion.count_ref
  210.4 0.6 pad_maximum_fusion.2.cw_ref
  211.0 0.9 fusion.collect_ref
  211.9 0.6 broadcast_in_dim.112.gain_ref
  212.5 0.6 broadcast_in_dim.115.cb_ref
  213.1 0.6 broadcast_in_dim.118.dwide_ref
  213.7 0.6 broadcast_in_dim.120.og_ref
  214.4 48.0 %layer_forward.1 = (f32[2,2048,1024]{2,1,0:T(8,128)}, f32[2,2048,1280]{2,1,0:T(8,128)}, f32[2,2048,128]{2,1,0:T(8,128)}, f32[2,2048,1024]{2,1,0:T(8,128)}, f32[2...) custom-call(s32[2]{0:T(128)} %get-tuple-element.118.nb_ref, ...), custom_call_target="tpu_custom_call" | custom-call | flops 14562623488 | bytes 62914560 | tf_op jit(solution)/shard_map/layer_forward/pallas_call | solution.py:219
  262.4 1.6 copy-done.5
  264.0 17.4 %layer_middle.1 = (f32[2,2048,1024]{2,1,0:T(8,128)}, f32[128,256]{1,0:T(8,128)S(1)}, bf16[2,2048,1024]{2,1,0:T(8,128)(2,1)S(1)}) custom-call(s32[2]{0:T(128)S(1)} %copy-done.3, s32[2]{0:T(128)S(1)} %get-tuple-element.119.len_ref, bf16[2,2048,1024]{2,1,0:T(8,128)(2,1)} %all-gather.3.cloned.1.call-done.cot_ref, f32[2,2048,1024]{2,1,0:T(8,128)} %get-tuple-element.46.sc_ref, ...), custom_call_target="tpu_custom_call" | custom-call | flops 10000000000 | bytes 31457280 | tf_op jit(solution)/shard_map/layer_middle/pallas_call | solution.py:267
  281.4 8.4 %exchange.1 = (bf16[2048,1024]{1,0:T(8,128)(2,1)S(1)}, f32[128,256]{1,0:T(8,128)S(1)}) custom-call(bf16[2,2048,1024]{2,1,0:T(8,128)(2,1)S(1)} %get-tuple-element.48.bp, f32[128,256]{1,0:T(8,128)S(1)} %copy-done.1, f32[128,256]{1,0:T(8,128)S(1)} %get-tuple-element.50.v_ref), custom_call_target="tpu_custom_call" | custom-call | tf_op jit(solution)/shard_map/exchange/pallas_call | solution.py:747
  289.8 2.0 copy-done
  291.8 0.7 copy-done.2
  292.5 4.6 all-to-all-start.1
  297.1 116.5 %layer_backward.1 = (bf16[2,2048,1024]{2,1,0:T(8,128)(2,1)}, bf16[1024,2432]{1,0:T(8,128)(2,1)}, bf16[1024,1024]{1,0:T(8,128)(2,1)}, f32[8,1280]{1,0:T(8,128)}, ...) custom-call(s32[2]{0:T(128)} %get-tuple-element.118.nb_ref, s32[2]{0:T(128)} %copy-done.4, ...), custom_call_target="tpu_custom_call" | custom-call | flops 29125246976 | bytes 104857600 | tf_op jit(solution)/shard_map/layer_backward/pallas_call | solution.py:529
  413.5 0.7 slice.154
  414.2 0.8 slice_select_fusion.1
  415.4 0.8 fusion.7
  416.5 0.7 slice.156
  417.5 0.6 copy.111
  418.2 149.3 %finish.1 = (bf16[8,256,1024]{2,1,0:T(8,128)(2,1)}, f32[128,4384]{1,0:T(8,128)}, f32[256,1024]{1,0:T(8,128)}, f32[24,128]{1,0:T(8,128)}) custom-call(s32[1]{0:T(128)} %dynamic_slice.25.length_ref, bf16[2,2048,1024]{2,1,0:T(8,128)(2,1)} %get-tuple-element.59.gn, bf16[2,2048,1024]{2,1,0:T(8,128)(2,1)} %get-tuple-element.43.tok_ref.tok, ...), custom_call_target="tpu_custom_call" | custom-call | tf_op jit(solution)/shard_map/finish/pallas_call | solution.py:1045
  567.5 0.7 slice.159
  568.2 1.3 slice.191
  569.5 1.3 slice.195
  570.8 3.0 copy.96
  573.8 0.7 slice.160
  574.5 8.6 %combine.3 = bf16[8,256,1024]{2,1,0:T(8,128)(2,1)} custom-call(s32[8]{0:T(128)} %copy-done.8, s32[8]{0:T(128)} %subtract_clamp_fusion.count_ref, bf16[8,256,1024]{2,1,0:T(8,128)(2,1)} %bitcast.54, bf16[8,256,1024]{2,1,0:T(8,128)(2,1)} %get-tuple-element.66.part_ref), custom_call_target="tpu_custom_call" | custom-call | tf_op jit(solution)/shard_map/combine/pallas_call | solution.py:562
  583.1 1.2 slice_bitcast_fusion.1
  584.3 1.4 fusion.21
  585.7 8.8 %combine.2 = bf16[8,256,1024]{2,1,0:T(8,128)(2,1)} custom-call(s32[8]{0:T(128)} %copy-done.8, s32[8]{0:T(128)} %subtract_clamp_fusion.count_ref, bf16[8,256,1024]{2,1,0:T(8,128)(2,1)} %bitcast.56, bf16[8,256,1024]{2,1,0:T(8,128)(2,1)} %all-to-all-done.1.part_ref), custom_call_target="tpu_custom_call" | custom-call | tf_op jit(solution)/shard_map/combine/pallas_call | solution.py:562
  594.4 1.0 copy.115
  (121 shorter events, 4.8 us)
Async XLA Ops:
  8.2 6.5 %copy-start.8 = (s32[8]{0:T(128)}, s32[8]{0:T(128)S(1)}, u32[]{:S(2)}) copy-start(s32[8]{0:T(128)S(1)} %compare_select_fusion.1.place_ref) | copy-start | bytes 100
  14.7 5.5 slice-start
  14.7 5.6 slice-start.1
  19.8 1.1 copy-start.9
  19.8 1.2 copy-start.10
  19.8 1.2 copy-start.11
  19.8 1.2 copy-start.12
  136.0 69.1 %all-to-all-start = ((bf16[8,256,1024]{2,1,0:T(8,128)(2,1)}), bf16[8,256,1024]{2,1,0:T(8,128)(2,1)}, u32[]{:S(2)}, u32[]{:S(2)}) async-start(bf16[8,256,1024]{2,1,0:T(8,128)(2,1)} %get-tuple-element.42), calls=%async_computation | async-start | bytes 8388608 | tf_op jit(solution)/shard_map/all_to_all | solution.py:1148
  140.5 64.6 %copy-start.7 = (bf16[8,16,128]{2,1,0:T(8,128)(2,1)S(1)}, bf16[8,16,128]{2,1,0:T(8,128)(2,1)}, u32[]{:S(2)}) copy-start(bf16[8,16,128]{2,1,0:T(8,128)(2,1)} %get-tuple-element.44) | copy-start | bytes 98308
  140.6 65.2 %copy-start.13 = (f32[32]{0:T(128)S(1)}, f32[32]{0:T(128)}, u32[]{:S(2)}) copy-start(f32[32]{0:T(128)} %param.23) | copy-start | bytes 388
  140.6 65.4 %copy-start.15 = (f32[32]{0:T(128)S(1)}, f32[32]{0:T(128)}, u32[]{:S(2)}) copy-start(f32[32]{0:T(128)} %param.24) | copy-start | bytes 388
  140.6 65.6 %copy-start.14 = (f32[32]{0:T(128)S(1)}, f32[32]{0:T(128)}, u32[]{:S(2)}) copy-start(f32[32]{0:T(128)} %param.25) | copy-start | bytes 388
  140.6 121.8 %all-gather.5.cloned.1.call-start = ((), (), s32[]{:S(2)}) async-start(), calls=%async_computation.3 | async-start | bytes 2621440 | tf_op jit(solution)/shard_map/all_gather | solution.py:1151
  141.3 121.0 %all-gather.3.cloned.1.call-start = ((), (), s32[]{:S(2)}) async-start(), calls=%async_computation.2 | async-start | bytes 12582912 | tf_op jit(solution)/shard_map/all_gather | solution.py:1149
  208.9 53.5 %copy-start.4 = (s32[2]{0:T(128)}, s32[2]{0:T(128)S(1)}, u32[]{:S(2)}) copy-start(s32[2]{0:T(128)S(1)} %get-tuple-element.119.len_ref) | copy-start | bytes 28
  214.4 48.0 %copy-start.3 = (s32[2]{0:T(128)S(1)}, s32[2]{0:T(128)}, u32[]{:S(2)}) copy-start(s32[2]{0:T(128)} %get-tuple-element.118.nb_ref) | copy-start | bytes 28
  262.4 1.6 copy-start.5
  264.0 17.4 %copy-start.1 = (f32[128,256]{1,0:T(8,128)S(1)}, f32[128,256]{1,0:T(8,128)}, u32[]{:S(2)}) copy-start(f32[128,256]{1,0:T(8,128)} %get-tuple-element.49.ss_ref) | copy-start | bytes 393220
  289.8 2.0 copy-start
  291.8 0.7 copy-start.2
  292.5 293.2 %all-to-all-start.1 = ((bf16[8,256,1024]{2,1,0:T(8,128)(2,1)}), bf16[8,256,1024]{2,1,0:T(8,128)(2,1)}, u32[]{:S(2)}, u32[]{:S(2)}) async-start(bf16[8,256,1024]{2,1,0:T(8,128)(2,1)} %bitcast.52), calls=%async_computation.1 | async-start | bytes 8388608 | tf_op jit(solution)/shard_map/all_to_all | solution.py:1182
  585.6 8.8 %copy-start.6 = (f32[256,1024]{1,0:T(8,128)S(1)}, f32[256,1024]{1,0:T(8,128)}, u32[]{:S(2)}) copy-start(f32[256,1024]{1,0:T(8,128)} %get-tuple-element.165) | copy-start | bytes 3145732
Sparse Core Ops, SparseCore 0:
  143.3 63.3 all-gather.4
  208.2 19.2 all-gather.2

commit v2 on v1

v2 whole, which is shorter than its diff:
```python
import functools
import jax
import jax.numpy as jnp
from jax import lax
from jax.experimental import pallas as pl
from jax.experimental.pallas import tpu as pltpu
from jax.sharding import PartitionSpec as P

STATE = 128
HEADDIM = 64
HEADS = 32
INNER = 2048
CONV = 4
BLOCK = 256
CHUNK = 128
LANES = 128
MESH = pl.DeviceIdType.MESH
EPS = 1e-05
F32 = jnp.float32
BF16 = jnp.bfloat16
FAR = -1e9
TILE = 32
NT = (((1,), (1,)), ((), ()))
TN = (((0,), (0,)), ((), ()))


def mm(a, b, dims=(((1,), (0,)), ((), ()))):
    return lax.dot_general(a, b, dims, preferred_element_type=F32)


def two_parts(v):
    high = v.astype(BF16)
    return high, (v - high.astype(F32)).astype(BF16)


def spread(v, expand):
    high, low = two_parts(v)
    return mm(jnp.concatenate([high, low], axis=1), expand)


def gather_heads(v, collect):
    high, low = two_parts(v)
    return mm(high, collect) + mm(low, collect)


def sigmoid(v):
    return 0.5 + 0.5 * jnp.tanh(0.5 * v)


def mm_state(rows, state):
    return mm(jnp.concatenate([rows, rows], axis=1), jnp.concatenate(two_parts(state), axis=0))


def softplus(v):
    return jnp.maximum(v, 0.0) + jnp.log1p(jnp.exp(-jnp.abs(v)))


def three_parts(v):
    high = v.astype(BF16)
    rest = v - high.astype(F32)
    middle = rest.astype(BF16)
    return jnp.concatenate([high, middle, (rest - middle.astype(F32)).astype(BF16)], axis=0)


def triangle(backward):
    rows = lax.broadcasted_iota(jnp.int32, (BLOCK, BLOCK), 0)
    cols = lax.broadcasted_iota(jnp.int32, (BLOCK, BLOCK), 1)
    keep = (cols >= rows) if backward else (rows >= cols)
    tri = (keep & (rows // CHUNK == cols // CHUNK)).astype(F32).astype(BF16)
    return jnp.concatenate([tri, tri, tri], axis=1)


def chunk_rows(c):
    return slice(c * CHUNK, (c + 1) * CHUNK)


def each_last(cum):
    return jnp.concatenate(
        [
            jnp.broadcast_to(cum[(c + 1) * CHUNK - 1 : (c + 1) * CHUNK], (CHUNK, cum.shape[1]))
            for c in range(BLOCK // CHUNK)
        ],
        axis=0,
    )


def causal_sum(log_decay):
    return mm(triangle(False), three_parts(log_decay))


def reverse_sum(v):
    return mm(triangle(True), three_parts(v))


def convolve(cbuf, cw_ref, cb_ref, cols):
    total = cb_ref[0:1, cols] + cw_ref[3:4, cols] * cbuf[8 : 8 + BLOCK, cols]
    for k in range(CONV - 1):
        total = total + cw_ref[k : k + 1, cols] * cbuf[5 + k : 5 + k + BLOCK, cols]
    return total


def where_at(i, nb):
    i = jnp.minimum(i, nb[0] + nb[1] - 1)
    seq = (i >= nb[0]).astype(jnp.int32)
    return seq, i - seq * nb[0]


def most_blocks(count, length):
    blocks, best = length // BLOCK, 0
    for r in range(count // 2):
        for a in range(1, blocks + 1):
            for b in range(1, a + 1):
                upper, lower = (a - 1) * BLOCK + 1, (b - 1) * BLOCK + 1
                if length + r * upper + (count - 1 - 2 * r) * lower + r <= count // 2 * length and (r or a == blocks):
                    best = max(best, a + b)
    return best


def normalize(tok_ref, gain_ref):
    hidden = tok_ref[0].astype(F32)
    scale = lax.rsqrt(jnp.mean(hidden * hidden, axis=1, keepdims=True) + EPS)
    return (hidden * scale * gain_ref[0:1, :]).astype(BF16)


def fwd_kernel(
    inner, heads,
    nb_ref, tok_ref, gain_ref, win_ref, cw_ref, cb_ref, hp_ref, dwide_ref, og_ref,
    gate_ref, cin_ref, raw_ref, y_ref, s_ref, ss_ref, sc_ref,
    cbuf, xbuf, state, expand_ref,
):
    step_id = pl.program_id(0)
    _, blk = where_at(step_id, nb_ref)
    chan = inner + 2 * STATE

    @pl.when(step_id == 0)
    def _():
        fill_expand(expand_ref)

    @pl.when(step_id < nb_ref[0] + nb_ref[1])
    def _():
        @pl.when(blk == 0)
        def _():
            cbuf[0:8, :] = jnp.zeros((8, chan), F32)
            state[...] = jnp.zeros_like(state)

        @pl.when(blk > 0)
        def _():
            cbuf[0:8, :] = cbuf[BLOCK : BLOCK + 8, :]

        normed = normalize(tok_ref, gain_ref)
        for j in range(0, inner, 256):
            gate_ref[0, :, j : j + 256] = mm(normed, win_ref[:, j : j + 256])
        for j in range(0, chan, 256):
            part = mm(normed, win_ref[:, inner + j : inner + j + 256])
            cin_ref[0, :, j : j + 256] = part
            cbuf[8 : 8 + BLOCK, j : j + 256] = part
        raw = mm(normed, win_ref[:, inner + chan :])
        raw_ref[0] = raw
        for j in range(0, chan, 256):
            u = convolve(cbuf, cw_ref, cb_ref, slice(j, j + 256))
            xbuf[:, j : j + 256] = u * sigmoid(u)
        step = softplus(raw + hp_ref[0:1, :])
        log_decay = -step * hp_ref[1:2, :]
        rows = lax.broadcasted_iota(jnp.int32, (CHUNK, CHUNK), 0)
        cols = lax.broadcasted_iota(jnp.int32, (CHUNK, CHUNK), 1)
        causal = rows >= cols
        left = cols < HEADDIM
        cum = causal_sum(log_decay)
        cum_t = cum.T
        three = jnp.concatenate([jnp.exp(cum), step, jnp.exp(each_last(cum) - cum) * step], axis=0)
        wide = spread(three, expand_ref[...])
        e_wide, dt_wide, w_wide = wide[:BLOCK], wide[BLOCK : 2 * BLOCK], wide[2 * BLOCK :]
        all_in = xbuf[:, inner : inner + STATE].astype(BF16)
        all_out = xbuf[:, inner + STATE :].astype(BF16)
        x = xbuf[:, :inner]
        xd = (x * dt_wide).astype(BF16)
        xw = (x * w_wide).astype(BF16)
        crosses = []
        for c in range(BLOCK // CHUNK):
            at = chunk_rows(c)
            crosses.append(mm(all_out[at], all_in[at], NT))
        for p in range(heads // 2):
            lanes = slice(p * 128, (p + 1) * 128)
            for c in range(BLOCK // CHUNK):
                at = chunk_rows(c)
                pair = xd[at, lanes]
                zero = jnp.zeros_like(pair)
                both = jnp.concatenate([jnp.where(left, pair, zero), jnp.where(left, zero, pair)], axis=0)
                parts = []
                for h in (2 * p, 2 * p + 1):
                    gap = cum[at, h : h + 1] - cum_t[h : h + 1, at]
                    parts.append((crosses[c] * jnp.exp(jnp.where(causal, gap, FAR))).astype(BF16))
                y_ref[0, at, lanes] = mm(jnp.concatenate(parts, axis=1), both)
        for c in range(BLOCK // CHUNK):
            at = chunk_rows(c)
            held = state[...]
            s_ref[0, c] = held
            y_ref[0, at, :] += e_wide[at] * mm_state(all_out[at], held)
            last = e_wide[(c + 1) * CHUNK - 1 : (c + 1) * CHUNK]
            state[...] = last * held + mm(all_in[at], xw[at], TN)
        total = jnp.zeros((BLOCK, 1), F32)
        for j in range(0, inner, 256):
            at = slice(j, j + 256)
            gate = gate_ref[0, :, at]
            summed = y_ref[0, :, at] + dwide_ref[0:1, at] * xbuf[:, at]
            y_ref[0, :, at] = summed
            gated = summed * (gate * sigmoid(gate))
            total = total + jnp.sum(gated * gated, axis=1, keepdims=True)
            sc_ref[0, :, at] = (gated * og_ref[0:1, at]).astype(BF16)
        ss_ref[...] = jnp.broadcast_to(total, (BLOCK, 8)).T


def fixed(shape):
    return pl.BlockSpec(shape, lambda *_: (0,) * len(shape), pipeline_mode=pl.Buffered(1))


def fwd_call(steps, nb, tok, gain, win, cw, cb, hp, dwide, og):
    nseq, length, width = tok.shape
    inner = dwide.shape[1]
    heads = inner // HEADDIM
    chan = inner + 2 * STATE
    blocks = length // BLOCK

    def rows(i, nb):
        seq, blk = where_at(i, nb)
        return (seq, blk, 0)

    def srows(i, nb):
        seq, blk = where_at(i, nb)
        return (seq, blk, 0, 0)

    def ssrows(i, nb):
        seq, blk = where_at(i, nb)
        return (seq * blocks + blk, 0)

    grid_spec = pltpu.PrefetchScalarGridSpec(
        num_scalar_prefetch=1,
        grid=(steps,),
        in_specs=[
            pl.BlockSpec((1, BLOCK, width), rows),
            fixed(gain.shape), fixed(win.shape), fixed(cw.shape), fixed(cb.shape),
            fixed(hp.shape), fixed(dwide.shape), fixed(og.shape),
        ],
        out_specs=[
            pl.BlockSpec((1, BLOCK, inner), rows),
            pl.BlockSpec((1, BLOCK, chan), rows),
            pl.BlockSpec((1, BLOCK, LANES), rows),
            pl.BlockSpec((1, BLOCK, inner), rows),
            pl.BlockSpec((1, BLOCK // CHUNK, STATE, inner), srows),
            pl.BlockSpec((8, BLOCK), ssrows),
            pl.BlockSpec((1, BLOCK, inner), rows),
        ],
        scratch_shapes=[
            pltpu.VMEM((BLOCK + 8, chan), F32),
            pltpu.VMEM((BLOCK, chan), F32),
            pltpu.VMEM((STATE, inner), F32),
            pltpu.VMEM((2 * LANES, inner), BF16),
        ],
    )
    shapes = [
        jax.ShapeDtypeStruct((nseq, length, inner), F32),
        jax.ShapeDtypeStruct((nseq, length, chan), F32),
        jax.ShapeDtypeStruct((nseq, length, LANES), F32),
        jax.ShapeDtypeStruct((nseq, length, inner), F32),
        jax.ShapeDtypeStruct((nseq, length // CHUNK, STATE, inner), F32),
        jax.ShapeDtypeStruct((nseq * blocks * 8, BLOCK), F32),
        jax.ShapeDtypeStruct((nseq, length, inner), BF16),
    ]
    return pl.pallas_call(
        functools.partial(fwd_kernel, inner, heads),
        grid_spec=grid_spec,
        out_shape=shapes,
        compiler_params=pltpu.CompilerParams(
            dimension_semantics=("arbitrary",), vmem_limit_bytes=60 * 1024 * 1024
        ),
        cost_estimate=pl.CostEstimate(
            flops=nseq * length * width * (3 * inner + 400), bytes_accessed=60 << 20, transcendentals=0
        ),
        name="layer_forward",
    )(nb, tok, gain, win, cw, cb, hp, dwide, og)


def mid_kernel(nb_ref, len_ref, cot_ref, sc_ref, wout_ref, gm_ref, v_ref, bp_ref):
    seq, blk = where_at(pl.program_id(0), nb_ref)

    @pl.when(pl.program_id(0) < nb_ref[0] + nb_ref[1])
    def _():
        cot = cot_ref[0]
        position = blk * BLOCK + lax.broadcasted_iota(jnp.int32, cot.shape, 0)
        gb = jnp.where(position < len_ref[seq], cot, jnp.zeros_like(cot))
        total = jnp.zeros((BLOCK, 1), F32)
        for j in range(0, sc_ref.shape[2], 256):
            at = slice(j, j + 256)
            gm = mm(gb, wout_ref[at, :], NT)
            gm_ref[0, :, at] = gm
            total = total + jnp.sum(gm * sc_ref[0, :, at].astype(F32), axis=1, keepdims=True)
        v_ref[...] = jnp.broadcast_to(total, (BLOCK, 8)).T
        scaled = sc_ref[0]
        for j in range(0, cot.shape[1], 256):
            bp_ref[0, :, j : j + 256] = mm(scaled, wout_ref[:, j : j + 256]).astype(BF16)


def mid_call(steps, nb, lens, cot, scaled, wout):
    nseq, length, width = cot.shape
    inner = wout.shape[0]
    blocks = length // BLOCK

    def rows(i, nb, lens):
        seq, blk = where_at(i, nb)
        return (seq, blk, 0)

    def vrows(i, nb, lens):
        seq, blk = where_at(i, nb)
        return (seq * blocks + blk, 0)

    return pl.pallas_call(
        mid_kernel,
        grid_spec=pltpu.PrefetchScalarGridSpec(
            num_scalar_prefetch=2,
            grid=(steps,),
            in_specs=[pl.BlockSpec((1, BLOCK, width), rows), pl.BlockSpec((1, BLOCK, inner), rows), fixed(wout.shape)],
            out_specs=[
                pl.BlockSpec((1, BLOCK, inner), rows), pl.BlockSpec((8, BLOCK), vrows),
                pl.BlockSpec((1, BLOCK, width), rows),
            ],
        ),
        out_shape=[
            jax.ShapeDtypeStruct((nseq, length, inner), F32),
            jax.ShapeDtypeStruct((nseq * blocks * 8, BLOCK), F32),
            jax.ShapeDtypeStruct((nseq, length, width), BF16),
        ],
        compiler_params=pltpu.CompilerParams(
            dimension_semantics=("arbitrary",), vmem_limit_bytes=60 * 1024 * 1024
        ),
        cost_estimate=pl.CostEstimate(flops=10**10, bytes_accessed=30 << 20, transcendentals=0),
        name="layer_middle",
    )(nb, lens, cot, scaled, wout)


def gate_kernel(
    parts,
    nb_ref, len_ref, chip_ref, tok_ref, cot_ref, gain_ref, wgate_ref, gm_ref, og_ref, gate_ref, y_ref, rv_ref,
    dy_ref, gp_ref, dog_ref, *refs,
):
    wgate_out, wout_out = refs[:parts], refs[parts : 2 * parts]
    normed_t, dgate_buf, mixed_buf, dwgate, dwout = refs[2 * parts :]
    step_id = pl.program_id(0)
    seq, blk = where_at(step_id, nb_ref)
    inner = gm_ref.shape[2]
    width = tok_ref.shape[2]

    @pl.when(step_id == 0)
    def _():
        dwgate[...] = jnp.zeros_like(dwgate)
        dwout[...] = jnp.zeros_like(dwout)
        dog_ref[...] = jnp.zeros_like(dog_ref)

    @pl.when(step_id < nb_ref[0] + nb_ref[1])
    def _():
        position = blk * BLOCK + lax.broadcasted_iota(jnp.int32, (BLOCK, width), 0)
        cot = cot_ref[0]
        gb = jnp.where(position < len_ref[seq], cot, jnp.zeros_like(cot))
        rv = rv_ref[...].T
        scale, coef = rv[:, 0:1], rv[:, 1:2]
        normed_t[...] = normalize(tok_ref, gain_ref).T
        for j in range(0, inner, 256):
            at = slice(j, j + 256)
            gain = og_ref[0:1, at]
            total = jnp.zeros((8, 256), F32)
            for r in range(0, BLOCK, TILE):
                row = slice(r, r + TILE)
                gm = gm_ref[0, row, at]
                gate = gate_ref[0, row, at]
                sig = sigmoid(gate)
                ysum = y_ref[0, row, at]
                silu = gate * sig
                gated = ysum * silu
                normal = gated * scale[row]
                mixed_buf[row, at] = (normal * gain).astype(BF16)
                product = gm * normal
                for k in range(0, TILE, 8):
                    total = total + product[k : k + 8]
                dgated = scale[row] * (gm * gain) - gated * coef[row]
                dgate_buf[row, at] = (dgated * ysum * (sig + silu * (1.0 - sig))).astype(BF16)
                dy_ref[0, row, at] = dgated * silu
            dog_ref[0:1, at] += jnp.sum(total, axis=0, keepdims=True)
            dwout[at, :] += mm(mixed_buf[:, at], gb, TN)
            dwgate[:, at] += mm(normed_t[...], dgate_buf[:, at])
        for j in range(0, width, 256):
            gp_ref[0, :, j : j + 256] = mm(dgate_buf[...], wgate_ref[j : j + 256, :], NT).astype(BF16)

    @pl.when(step_id == pl.num_programs(0) - 1)
    def _():
        for i in range(parts):
            chip = lax.rem(chip_ref[0] + i, parts)
            for out, total in ((wgate_out[i], dwgate), (wout_out[i], dwout)):
                size = out.shape[0]
                out[...] = total[pl.ds(pl.multiple_of(chip * size, size), size), :].astype(BF16)


def gate_call(steps, nb, lens, chip, parts, tok, cot, gain, win, gm, og, gate, y, rv):
    nseq, length, width = tok.shape
    inner = gm.shape[2]
    blocks = length // BLOCK

    def rows(i, nb, lens, chip):
        seq, blk = where_at(i, nb)
        return (seq, blk, 0)

    def rvrows(i, nb, lens, chip):
        seq, blk = where_at(i, nb)
        return (seq * blocks + blk, 0)

    tall, deep = pl.BlockSpec((1, BLOCK, width), rows), pl.BlockSpec((1, BLOCK, inner), rows)
    return pl.pallas_call(
        functools.partial(gate_kernel, parts),
        grid_spec=pltpu.PrefetchScalarGridSpec(
            num_scalar_prefetch=3,
            grid=(steps,),
            in_specs=[
                tall, tall, fixed(gain.shape), fixed((width, inner)), deep, fixed(og.shape), deep, deep,
                pl.BlockSpec((8, BLOCK), rvrows),
            ],
            out_specs=[deep, tall, fixed((8, inner))]
            + [fixed((width // parts, inner))] * parts
            + [fixed((inner // parts, width))] * parts,
            scratch_shapes=[
                pltpu.VMEM((width, BLOCK), BF16), pltpu.VMEM((BLOCK, inner), BF16), pltpu.VMEM((BLOCK, inner), BF16),
                pltpu.VMEM((width, inner), F32), pltpu.VMEM((inner, width), F32),
            ],
        ),
        out_shape=[
            jax.ShapeDtypeStruct((nseq, length, inner), F32),
            jax.ShapeDtypeStruct((nseq, length, width), BF16),
            jax.ShapeDtypeStruct((8, inner), F32),
        ]
        + [jax.ShapeDtypeStruct((width // parts, inner), BF16)] * parts
        + [jax.ShapeDtypeStruct((inner // parts, width), BF16)] * parts,
        compiler_params=pltpu.CompilerParams(
            dimension_semantics=("arbitrary",), vmem_limit_bytes=60 * 1024 * 1024
        ),
        cost_estimate=pl.CostEstimate(flops=2 * 10**10, bytes_accessed=60 << 20, transcendentals=0),
        name="layer_gate",
    )(nb, lens, chip, tok, cot, gain, win, gm, og, gate, y, rv)


def bwd_kernel(
    inner, heads,
    nb_ref,
    tok_ref, gain_ref, win_ref, cw_ref, cb_ref, hp_ref, dwide_ref, dog_ref, dy_ref, gp_ref, cin_ref, halo_ref, raw_ref, y_ref, s_ref,
    gn_ref, win_out, dcw_ref,
    cbuf, ubuf, dbuf, xbuf, dybuf, dproj, dstate, later, dwin_ref, normed_t, dhp_ref, ddw_ref, expand_ref, collect_ref,
):
    grid_id = pl.program_id(0)
    seq, step_id = where_at(grid_id, nb_ref)
    chan = inner + 2 * STATE
    width = tok_ref.shape[2]
    nb = nb_ref[seq]
    blk = nb - 1 - step_id

    @pl.when(grid_id == 0)
    def _():
        fill_expand(expand_ref)
        fill_collect(collect_ref)
        dwin_ref[...] = jnp.zeros_like(dwin_ref)
        dcw_ref[...] = jnp.zeros_like(dcw_ref)
        dhp_ref[...] = jnp.zeros_like(dhp_ref)
        ddw_ref[...] = jnp.zeros_like(ddw_ref)

    @pl.when(grid_id < nb_ref[0] + nb_ref[1])
    def _():
        @pl.when(step_id == 0)
        def _():
            dbuf[BLOCK : BLOCK + 8, :] = jnp.zeros((8, chan), F32)
            dstate[...] = jnp.zeros_like(dstate)
            later[...] = jnp.zeros_like(later)

        @pl.when(step_id > 0)
        def _():
            dbuf[BLOCK : BLOCK + 8, :] = dbuf[0:8, :]

        @pl.when(blk == 0)
        def _():
            cbuf[0:8, :] = jnp.zeros((8, chan), F32)

        @pl.when(blk > 0)
        def _():
            cbuf[0:8, :] = halo_ref[0]

        cbuf[8 : 8 + BLOCK, :] = cin_ref[0]
        normed_t[...] = normalize(tok_ref, gain_ref).T
        for j in range(0, chan, 256):
            at = slice(j, j + 256)
            u = convolve(cbuf, cw_ref, cb_ref, at)
            sig = sigmoid(u)
            xbuf[:, at] = u * sig
            ubuf[:, at] = sig * (1.0 + u * (1.0 - sig))
        raw = raw_ref[0] + hp_ref[0:1, :]
        step = softplus(raw)
        log_decay = -step * hp_ref[1:2, :]
        rows = lax.broadcasted_iota(jnp.int32, (CHUNK, CHUNK), 0)
        cols = lax.broadcasted_iota(jnp.int32, (CHUNK, CHUNK), 1)
        causal = cols >= rows
        left = cols < HEADDIM
        cum = causal_sum(log_decay)
        cum_t = cum.T
        four = jnp.concatenate([jnp.exp(cum), step, jnp.exp(each_last(cum) - cum)], axis=0)
        wide = spread(four, expand_ref[...])
        e_wide, dt_wide, t_wide = wide[:BLOCK], wide[BLOCK : 2 * BLOCK], wide[2 * BLOCK :]
        all_in = xbuf[:, inner : inner + STATE].astype(BF16)
        all_out = xbuf[:, inner + STATE :].astype(BF16)
        x = xbuf[:, :inner]
        dy = dy_ref[0]
        dy16 = dy.astype(BF16)
        ddw_ref[0:1, :] += jnp.sum(dy * x, axis=0, keepdims=True)
        xd32 = x * dt_wide
        xd = xd32.astype(BF16)
        xw = (xd32 * t_wide).astype(BF16)
        edy = (e_wide * dy).astype(BF16)
        count = BLOCK // CHUNK
        crosses, reaches, outers = [], [], []
        for c in range(count):
            at = chunk_rows(c)
            crosses.append(mm(all_in[at], all_out[at], NT))
            reaches.append(mm_state(all_out[at], s_ref[0, c]))
            outers.append(mm(all_out[at], edy[at], TN))
        dcrosses = [jnp.zeros((CHUNK, CHUNK), F32)] * count
        insides = [[] for _ in range(count)]
        for p in range(heads // 2):
            lanes = slice(p * 128, (p + 1) * 128)
            for c in range(count):
                at = chunk_rows(c)
                pair = xd[at, lanes]
                dpair = dy16[at, lanes]
                zero = jnp.zeros_like(pair)
                both = jnp.concatenate([jnp.where(left, dpair, zero), jnp.where(left, zero, dpair)], axis=0)
                dweights = mm(pair, both, NT)
                parts = []
                for i, h in enumerate((2 * p, 2 * p + 1)):
                    gap = cum_t[h : h + 1, at] - cum[at, h : h + 1]
                    decay = jnp.exp(jnp.where(causal, gap, FAR))
                    parts.append((crosses[c] * decay).astype(BF16))
                    dcrosses[c] = dcrosses[c] + dweights[:, i * CHUNK : (i + 1) * CHUNK] * decay
                insides[c].append(mm(jnp.concatenate(parts, axis=1), both))
        backs, folds = [None] * count, [None] * count
        for c in reversed(range(count)):
            at = chunk_rows(c)
            dheld = dstate[...]
            backs[c] = mm_state(all_in[at], dheld)
            folds[c] = jnp.sum(dheld * later[...], axis=0, keepdims=True)
            later[...] = s_ref[0, c]
            dstate[...] = e_wide[(c + 1) * CHUNK - 1 : (c + 1) * CHUNK] * dheld + outers[c]
            dcross16 = dcrosses[c].astype(BF16)
            ds_in = mm(dcross16, all_out[at]) + mm(xw[at], dheld.astype(BF16), NT)
            ds_out = mm(dcross16, all_in[at], TN) + mm(edy[at], s_ref[0, c].astype(BF16), NT)
            dbuf[at, inner : inner + STATE] = ds_in
            dbuf[at, inner + STATE :] = ds_out
        back = jnp.concatenate(backs, axis=0)
        reach = jnp.concatenate(reaches, axis=0)
        inside = jnp.concatenate([jnp.concatenate(part, axis=1) for part in insides], axis=0)
        dxd = inside + t_wide * back
        dybuf[...] = dt_wide * dxd + dwide_ref[0:1, :] * dy
        scanned = (y_ref[0] - dwide_ref[0:1, :] * x - e_wide * reach) * dy16.astype(F32) + edy.astype(F32) * reach
        scanned = scanned - xd.astype(F32) * inside - xw.astype(F32) * back
        high, low = two_parts(scanned)
        direct_high, direct_low = two_parts(x * dxd)
        rest = [part for fold in folds for part in two_parts(jnp.broadcast_to(fold, (16, inner)))]
        stacked = jnp.concatenate([direct_high, direct_low, high, low] + rest, axis=0)
        small = mm(stacked, collect_ref[...])
        ddirect = small[:BLOCK] + small[BLOCK : 2 * BLOCK]
        dcum = small[2 * BLOCK : 3 * BLOCK] + small[3 * BLOCK : 4 * BLOCK]
        dfold = jnp.concatenate(
            [
                jnp.broadcast_to(
                    small[4 * BLOCK + 32 * c : 4 * BLOCK + 32 * c + 1]
                    + small[4 * BLOCK + 32 * c + 16 : 4 * BLOCK + 32 * c + 17],
                    (CHUNK, LANES),
                )
                for c in range(count)
            ],
            axis=0,
        )
        dlog = reverse_sum(dcum) + dfold
        draw = (ddirect - dlog * hp_ref[1:2, :]) * sigmoid(raw)
        dhp_ref[0:1, :] += jnp.sum(draw, axis=0, keepdims=True)
        dhp_ref[1:2, :] += jnp.sum(dlog * log_decay, axis=0, keepdims=True)
        dproj[:, chan:] = draw.astype(BF16)
        for j in range(0, chan, 256):
            at = slice(j, j + 256)
            grad = dybuf[:, at] if j < inner else dbuf[0:BLOCK, at]
            du = grad * ubuf[:, at]
            dbuf[0:BLOCK, at] = du
            dcw_ref[CONV : CONV + 1, at] += jnp.sum(du, axis=0, keepdims=True)
            for k in range(CONV):
                dcw_ref[k : k + 1, at] += jnp.sum(du * cbuf[5 + k : 5 + k + BLOCK, at], axis=0, keepdims=True)
            dcin = cw_ref[CONV - 1 : CONV, at] * du
            for k in range(CONV - 1):
                dcin = dcin + cw_ref[k : k + 1, at] * dbuf[3 - k : 3 - k + BLOCK, at]
            dcin = dcin.astype(BF16)
            dproj[:, at] = dcin
            dwin_ref[:, at] += mm(normed_t[...], dcin)
        dwin_ref[:, chan:] += mm(normed_t[...], dproj[:, chan:])
        for j in range(0, width, 256):
            at = slice(j, j + 256)
            gn_ref[0, :, at] = (gp_ref[0, :, at].astype(F32) + mm(dproj[...], win_ref[at, inner:], NT)).astype(BF16)

    @pl.when(grid_id == pl.num_programs(0) - 1)
    def _():
        win_out[...] = dwin_ref[...].astype(BF16)
        dcw_ref[CONV + 1 : CONV + 2, :inner] = dog_ref[0:1, :]
        dcw_ref[CONV + 2 : CONV + 3, :LANES] = gather_heads(ddw_ref[...], collect_ref[...])[0:1]
        dcw_ref[CONV + 2 : CONV + 3, LANES : 2 * LANES] = dhp_ref[0:1, :]
        dcw_ref[CONV + 2 : CONV + 3, 2 * LANES : 3 * LANES] = dhp_ref[1:2, :]


def bwd_call(steps, nb, tok, gain, win, cw, cb, hp, dwide, dog, dy, gp, cin, raw, y, s):
    nseq, length, width = tok.shape
    inner = dy.shape[2]
    rest = win.shape[1] - inner
    heads = inner // HEADDIM
    chan = inner + 2 * STATE

    def place(i, nb):
        seq, back = where_at(i, nb)
        return seq, nb[seq] - 1 - back

    def rows(i, nb):
        seq, blk = place(i, nb)
        return (seq, blk, 0)

    def srows(i, nb):
        seq, blk = place(i, nb)
        return (seq, blk, 0, 0)

    def halo(i, nb):
        seq, blk = place(i, nb)
        return (seq, jnp.maximum(blk * (BLOCK // 8) - 1, 0), 0)

    def whole(shape):
        return pl.BlockSpec(shape, lambda *_: (0,) * len(shape), pipeline_mode=pl.Buffered(1))

    grid_spec = pltpu.PrefetchScalarGridSpec(
        num_scalar_prefetch=1,
        grid=(steps,),
        in_specs=[
            pl.BlockSpec((1, BLOCK, width), rows),
            fixed(gain.shape), fixed(win.shape), fixed(cw.shape), fixed(cb.shape),
            fixed(hp.shape), fixed(dwide.shape), fixed(dog.shape),
            pl.BlockSpec((1, BLOCK, inner), rows),
            pl.BlockSpec((1, BLOCK, width), rows),
            pl.BlockSpec((1, BLOCK, chan), rows),
            pl.BlockSpec((1, 8, chan), halo),
            pl.BlockSpec((1, BLOCK, LANES), rows),
            pl.BlockSpec((1, BLOCK, inner), rows),
            pl.BlockSpec((1, BLOCK // CHUNK, STATE, inner), srows),
        ],
        out_specs=[
            pl.BlockSpec((1, BLOCK, width), rows),
            whole((width, rest)), whole((8, chan)),
        ],
        scratch_shapes=[
            pltpu.VMEM((BLOCK + 8, chan), F32),
            pltpu.VMEM((BLOCK, chan), F32),
            pltpu.VMEM((BLOCK + 8, chan), F32),
            pltpu.VMEM((BLOCK, chan), F32),
            pltpu.VMEM((BLOCK, inner), F32),
            pltpu.VMEM((BLOCK, rest), BF16),
            pltpu.VMEM((STATE, inner), F32),
            pltpu.VMEM((STATE, inner), F32),
            pltpu.VMEM((width, rest), F32),
            pltpu.VMEM((width, BLOCK), BF16),
            pltpu.VMEM((8, LANES), F32),
            pltpu.VMEM((8, inner), F32),
            pltpu.VMEM((2 * LANES, inner), BF16),
            pltpu.VMEM((inner, LANES), BF16),
        ],
    )
    shapes = [
        jax.ShapeDtypeStruct((nseq, length, width), BF16),
        jax.ShapeDtypeStruct((width, rest), BF16),
        jax.ShapeDtypeStruct((8, chan), F32),
    ]
    return pl.pallas_call(
        functools.partial(bwd_kernel, inner, heads),
        grid_spec=grid_spec,
        out_shape=shapes,
        compiler_params=pltpu.CompilerParams(
            dimension_semantics=("arbitrary",), vmem_limit_bytes=63 * 1024 * 1024
        ),
        cost_estimate=pl.CostEstimate(
            flops=10**11, bytes_accessed=100 << 20, transcendentals=0
        ),
        name="layer_backward",
    )(nb, tok, gain, win, cw, cb, hp, dwide, dog, dy, gp, cin, cin, raw, y, s)


def fill_expand(expand):
    owner = lax.broadcasted_iota(jnp.int32, expand.shape, 1) // HEADDIM
    head = lax.rem(lax.broadcasted_iota(jnp.int32, expand.shape, 0), LANES)
    expand[...] = (owner == head).astype(F32).astype(BF16)


def fill_collect(collect):
    owner = lax.broadcasted_iota(jnp.int32, collect.shape, 0) // HEADDIM
    head = lax.broadcasted_iota(jnp.int32, collect.shape, 1)
    collect[...] = (owner == head).astype(F32).astype(BF16)


def combine_kernel(place_ref, count_ref, base_ref, part_ref, out_ref):
    kept = count_ref[pl.program_id(0)]
    base = base_ref[0]
    row = lax.broadcasted_iota(jnp.int32, base.shape, 0)
    part = jnp.where(row < kept, part_ref[0].astype(F32), 0.0)
    out_ref[0] = (base.astype(F32) + part).astype(BF16)


def combine_call(place, kept, base, part):
    count, span, width = base.shape
    block = (1, span, width)
    return pl.pallas_call(
        combine_kernel,
        grid_spec=pltpu.PrefetchScalarGridSpec(
            num_scalar_prefetch=2,
            grid=(count,),
            in_specs=[
                pl.BlockSpec(block, lambda s, place, kept: (s, 0, 0)),
                pl.BlockSpec(block, lambda s, place, kept: (place[s], 0, 0)),
            ],
            out_specs=pl.BlockSpec(block, lambda s, place, kept: (s, 0, 0)),
        ),
        out_shape=jax.ShapeDtypeStruct(base.shape, BF16),
        name="combine",
    )(place, kept, base, part)


def peers_of(n):
    return [(away, turn) for away in range(n // 2) for turn in range(2) if away or turn]


def enter(n, me):
    barrier = pltpu.get_barrier_semaphore()
    for away, turn in peers_of(n):
        pl.semaphore_signal(barrier, inc=1, device_id={"fsdp": peer_at(n, me, away, turn)}, device_id_type=MESH)
    pl.semaphore_wait(barrier, n - 1)


def peer_at(n, me, away, turn):
    chip = lax.rem(lax.div(me, 2) + away, n // 2)
    return 2 * chip + lax.rem(lax.rem(me, 2) + turn, 2)


def sender_at(n, me, away, turn):
    chip = lax.rem(lax.div(me, 2) + n // 2 - away, n // 2)
    return 2 * chip + lax.rem(lax.rem(me, 2) + turn, 2)


def rows_at(index, size):
    return pl.ds(pl.multiple_of(index * size, size), size)


def start_kernel(
    n, source_ref, tokens, grads, shards, small, tok, win, smalls, sent_grad, rows_in, sent, w_held, s_held, here, w_send, w_recv, t_send, t_recv, f_send, f_recv, s_send, s_recv
):
    me = lax.axis_index("fsdp")
    core = lax.rem(me, 2)
    partner = 2 * lax.div(me, 2) + 1 - core
    span, rows = tokens.shape[1], shards.shape[1]
    loads = [
        pltpu.make_async_copy(tokens, rows_in, here.at[0]),
        pltpu.make_async_copy(shards.at[core], w_held, here.at[1]),
        pltpu.make_async_copy(small, s_held, here.at[2]),
    ]
    for copy in loads:
        copy.start()

    def place_rows(index):
        chosen = source_ref[index]
        step = 32

        @pl.loop(0, span // step)
        def _(i):
            at = pl.ds(pl.multiple_of(i * step, step), step)
            sent[index, at, :] = rows_in[chosen, at, :]

    enter(n, me)
    pending = []
    loads[0].wait()
    for index, (away, turn) in enumerate(peers_of(n)):
        peer = peer_at(n, me, away, turn)
        theirs = lax.rem(core + turn, 2)

        def push(src, dst, send, recv):
            copy = pltpu.make_async_remote_copy(
                src_ref=src, dst_ref=dst, send_sem=send, recv_sem=recv, device_id={"fsdp": peer}, device_id_type=MESH
            )
            copy.start()
            pending.append(copy)

        place_rows(peer)
        push(sent.at[peer], tok.at[theirs, rows_at(me, span)], t_send.at[index], t_recv.at[index])
        push(shards.at[theirs], win.at[rows_at(me, rows)], w_send.at[index], w_recv.at[index])
        push(small, smalls.at[me], s_send.at[index], s_recv.at[index])
    place_rows(me)
    for copy in loads[1:]:
        copy.wait()
    local = [
        pltpu.make_async_copy(sent.at[me], tok.at[core, rows_at(me, span)], here.at[0]),
        pltpu.make_async_copy(sent.at[partner], tok.at[1 - core, rows_at(me, span)], here.at[1]),
        pltpu.make_async_copy(w_held, win.at[rows_at(me, rows)], here.at[2]),
        pltpu.make_async_copy(s_held, smalls.at[me], here.at[3]),
    ]
    for copy in local:
        copy.start()
    more = pltpu.make_async_copy(grads, rows_in, here.at[4])
    more.start()

    def forward(index, src, owner):
        copy = pltpu.make_async_remote_copy(
            src_ref=src, dst_ref=tok.at[core, rows_at(owner, span)], send_sem=f_send.at[index],
            recv_sem=f_recv.at[index], device_id={"fsdp": partner}, device_id_type=MESH,
        )
        copy.start()
        return copy

    passed = [forward(0, sent.at[me], me)]
    for index, (away, turn) in enumerate(peers_of(n)):
        owner = sender_at(n, me, away, turn)
        block = tok.at[core, rows_at(owner, span)]
        pltpu.make_async_remote_copy(
            src_ref=block, dst_ref=block, send_sem=t_send.at[index], recv_sem=t_recv.at[index],
            device_id={"fsdp": partner}, device_id_type=MESH,
        ).wait_recv()
        if away:
            passed.append(forward(index, block, owner))
    for copy in passed:
        copy.wait()
    for copy in pending:
        copy.wait_send()
    for copy in local:
        copy.wait()
    more.wait()

    @pl.loop(0, n)
    def _(index):
        place_rows(index)

    back = pltpu.make_async_copy(sent, sent_grad, here.at[4])
    back.start()
    for index, (away, turn) in enumerate(peers_of(n)):
        owner = sender_at(n, me, away, turn)
        checks = [(win.at[rows_at(owner, rows)], w_send, w_recv), (smalls.at[owner], s_send, s_recv)]
        for block, send, recv in checks:
            pltpu.make_async_remote_copy(
                src_ref=block, dst_ref=block, send_sem=send.at[index], recv_sem=recv.at[index],
                device_id={"fsdp": partner}, device_id_type=MESH,
            ).wait_recv()
    back.wait()


def start_call(n, source, tokens, grads, shards, small):
    span, width = tokens.shape[1:]
    _, rows, wide = shards.shape
    count = n - 1
    anywhere = pl.BlockSpec(memory_space=pl.ANY)
    return pl.pallas_call(
        functools.partial(start_kernel, n),
        out_shape=[
            jax.ShapeDtypeStruct((2, n * span, width), BF16),
            jax.ShapeDtypeStruct((n * rows, wide), BF16),
            jax.ShapeDtypeStruct((n,) + small.shape, BF16),
            jax.ShapeDtypeStruct(tokens.shape, BF16),
        ],
        in_specs=[pl.BlockSpec(memory_space=pltpu.SMEM)] + [anywhere] * 4,
        out_specs=[anywhere] * 4,
        scratch_shapes=[
            pltpu.VMEM(tokens.shape, BF16), pltpu.VMEM(tokens.shape, BF16), pltpu.VMEM((rows, wide), BF16), pltpu.VMEM(small.shape, BF16),
        ]
        + [pltpu.SemaphoreType.DMA((5,))] + [pltpu.SemaphoreType.DMA((count,))] * 8,
        compiler_params=pltpu.CompilerParams(
            collective_id=0, has_side_effects=True, vmem_limit_bytes=60 * 1024 * 1024
        ),
        name="start",
    )(source, tokens, grads, shards, small)


def exchange_kernel(
    bp, ss_ref, v_ref, branch, rv_ref, mine, theirs, ss_in, v_in, here, put, b_send, b_recv, s_send, s_recv
):
    me = lax.axis_index("fsdp")
    core = lax.rem(me, 2)
    partner = 2 * lax.div(me, 2) + 1 - core
    length, width = mine.shape
    blocks = length // BLOCK
    barrier = pltpu.get_barrier_semaphore()
    pl.semaphore_signal(barrier, inc=1, device_id={"fsdp": partner}, device_id_type=MESH)
    pl.semaphore_wait(barrier, 1)

    def remote(src, dst, send, recv):
        return pltpu.make_async_remote_copy(
            src_ref=src, dst_ref=dst, send_sem=send, recv_sem=recv, device_id={"fsdp": partner}, device_id_type=MESH
        )

    load = pltpu.make_async_copy(bp.at[core], mine, here.at[0])
    load.start()
    copies = [
        remote(ss_ref, ss_in, s_send.at[0], s_recv.at[0]),
        remote(v_ref, v_in, s_send.at[1], s_recv.at[1]),
    ]
    for b in range(blocks):
        at = pl.ds(b * BLOCK, BLOCK)
        copies.append(remote(bp.at[1 - core, at], theirs.at[at], b_send.at[b], b_recv.at[b]))
    for copy in copies:
        copy.start()
    for copy in copies[:2]:
        copy.wait_recv()
    scale = lax.rsqrt((ss_ref[...] + ss_in[...]) * (1.0 / INNER) + EPS)
    coef = scale * scale * scale * (v_ref[...] + v_in[...]) * (1.0 / INNER)
    sub = lax.rem(lax.broadcasted_iota(jnp.int32, scale.shape, 0), 8)
    rv_ref[...] = jnp.where(sub == 0, scale, coef)
    load.wait()
    puts = []
    for b in range(blocks):
        at = pl.ds(b * BLOCK, BLOCK)
        copies[2 + b].wait_recv()
        rows = rv_ref[pl.ds(pl.multiple_of((core * blocks + b) * 8, 8), 8), :]
        column = jnp.concatenate([rows, jnp.zeros((LANES - 8, BLOCK), F32)], axis=0).T[:, 0:1]
        mine[at, :] = ((mine[at, :].astype(F32) + theirs[at, :].astype(F32)) * column).astype(BF16)
        copy = pltpu.make_async_copy(mine.at[at], branch.at[at], put.at[b])
        copy.start()
        puts.append(copy)
    for copy in copies:
        copy.wait_send()
    for copy in puts:
        copy.wait()


def exchange_call(bp, ss, v):
    _, length, width = bp.shape
    blocks = length // BLOCK
    vmem = pl.BlockSpec(memory_space=pltpu.VMEM)
    anywhere = pl.BlockSpec(memory_space=pl.ANY)
    dma = pltpu.SemaphoreType.DMA
    return pl.pallas_call(
        exchange_kernel,
        out_shape=[jax.ShapeDtypeStruct((length, width), BF16), jax.ShapeDtypeStruct(ss.shape, F32)],
        in_specs=[anywhere, vmem, vmem],
        out_specs=[anywhere, vmem],
        scratch_shapes=[
            pltpu.VMEM((length, width), BF16), pltpu.VMEM((length, width), BF16),
            pltpu.VMEM(ss.shape, F32), pltpu.VMEM(ss.shape, F32),
            dma((1,)), dma((blocks,)), dma((blocks,)), dma((blocks,)), dma((2,)), dma((2,)),
        ],
        compiler_params=pltpu.CompilerParams(
            collective_id=2, has_side_effects=True, vmem_limit_bytes=60 * 1024 * 1024
        ),
        name="exchange",
    )(bp, ss, v)


def pair_kernel(mine, both, own, theirs, load, put, send, recv):
    me = lax.axis_index("fsdp")
    core = lax.rem(me, 2)
    partner = 2 * lax.div(me, 2) + 1 - core
    barrier = pltpu.get_barrier_semaphore()
    pl.semaphore_signal(barrier, inc=1, device_id={"fsdp": partner}, device_id_type=MESH)
    pl.semaphore_wait(barrier, 1)
    parts = send.shape[0]
    size = mine.shape[0] // parts
    slices = [pl.ds(i * size, size) for i in range(parts)]
    loads = [pltpu.make_async_copy(mine.at[at], own.at[at], load.at[i]) for i, at in enumerate(slices)]
    copies = [
        pltpu.make_async_remote_copy(
            src_ref=mine.at[at], dst_ref=theirs.at[at], send_sem=send.at[i], recv_sem=recv.at[i],
            device_id={"fsdp": partner}, device_id_type=MESH,
        )
        for i, at in enumerate(slices)
    ]
    for copy in copies + loads:
        copy.start()
    puts = []
    for i, at in enumerate(slices):
        loads[i].wait()
        puts.append(pltpu.make_async_copy(own.at[at], both.at[core, at], put.at[i]))
        puts[-1].start()
    for i, at in enumerate(slices):
        copies[i].wait()
        puts.append(pltpu.make_async_copy(theirs.at[at], both.at[1 - core, at], put.at[parts + i]))
        puts[-1].start()
    for copy in puts:
        copy.wait()


def pair_call(mine):
    parts = 8
    anywhere = pl.BlockSpec(memory_space=pl.ANY)
    dma = pltpu.SemaphoreType.DMA
    return pl.pallas_call(
        pair_kernel,
        out_shape=jax.ShapeDtypeStruct((2,) + mine.shape, BF16),
        in_specs=[anywhere],
        out_specs=anywhere,
        scratch_shapes=[
            pltpu.VMEM(mine.shape, BF16), pltpu.VMEM(mine.shape, BF16), dma((parts,)), dma((2 * parts,)),
            dma((parts,)), dma((parts,)),
        ],
        compiler_params=pltpu.CompilerParams(
            collective_id=3, has_side_effects=True, vmem_limit_bytes=60 * 1024 * 1024
        ),
        name="pair",
    )(mine)


def finish_kernel(
    n, planes, cuts, groups, length_ref, place_ref, kept_ref, gn, tok, gain_ref, early, dwin, o_early,
    sums, base, base_grad, branch,
    output, token_grad, w_ref, o_ref, sums_ref,
    gn_mine, gn_theirs, hidden, grad, dgain, w_own, w_in, o_own, o_in, w_give, w_pair, w_chip, z_in, oz_in, z_out,
    oz_out, w_all, o_all, s_own, s_in, d_in, s_tot, s_up, back, out_buf, grad_buf, part,
    here, g_send, g_recv, b_send, b_recv, w_send, w_recv, o_send, o_recv, p_send, p_recv,
    z_send, z_recv, oz_send, oz_recv, y_send, y_recv, oy_send, oy_recv, s_send, s_recv, d_send, d_recv,
    u_send, u_recv,
):
    me = lax.axis_index("fsdp")
    level = lax.axis_index("rep")
    core = lax.rem(me, 2)
    chip = lax.div(me, 2)
    partner = 2 * chip + 1 - core
    span = back.shape[1]
    ahead = early[0].shape[1]
    first_cut = 1
    chip_rows = w_own.shape[0]
    rows = chip_rows // 2
    outs = o_own.shape[0]
    zrows, orows = rows // planes, outs // planes
    others = n // 2 - 1
    tile = 16
    barrier = pltpu.get_barrier_semaphore()
    for away, turn in peers_of(n):
        pl.semaphore_signal(barrier, inc=1, device_id={"fsdp": peer_at(n, me, away, turn)}, device_id_type=MESH)
    for up in range(1, planes):
        pl.semaphore_signal(barrier, inc=1, device_id={"rep": lax.rem(level + up, planes)}, device_id_type=MESH)
    pl.semaphore_wait(barrier, n - 1 + planes - 1)

    def remote(src, dst, send, recv, where):
        return pltpu.make_async_remote_copy(
            src_ref=src, dst_ref=dst, send_sem=send, recv_sem=recv, device_id=where, device_id_type=MESH
        )

    def arrived(block, send, recv):
        remote(block, block, send, recv, {"fsdp": partner}).wait_recv()

    pending = []

    def push(src, dst, send, recv, where):
        copy = remote(src, dst, send, recv, where)
        copy.start()
        pending.append(copy)

    def above(up):
        return lax.rem(level + up, planes)

    loads = [
        pltpu.make_async_copy(early[0], w_own.at[:, pl.ds(0, ahead)], here.at[0]),
        pltpu.make_async_copy(
            dwin.at[rows_at(chip, chip_rows)], w_own.at[:, pl.ds(ahead, dwin.shape[1])], here.at[1]
        ),
        pltpu.make_async_copy(o_early[0], o_own, here.at[2]),
        pltpu.make_async_copy(gn.at[core], gn_mine, here.at[3]),
        pltpu.make_async_copy(tok.at[core], hidden, here.at[4]),
        pltpu.make_async_copy(sums, s_own, here.at[5]),
        pltpu.make_async_copy(base, out_buf, here.at[6]),
        pltpu.make_async_copy(base_grad, grad_buf, here.at[7]),
        pltpu.make_async_copy(branch, part, here.at[8]),
    ]
    for i in range(others):
        loads.append(pltpu.make_async_copy(early[i + 1], w_in.at[i, :, pl.ds(0, ahead)], here.at[9 + 2 * i]))
        loads.append(pltpu.make_async_copy(o_early[i + 1], o_in.at[i], here.at[10 + 2 * i]))
    everyone = [(0, 0)] + peers_of(n)
    for c, cols in enumerate(cuts):
        if c >= first_cut:
            for i in range(others):
                target = {"fsdp": peer_at(n, me, i + 1, 0)}
                other = lax.rem(chip + i + 1, n // 2)
                k = c * others + i
                given = pl.ds(cols.start - ahead, cols.size)
                push(
                    dwin.at[rows_at(other, chip_rows), given], w_in.at[i, :, cols], w_send.at[k], w_recv.at[k],
                    target,
                )
    for copy in loads:
        copy.start()
    for index, (away, turn) in enumerate(everyone):
        if index:
            peer = peer_at(n, me, away, turn)
            push(sums, s_in.at[index - 1], s_send.at[index], s_recv.at[index], {"fsdp": peer})
    for index, (away, turn) in enumerate(everyone):
        block = rows_at(peer_at(n, me, away, turn), span)
        push(gn.at[1 - core, block], gn_theirs.at[block], g_send.at[index], g_recv.at[index], {"fsdp": partner})
    step = 64

    def norm_back(index):
        away, turn = everyone[index]
        target = peer_at(n, me, away, turn)
        block = rows_at(target, span)
        sender_index = everyone.index((away, 1 - turn))
        arrived(gn_theirs.at[block], g_send.at[sender_index], g_recv.at[sender_index])
        first = target * span

        @pl.loop(0, span // step)
        def _(i):
            at = pl.ds(pl.multiple_of(first + i * step, step), step)
            position = first + i * step + lax.broadcasted_iota(jnp.int32, (step, gn_mine.shape[1]), 0)
            total = gn_mine[at, :].astype(F32) + gn_theirs[at, :].astype(F32)
            total = jnp.where(position < length_ref[0], total, 0.0)
            h = hidden[at, :].astype(F32)
            inv = lax.rsqrt(jnp.mean(h * h, axis=1, keepdims=True) + EPS)
            normal = h * inv
            dgain[0:1, :] += jnp.sum(total * normal, axis=0, keepdims=True)
            scaled = total * gain_ref[0:1, :]
            mean = jnp.mean(scaled * normal, axis=1, keepdims=True)
            grad[at, :] = (inv * (scaled - normal * mean)).astype(BF16)

    def give_back(index):
        away, turn = everyone[index]
        peer = peer_at(n, me, away, turn)
        push(grad.at[rows_at(peer, span)], back.at[me], b_send.at[index], b_recv.at[index], {"fsdp": peer})

    def add_up(own, pieces, at, cols):
        total = own[at, cols].astype(F32)
        for i in range(pieces.shape[0]):
            total = total + pieces[i, at, cols].astype(F32)
        return total.astype(BF16)

    def stage_sum(c):
        cols = cuts[c]
        if c >= first_cut:
            for i in range(others):
                k = c * others + i
                arrived(w_in.at[i, :, cols], w_send.at[k], w_recv.at[k])

        @pl.loop(0, rows // tile)
        def _(i):
            at = pl.ds(pl.multiple_of((1 - core) * rows + i * tile, tile), tile)
            w_give[pl.ds(pl.multiple_of(i * tile, tile), tile), cols] = add_up(w_own, w_in, at, cols)

        push(w_give.at[:, cols], w_pair.at[:, cols], p_send.at[c], p_recv.at[c], {"fsdp": partner})

        @pl.loop(0, rows // tile)
        def _(i):
            at = pl.ds(pl.multiple_of(core * rows + i * tile, tile), tile)
            w_chip[core, pl.ds(pl.multiple_of(i * tile, tile), tile), cols] = add_up(w_own, w_in, at, cols)

    def stage_up(c):
        cols = cuts[c]
        arrived(w_pair.at[:, cols], p_send.at[c], p_recv.at[c])
        w_chip[1 - core, :, cols] = w_pair[:, cols]
        for up in range(1, planes):
            k = c * (planes - 1) + up - 1
            push(
                w_chip.at[:, rows_at(above(up), zrows), cols], z_in.at[up - 1, :, :, cols],
                z_send.at[k], z_recv.at[k], {"rep": above(up)},
            )

    def stage_total(c):
        cols = cuts[c]
        for up in range(1, planes):
            k = c * (planes - 1) + up - 1
            arrived(z_in.at[up - 1, :, :, cols], z_send.at[k], z_recv.at[k])
        at = rows_at(level, zrows)
        for q in range(2):
            total = w_chip[q, at, cols].astype(F32)
            for k in range(planes - 1):
                total = total + z_in[k, q, :, cols].astype(F32)
            z_out[q, :, cols] = total.astype(BF16)
            w_all[q, at, cols] = total.astype(BF16)
        for up in range(1, planes):
            k = c * (planes - 1) + up - 1
            push(z_out.at[:, :, cols], w_all.at[:, at, cols], y_send.at[k], y_recv.at[k], {"rep": above(up)})

    def finish_rows(buf, pieces, s):
        kept = kept_ref[s]
        chosen = place_ref[s]

        @pl.loop(0, span // step)
        def _(i):
            at = pl.ds(pl.multiple_of(i * step, step), step)
            row = i * step + lax.broadcasted_iota(jnp.int32, (step, buf.shape[2]), 0)
            added = jnp.where(row < kept, pieces[chosen, at, :].astype(F32), 0.0)
            buf[s, at, :] = (buf[s, at, :].astype(F32) + added).astype(BF16)

    for copy in loads[:3] + loads[9:]:
        copy.wait()
    stage_sum(0)

    @pl.loop(0, outs // tile)
    def _(i):
        at = pl.ds(pl.multiple_of(i * tile, tile), tile)
        o_own[at, :] = add_up(o_own, o_in, at, slice(None))

    for up in range(1, planes):
        push(
            o_own.at[rows_at(above(up), orows)], oz_in.at[up - 1], oz_send.at[up - 1], oz_recv.at[up - 1],
            {"rep": above(up)},
        )
    stage_up(0)
    for copy in loads[3:6]:
        copy.wait()
    dgain[...] = jnp.zeros_like(dgain)
    for index in range(n):
        norm_back(index)
    seg = dgain.shape[1] // n
    for index, (away, turn) in enumerate(everyone):
        if index:
            peer = peer_at(n, me, away, turn)
            cols = pl.ds(pl.multiple_of(peer * seg, seg), seg)
            push(dgain.at[:, cols], d_in.at[index - 1], d_send.at[index], d_recv.at[index], {"fsdp": peer})
    s_tot[core] = s_own[...]
    s_tot[1 - core] = jnp.zeros_like(s_own)
    for index, (away, turn) in enumerate(everyone):
        if index:
            arrived(s_in.at[index - 1], s_send.at[index], s_recv.at[index])
            arrived(d_in.at[index - 1], d_send.at[index], d_recv.at[index])
            theirs = lax.rem(core + turn, 2)
            s_tot[theirs] = s_tot[theirs] + s_in[index - 1]
    mine = dgain[:, pl.ds(pl.multiple_of(me * seg, seg), seg)]
    for index in range(n - 1):
        mine = mine + d_in[index]
    s_tot[0, CONV + 3 : CONV + 4, 0:seg] = mine[0:1]
    for up in range(1, planes):
        push(s_tot, s_up.at[up - 1], u_send.at[up - 1], u_recv.at[up - 1], {"rep": above(up)})
    count = len(cuts)
    waiting = list(range(1, n))
    for c in range(1, count):
        stage_sum(c)
        for index in waiting[: 2 if c < count - 1 else n]:
            give_back(index)
        del waiting[:2]
        stage_up(c)
        stage_total(c - 1)
        if c == 1:
            for i in range(planes - 1):
                arrived(oz_in.at[i], oz_send.at[i], oz_recv.at[i])
            at = rows_at(level, orows)
            total = o_own[at, :].astype(F32)
            for k in range(planes - 1):
                total = total + oz_in[k].astype(F32)
            oz_out[...] = total.astype(BF16)
            o_all[at, :] = total.astype(BF16)
            for up in range(1, planes):
                push(oz_out, o_all.at[at], oy_send.at[up - 1], oy_recv.at[up - 1], {"rep": above(up)})
    for copy in loads[6:9]:
        copy.wait()
    for s in range(n):
        finish_rows(out_buf, part, s)
    stores = [pltpu.make_async_copy(out_buf, output, here.at[6])]
    stores[0].start()
    stage_total(count - 1)

    for i in range(planes - 1):
        arrived(s_up.at[i], u_send.at[i], u_recv.at[i])
    total = s_tot[...]
    for k in range(planes - 1):
        total = total + s_up[k]
    sums_ref[...] = total
    for c, cols in enumerate(cuts):
        for up in range(1, planes):
            below = lax.rem(level + planes - up, planes)
            k = c * (planes - 1) + up - 1
            arrived(w_all.at[:, rows_at(below, zrows), cols], y_send.at[k], y_recv.at[k])
    inner, group, heads = groups
    for g in range(2 * inner // group):
        q, at = g % 2, g // 2 * group
        w_ref[:, g * group : (g + 1) * group] = w_all[q, :, at : at + group].astype(F32)
        w_ref[:, 2 * inner + g * group : 2 * inner + (g + 1) * group] = (
            w_all[q, :, inner + at : inner + at + group].astype(F32)
        )
    both = w_all[0, :, 2 * inner : 2 * inner + 2 * STATE].astype(F32)
    both = both + w_all[1, :, 2 * inner : 2 * inner + 2 * STATE].astype(F32)
    w_ref[:, 4 * inner : 4 * inner + 2 * STATE] = both
    first = 2 * inner + 2 * STATE
    tails = [w_all[q, :, first : first + LANES].astype(F32) for q in range(2)]
    size = group // HEADDIM
    pieces = [tails[g % 2][:, g // 2 * size : (g // 2 + 1) * size] for g in range(2 * inner // group)]
    w_ref[:, 4 * inner + 2 * STATE :] = jnp.concatenate(pieces, axis=1)
    for up in range(1, planes):
        below = lax.rem(level + planes - up, planes)
        arrived(o_all.at[rows_at(below, orows)], oy_send.at[up - 1], oy_recv.at[up - 1])
    o_ref[...] = o_all[...].astype(F32)
    for index, (away, turn) in enumerate(everyone):
        if index:
            owner = sender_at(n, me, away, turn)
            arrived(back.at[owner], b_send.at[index], b_recv.at[index])
    back[me] = grad[rows_at(me, span), :]
    for s in range(n):
        finish_rows(grad_buf, back, s)
    stores.append(pltpu.make_async_copy(grad_buf, token_grad, here.at[7]))
    stores[1].start()
    for copy in pending:
        copy.wait_send()
    for copy in stores:
        copy.wait()


def finish_call(
    n, planes, group, length, place, kept, gn, tok, gain, early, dwin, o_early, sums, base, base_grad, branch,
):
    _, total, width = gn.shape
    span = total // n
    ahead = early[0].shape[1]
    wide = ahead + dwin.shape[1]
    inner = (n // 2) * o_early[0].shape[0]
    heads = inner // HEADDIM
    chip_rows, outs = dwin.shape[0] // (n // 2), inner // (n // 2)
    rows = chip_rows // 2
    others = n // 2 - 1
    lane_tiles = dwin.shape[1] // LANES
    late = 3
    bounds = [ahead + (lane_tiles * i + late - 1) // late * LANES for i in range(late + 1)]
    cuts = [pl.ds(0, ahead)] + [pl.ds(bounds[i], bounds[i + 1] - bounds[i]) for i in range(late)]
    pieces = late + 1
    anywhere = pl.BlockSpec(memory_space=pl.ANY)
    vmem = pl.BlockSpec(memory_space=pltpu.VMEM)
    smem = pl.BlockSpec(memory_space=pltpu.SMEM)
    dma = pltpu.SemaphoreType.DMA
    up = planes - 1
    return pl.pallas_call(
        functools.partial(finish_kernel, n, planes, cuts, (inner, group, heads)),
        out_shape=[
            jax.ShapeDtypeStruct((n, span, width), BF16),
            jax.ShapeDtypeStruct((n, span, width), BF16),
            jax.ShapeDtypeStruct((rows, 4 * inner + 2 * STATE + 2 * heads), F32),
            jax.ShapeDtypeStruct((outs, width), F32),
            jax.ShapeDtypeStruct((2,) + sums.shape, F32),
        ],
        in_specs=[smem, smem, smem, anywhere, anywhere, vmem, [anywhere] * len(early), anywhere]
        + [[anywhere] * len(early), anywhere, anywhere, anywhere, anywhere],
        out_specs=[anywhere, anywhere, vmem, vmem, vmem],
        scratch_shapes=[
            pltpu.VMEM((total, width), BF16), pltpu.VMEM((total, width), BF16), pltpu.VMEM((total, width), BF16),
            pltpu.VMEM((total, width), BF16), pltpu.VMEM((8, width), F32),
            pltpu.VMEM((chip_rows, wide), BF16), pltpu.VMEM((others, chip_rows, wide), BF16),
            pltpu.VMEM((outs, width), BF16), pltpu.VMEM((others, outs, width), BF16),
            pltpu.VMEM((rows, wide), BF16), pltpu.VMEM((rows, wide), BF16), pltpu.VMEM((2, rows, wide), BF16),
            pltpu.VMEM((up, 2, rows // planes, wide), BF16), pltpu.VMEM((up, outs // planes, width), BF16),
            pltpu.VMEM((2, rows // planes, wide), BF16), pltpu.VMEM((outs // planes, width), BF16),
            pltpu.VMEM((2, rows, wide), BF16), pltpu.VMEM((outs, width), BF16),
            pltpu.VMEM(sums.shape, F32), pltpu.VMEM((n - 1,) + sums.shape, F32),
            pltpu.VMEM((n - 1, 8, LANES), F32), pltpu.VMEM((2,) + sums.shape, F32),
            pltpu.VMEM((up, 2) + sums.shape, F32),
            pltpu.VMEM((n, span, width), BF16), pltpu.VMEM((n, span, width), BF16),
            pltpu.VMEM((n, span, width), BF16), pltpu.VMEM((n, span, width), BF16),
            dma((9 + 2 * others,)), dma((n,)), dma((n,)), dma((n,)), dma((n,)),
            dma((pieces * others,)), dma((pieces * others,)), dma((others,)), dma((others,)),
            dma((pieces,)), dma((pieces,)), dma((pieces * up,)), dma((pieces * up,)), dma((up,)), dma((up,)),
            dma((pieces * up,)), dma((pieces * up,)), dma((up,)), dma((up,)),
            dma((n,)), dma((n,)), dma((n,)), dma((n,)), dma((up,)), dma((up,)),
        ],
        compiler_params=pltpu.CompilerParams(
            collective_id=1, has_side_effects=True, vmem_limit_bytes=60 * 1024 * 1024
        ),
        name="finish",
    )(length, place, kept, gn, tok, gain, early, dwin, o_early, sums, base, base_grad, branch)


def pairs_of(n):
    return [[2 * c, 2 * c + 1] for c in range(n // 2)]


def columns_of(n):
    return [list(range(q, n, 2)) for q in range(2)]


def halves(array, axis, group):
    shape = array.shape
    view = array.reshape(shape[:axis] + (shape[axis] // (2 * group), 2, group) + shape[axis + 1 :])
    out = []
    for q in range(2):
        part = lax.index_in_dim(view, q, axis + 1, keepdims=False)
        out.append(part.reshape(shape[:axis] + (shape[axis] // 2,) + shape[axis + 1 :]))
    return out


def interleave(first, second, axis, group):
    shape = first.shape
    views = [
        part.reshape(shape[:axis] + (shape[axis] // group, 1, group) + shape[axis + 1 :]) for part in (first, second)
    ]
    return jnp.concatenate(views, axis=axis + 1).reshape(shape[:axis] + (2 * shape[axis],) + shape[axis + 1 :])


def body(
    tokens, cotangent, lengths, dealing, norm_gain, in_weight, conv_weight, conv_bias, dt_bias, a_log, skip_gain,
    out_gain, out_weight,
):
    n = lax.axis_size("fsdp")
    me = lax.axis_index("fsdp")
    core = lax.rem(me, 2)
    pairs, columns = pairs_of(n), columns_of(n)
    local_tokens, local_grad = tokens[0], cotangent[0]
    count, span, width = local_tokens.shape
    length = span * n
    inner = INNER // 2
    heads = HEADS // 2
    group = max(HEADDIM, INNER // n)
    blocks = length // BLOCK
    rows = in_weight.shape[0]

    slots = jnp.arange(count, dtype=jnp.int32)
    own = jnp.sum(jnp.where(dealing[0][:, None] == slots[None, :], lengths[0][None, :], 0), axis=1)
    ahead = (own[None, :] > own[:, None]) | ((own[None, :] == own[:, None]) & (slots[None, :] < slots[:, None]))
    rank = jnp.sum(ahead.astype(jnp.int32), axis=1)
    place = jnp.where(rank < count // 2, 2 * rank, 2 * (count - 1 - rank) + 1)
    source = jnp.sum(jnp.where(place[None, :] == slots[:, None], slots[None, :], 0), axis=1)
    placed = jnp.sum(jnp.where(place[None, :] == slots[:, None], own[None, :], 0), axis=1)
    chip_lens = lax.dynamic_slice_in_dim(placed, me - core, 2)
    chip_blocks = (chip_lens + BLOCK - 1) // BLOCK
    grid_steps = most_blocks(count, length)

    main = INNER + INNER + 2 * STATE
    gates = halves(in_weight[:, :INNER], 1, group)
    vals = halves(in_weight[:, INNER : 2 * INNER], 1, group)
    both = in_weight[:, 2 * INNER : main]
    steps = halves(in_weight[:, main:], 1, group // HEADDIM)
    pad = jnp.zeros((rows, LANES - heads), BF16)
    shards = jnp.stack([jnp.concatenate([gates[q], vals[q], both, steps[q], pad], axis=1) for q in range(2)])
    aligned = INNER // n >= HEADDIM
    small = jnp.concatenate([norm_gain, conv_weight.reshape(-1), conv_bias, out_gain])
    room = -(-small.shape[0] // (16 * LANES)) * 16
    small = jnp.pad(small, (0, room * LANES - small.shape[0])).reshape(room, LANES)
    tok, win, smalls, sent_grad = start_call(n, source, local_tokens, local_grad, shards, small)
    tok, sent_grad, out_weight = lax.optimization_barrier((tok, sent_grad, out_weight))
    smalls = smalls.reshape(n, -1).astype(F32)
    own_grad = lax.all_to_all(sent_grad, "fsdp", split_axis=0, concat_axis=0, tiled=True)
    if aligned:
        wout = lax.all_gather(out_weight, "fsdp", axis=0, tiled=True, axis_index_groups=columns)
    else:
        whole = lax.all_gather(out_weight, "fsdp", axis=0, tiled=True)
        wout = lax.dynamic_index_in_dim(jnp.stack(halves(whole, 0, group)), core, 0, keepdims=False)
    cuts = [norm_gain.shape[0], conv_weight.size, conv_bias.shape[0], out_gain.shape[0]]
    ends = [sum(cuts[: i + 1]) for i in range(4)]
    first_gain = smalls[:, : ends[0]].reshape(-1)
    conv_w = smalls[:, ends[0] : ends[1]].reshape(n, CONV, -1).transpose(1, 0, 2).reshape(CONV, -1)
    conv_b = smalls[:, ends[1] : ends[2]].reshape(1, -1)
    gated_gain = smalls[:, ends[2] : ends[3]].reshape(1, -1)

    def half_of(array, axis, size):
        return lax.dynamic_index_in_dim(jnp.stack(halves(array, axis, size)), core, 0, keepdims=False)

    conv_all = jnp.concatenate([conv_w, conv_b, jnp.zeros((3, conv_w.shape[1]), F32)], axis=0)
    conv_all = jnp.concatenate([half_of(conv_all[:, :INNER], 1, group), conv_all[:, INNER:]], axis=1)
    head_rows = jnp.stack([dt_bias, jnp.exp(a_log), skip_gain] + [jnp.zeros_like(dt_bias)] * 5)
    head_rows = half_of(head_rows, 1, group // HEADDIM)
    dwide = jnp.repeat(head_rows[2:3], HEADDIM, axis=1)
    hp = jnp.concatenate([head_rows, jnp.zeros((8, LANES - heads), F32)], axis=1)
    og = half_of(gated_gain, 1, group)
    gain = first_gain[None, :]
    cb = conv_all[CONV : CONV + 1]
    args = (gain, win, conv_all, cb, hp, dwide, og)
    gate, cin, raw, y, states, ss, mixing = fwd_call(grid_steps, chip_blocks, tok, *args)

    own_grad, mixing = lax.optimization_barrier((own_grad, mixing))
    cot = pair_call(own_grad.reshape(length, width))
    gm, v, bp = mid_call(grid_steps, chip_blocks, chip_lens, cot, mixing, wout)
    branch, rv = exchange_call(bp, ss, v)

    def restore(part):
        return lax.all_to_all(part.reshape(n, span, width), "fsdp", split_axis=0, concat_axis=0, tiled=True)

    kept = jnp.clip(own - me * span, 0, span)
    branch = restore(branch)
    parts = n // 2
    planes = lax.axis_size("rep")
    fused = aligned and rows % (16 * planes) == 0 and out_weight.shape[0] % (16 * planes) == 0
    chip = (me // 2 if fused else me * 0).reshape(1)
    dy, gp, dog, *early = gate_call(
        grid_steps, chip_blocks, chip_lens, chip, parts, tok, cot, gain, win, gm, og, gate, y, rv
    )
    early, dwout = early[:parts], early[parts:]
    if fused:

        def move(pieces):
            return [pieces[0]] + [
                lax.ppermute(pieces[away], "fsdp", [(d, (d + 2 * away) % n) for d in range(n)])
                for away in range(1, parts)
            ]

        early, dwout = move(early), move(dwout)
    gn, dwin, sums = bwd_call(
        grid_steps, chip_blocks, tok, gain, win, *args[2:6], dog, dy, gp, cin, raw, y, states
    )
    def widen(half, axis, size):
        zero = jnp.zeros_like(half)
        return interleave(jnp.where(core == 0, half, zero), jnp.where(core == 1, half, zero), axis, size)

    own_len = lax.dynamic_slice_in_dim(chip_lens, core, 1)
    if fused:
        output, token_grad, dwin, dwout, sums = finish_call(
            n, planes, group, own_len, place, kept, gn, tok, gain, early, dwin, dwout, sums, local_tokens, local_grad,
            branch,
        )
        dgain = sums[0, CONV + 3, : width // n]
        halves_of = [sums[0], sums[1]]
    else:
        halves_of = [jnp.where(core == q, sums, jnp.zeros_like(sums)) for q in range(2)]
    first, second = halves_of
    dconv = jnp.concatenate(
        [
            interleave(first[: CONV + 1, :inner], second[: CONV + 1, :inner], 1, group),
            first[: CONV + 1, inner:] + second[: CONV + 1, inner:],
        ],
        axis=1,
    )
    dheads = jnp.concatenate(
        [
            interleave(
                first[CONV + 2 : CONV + 3, at : at + heads], second[CONV + 2 : CONV + 3, at : at + heads], 1,
                group // HEADDIM,
            )
            for at in range(0, 3 * LANES, LANES)
        ],
        axis=0,
    )
    dog = interleave(first[CONV + 1, :inner], second[CONV + 1, :inner], 0, group)
    if not fused:
        other = lax.dynamic_index_in_dim(gn, 1 - core, 0, keepdims=False)
        other = lax.ppermute(other, "fsdp", [(2 * c + q, 2 * c + 1 - q) for c in range(n // 2) for q in range(2)])
        mine = lax.dynamic_index_in_dim(gn, core, 0, keepdims=False)
        hidden = lax.dynamic_index_in_dim(tok, core, 0, keepdims=False).astype(F32)
        inv = lax.rsqrt(jnp.mean(hidden * hidden, axis=-1, keepdims=True) + EPS)
        position = jnp.arange(length, dtype=jnp.int32)[:, None]
        grad_normed = jnp.where(position < own_len[0], mine.astype(F32) + other.astype(F32), 0.0)
        dgain = jnp.sum(grad_normed * hidden * inv, axis=0)
        scaled = grad_normed * first_gain[None, :]
        grad_hidden = inv * scaled - hidden * (inv * inv * inv) * jnp.mean(scaled * hidden, axis=-1, keepdims=True)
        back = restore(grad_hidden.astype(BF16))
        dwin = jnp.concatenate([jnp.concatenate(early, axis=0), dwin], axis=1)
        dwout = jnp.concatenate(dwout, axis=0)
        dwin = lax.psum_scatter(
            dwin.astype(F32), "fsdp", scatter_dimension=0, tiled=True, axis_index_groups=columns
        )
        dwin = lax.psum(dwin, "rep").reshape(2, rows, -1)
        dwin = lax.all_to_all(dwin, "fsdp", split_axis=0, concat_axis=0, tiled=True, axis_index_groups=pairs)
        if aligned:
            dwout = lax.psum_scatter(
                dwout.astype(F32), "fsdp", scatter_dimension=0, tiled=True, axis_index_groups=columns
            )
        else:
            wide_grad = widen(dwout.astype(F32), 0, group)
            dwout = lax.psum_scatter(wide_grad, "fsdp", scatter_dimension=0, tiled=True)
        dwout = lax.psum(dwout, "rep")
        c0, c1, c2 = inner, 2 * inner, 2 * inner + 2 * STATE
        dwin = jnp.concatenate(
            [
                interleave(dwin[0, :, :c0], dwin[1, :, :c0], 1, group),
                interleave(dwin[0, :, c0:c1], dwin[1, :, c0:c1], 1, group),
                dwin[0, :, c1:c2] + dwin[1, :, c1:c2],
                interleave(dwin[0, :, c2 : c2 + heads], dwin[1, :, c2 : c2 + heads], 1, group // HEADDIM),
            ],
            axis=1,
        )
        dconv, dheads, dog, dgain = lax.psum((dconv, dheads, dog, dgain), ("rep", "fsdp"))
        dgain = lax.dynamic_slice_in_dim(dgain, me * (width // n), width // n)
        output = combine_call(place, kept, local_tokens, branch)
        token_grad = combine_call(place, kept, local_grad, back)

    def shard(array):
        size = array.shape[-1] // n
        return lax.dynamic_slice_in_dim(array, me * size, size, axis=array.ndim - 1)

    dconv = shard(dconv)
    return (
        output[None], token_grad[None], dgain, dwin, dconv[:CONV], dconv[CONV], dheads[1], dheads[2], dheads[0],
        shard(dog), dwout,
    )


def solution(mesh):
    row = P("rep", None, "fsdp", None)
    per = P("rep", None)
    in_specs = (
        row, row, per, per, P("fsdp"), P("fsdp", None), P(None, "fsdp"), P("fsdp"), P(), P(), P(), P("fsdp"),
        P("fsdp", None),
    )
    out_specs = (
        row, row, P("fsdp"), P("fsdp", None), P(None, "fsdp"), P("fsdp"), P(), P(), P(), P("fsdp"), P("fsdp", None),
    )
    return jax.shard_map(body, mesh=mesh, in_specs=in_specs, out_specs=out_specs, check_vma=False)
```

time: 606 us -> 520 us (0.86)
  waiting for transfers between devices: 64.2 us -> 17.6 us
  Pallas kernels: 462 us -> 439 us
  other arithmetic: 15.5 us -> 6.01 us
  local copies, waits for them, and re-layouts: 36.6 us -> 29.6 us
    all_to_all x1, waiting for transfers between devices: 63.5 us -> 12.3 us  [body(): lax.all_to_all(sent_grad, 'fsdp', split_axis=0, concat_axis=0, tiled=True)]
    pallas_call x1, Pallas kernels: 149 us -> 111 us  [finish_call(): pl.pallas_call(functools.partial(finish_kernel, n, planes, cuts, (inner,...]
    gather x2 -> x0, local copies, waits for them, and re-layouts: 10.1 us -> none  [the longest x1 5.05 us: body(): jnp.take(local_tokens, source, axis=0)]
    pallas_call x3, Pallas kernels: 134 us -> 143 us  [the longest x1 96 us: bwd_call(): pl.pallas_call(functools.partial(bwd_kernel, inner, heads), grid_spec=gri...]
    select_n x6 -> x0, other arithmetic: 9.25 us -> none  [the longest x1 7.67 us: body(): sent_grad = jnp.take(local_grad, source, axis=0)]
  transfers between devices with their start and end apart: 4 -> 9, of which waited for: 1 -> 2; matrix products, arithmetic and copies ran while one was open for 4% -> 1% of each run, Pallas kernels for 54% -> 29%
where the time goes in v2:
time: 520 us; the launch traced here: 521 us
  Pallas kernels  439 us (84%)
  local copies, waits for them, and re-layouts  29.6 us (6%)
  waiting for transfers between devices  17.6 us (3%)
  between operations  14.5 us (3%)
  starting transfers between devices  14.3 us (3%)
  other arithmetic  6.01 us (1%)
    pallas_call x1, Pallas kernels, finish_call(): pl.pallas_call(functools.partial(finish_kernel, n, planes, cuts, (inner,...  111 us
    pallas_call x1, Pallas kernels, start_call(): pl.pallas_call(functools.partial(start_kernel, n), out_shape=[jax.ShapeDt...  107 us
    pallas_call x1, Pallas kernels, bwd_call(): pl.pallas_call(functools.partial(bwd_kernel, inner, heads), grid_spec=gri...  96 us
    pallas_call x1, Pallas kernels, fwd_call(): pl.pallas_call(functools.partial(fwd_kernel, inner, heads), grid_spec=gri...  47.5 us
    pallas_call x1, Pallas kernels, gate_call(): pl.pallas_call(functools.partial(gate_kernel, parts), grid_spec=pltpu.Pre...  38.7 us
    pallas_call x1, Pallas kernels, mid_call(): pl.pallas_call(mid_kernel, grid_spec=pltpu.PrefetchScalarGridSpec(num_sca...  19.3 us
    all_to_all x1, waiting for transfers between devices, body(): lax.all_to_all(sent_grad, 'fsdp', split_axis=0, concat_axis=0, tiled=True)  12.3 us
    unnamed x23, local copies, waits for them, and re-layouts  11.5 us
  transfers between devices with their start and end apart: 9, of which 2 were waited for; matrix products, arithmetic and copies ran while one was open for 1% of the time, Pallas kernels for 29%

profile of v2, /device:TPU:0, one launch (start us, length us, event | category | flops | bytes accessed | tf_op | source)
XLA Modules:
  0.0 520.8 jit_solution(13307260186301476782)
XLA Ops:
  7.2 0.7 slice.131
  7.9 0.8 slice.130
  8.8 1.3 fusion.9
  10.0 0.9 select_reduce_fusion.2
  11.1 0.5 copy-done.4
  11.6 0.6 select_reduce_fusion
  12.2 0.8 reshape.121
  13.0 2.1 concatenate.39
  15.1 0.6 pad_bitcast_fusion.small
  16.8 0.3 concatenate.38
  17.3 1.2 pad_maximum_fusion.shards
  18.5 107.5 %start.1 = (bf16[2,2048,1024]{2,1,0:T(8,128)(2,1)}, bf16[1024,2432]{1,0:T(8,128)(2,1)}, bf16[8,16,128]{2,1,0:T(8,128)(2,1)}, bf16[8,256,1024]{2,1,0:T(8,128)(2,1)}) custom-call(s32[8]{0:T(128)} %get-tuple-element.130.source_ref, bf16[8,256,1024]{2,1,0:T(8,128)(2,1)} %bitcast.54, bf16[8,256,1024]{2,1,0:T(8,128)(2,1)} %bitcast.56, ...), custom_call_target="tpu_custom_call" | custom-call | tf_op jit(solution)/shard_map/start/pallas_call | solution.py:865
  126.0 4.7 all-to-all-start
  131.3 0.6 slice.174
  132.9 0.6 concatenate.42.hp_ref
  133.8 0.7 broadcast_in_dim.59.dwide_ref
  134.5 0.6 and_select_fusion
  135.1 0.6 fusion.6.og_ref
  135.7 0.6 fusion.4.cb_ref
  136.3 0.6 pad_maximum_fusion.1.cw_ref
  136.9 47.5 %layer_forward.1 = (f32[2,2048,1024]{2,1,0:T(8,128)}, f32[2,2048,1280]{2,1,0:T(8,128)}, f32[2,2048,128]{2,1,0:T(8,128)}, f32[2,2048,1024]{2,1,0:T(8,128)}, f32[2...) custom-call(s32[2]{0:T(128)} %get-tuple-element.132.nb_ref, ...), custom_call_target="tpu_custom_call" | custom-call | flops 14562623488 | bytes 62914560 | tf_op jit(solution)/shard_map/layer_forward/pallas_call | solution.py:269
  184.5 12.3 %all-to-all-done = bf16[8,256,1024]{2,1,0:T(8,128)(2,1)} async-done(((bf16[8,256,1024]{2,1,0:T(8,128)(2,1)}), bf16[8,256,1024]{2,1,0:T(8,128)(2,1)}, u32[]{:S(2)}, u32[]{:S(2)}) %all-to-all-start) | async-done | bytes 4194336 | tf_op jit(solution)/shard_map/all_to_all | solution.py:1433
  196.7 8.5 %pair.1.cot_ref = bf16[2,2048,1024]{2,1,0:T(8,128)(2,1)} custom-call(bf16[2048,1024]{1,0:T(8,128)(2,1)} %bitcast.25.mine), custom_call_target="tpu_custom_call" | custom-call | tf_op jit(solution)/shard_map/pair/pallas_call | solution.py:997
  205.3 19.3 %layer_middle.1 = (f32[2,2048,1024]{2,1,0:T(8,128)}, f32[128,256]{1,0:T(8,128)}, bf16[2,2048,1024]{2,1,0:T(8,128)(2,1)}) custom-call(s32[2]{0:T(128)} %get-tuple-element.132.nb_ref, s32[2]{0:T(128)} %get-tuple-element.133.len_ref, bf16[2,2048,1024]{2,1,0:T(8,128)(2,1)} %pair.1.cot_ref, bf16[2,2048,1024]{2,1,0:T(8,128)(2,1)} %get-tuple-element.59.sc_ref, ...), custom_call_target="tpu_custom_call" | custom-call | flops 10000000000 | bytes 31457280 | tf_op jit(solution)/shard_map/layer_middle/pallas_call | solution.py:316
  224.5 10.7 %exchange.1 = (bf16[2048,1024]{1,0:T(8,128)(2,1)}, f32[128,256]{1,0:T(8,128)}) custom-call(bf16[2,2048,1024]{2,1,0:T(8,128)(2,1)} %get-tuple-element.64.bp, f32[128,256]{1,0:T(8,128)} %get-tuple-element.65.ss_ref, f32[128,256]{1,0:T(8,128)} %get-tuple-element.66.v_ref), custom_call_target="tpu_custom_call" | custom-call | tf_op jit(solution)/shard_map/exchange/pallas_call | solution.py:943
  235.2 38.7 %layer_gate.1 = (f32[2,2048,1024]{2,1,0:T(8,128)}, bf16[2,2048,1024]{2,1,0:T(8,128)(2,1)}, f32[8,1024]{1,0:T(8,128)}, bf16[256,1024]{1,0:T(8,128)(2,1)}, bf16[25...) custom-call(s32[2]{0:T(128)} %get-tuple-element.132.nb_ref, ...), custom_call_target="tpu_custom_call" | custom-call | flops 20000000000 | bytes 62914560 | tf_op jit(solution)/shard_map/layer_gate/pallas_call | solution.py:415
  274.0 0.6 dynamic_slice.27.length_ref
  274.5 0.5 subtract_clamp_fusion.kept_ref
  275.1 4.6 all-to-all-start.1
  279.6 1.9 collective-permute-start.1
  281.5 1.4 collective-permute-start.2
  283.0 0.6 collective-permute-start.3
  283.6 1.0 collective-permute-start.4
  284.6 5.3 %collective-permute-done.early_1_ = bf16[256,1024]{1,0:T(8,128)(2,1)S(1)} collective-permute-done((bf16[256,1024]{1,0:T(8,128)(2,1)}, bf16[256,1024]{1,0:T(8,128)(2,1)S(1)}, u32[]{:S(2)}, u32[]{:S(2)}) %collective-permute-start) | collective-permute-done | bytes 524320 | tf_op jit(solution)/shard_map/ppermute | solution.py:1483
  289.9 96.0 %layer_backward.1 = (bf16[2,2048,1024]{2,1,0:T(8,128)(2,1)}, bf16[1024,1408]{1,0:T(8,128)(2,1)}, f32[8,1280]{1,0:T(8,128)}) custom-call(s32[2]{0:T(128)} %get-tuple-element.132.nb_ref, bf16[2,2048,1024]{2,1,0:T(8,128)(2,1)} %get-tuple-element.53.tok_ref.tok, f32[1,1024]{1,0:T(1,128)} %bitcast.82, bf16[1024,2432]{1,0:T(8,128)(2,1)} %get-tuple-element.55.win_ref.wgate_ref, ...), custom_call_target="tpu_custom_call" | custom-call | flops 99999997952 | bytes 104857600 | tf_op jit(solution)/shard_map/layer_backward/pallas_call | solution.py:683
  385.9 110.7 %finish.1 = (bf16[8,256,1024]{2,1,0:T(8,128)(2,1)}, bf16[8,256,1024]{2,1,0:T(8,128)(2,1)}, f32[128,4384]{1,0:T(8,128)}, f32[256,1024]{1,0:T(8,128)}, f32[2,8,1280]{2,1,0:T(8,128)}) custom-call(s32[1]{0:T(128)} %dynamic_slice.27.length_ref, s32[8]{0:T(128)} %copy-done.4, s32[8]{0:T(128)} %subtract_clamp_fusion.kept_ref, ...), custom_call_target="tpu_custom_call" | custom-call | tf_op jit(solution)/shard_map/finish/pallas_call | solution.py:1326
  496.6 1.2 slice_bitcast_fusion.2
  497.8 0.8 slice_bitcast_fusion.1
  498.9 0.6 slice_reduce_fusion.1
  499.5 0.6 slice.193
  500.4 0.6 squeeze_reshape.9
  501.1 0.6 squeeze_reshape.10
  501.8 0.6 squeeze_reshape.11
  502.5 3.0 copy.78
  505.5 0.6 dynamic_slice.33
  506.1 4.8 copy.97
  510.9 2.0 copy.98
  513.0 1.0 copy.99
  (99 shorter events, 4.2 us)
Async XLA Ops:
  7.2 198.1 %all-gather.2.cloned.1.call-start = ((), (), s32[]{:S(2)}) async-start(), calls=%async_computation.2 | async-start | bytes 2621440 | tf_op jit(solution)/shard_map/all_gather | solution.py:1435
  11.1 0.5 copy-start.4
  126.0 4.8 copy-start.3
  126.0 6.0 %copy-start.7 = (f32[32]{0:T(128)S(1)}, f32[32]{0:T(128)}, u32[]{:S(2)}) copy-start(f32[32]{0:T(128)} %param.22) | copy-start | bytes 388
  126.0 6.1 %copy-start.5 = (f32[32]{0:T(128)S(1)}, f32[32]{0:T(128)}, u32[]{:S(2)}) copy-start(f32[32]{0:T(128)} %param.21) | copy-start | bytes 388
  126.0 6.1 %copy-start.6 = (f32[32]{0:T(128)S(1)}, f32[32]{0:T(128)}, u32[]{:S(2)}) copy-start(f32[32]{0:T(128)} %param.23) | copy-start | bytes 388
  126.0 70.7 %all-to-all-start = ((bf16[8,256,1024]{2,1,0:T(8,128)(2,1)}), bf16[8,256,1024]{2,1,0:T(8,128)(2,1)}, u32[]{:S(2)}, u32[]{:S(2)}) async-start(bf16[8,256,1024]{2,1,0:T(8,128)(2,1)} %get-tuple-element.56), calls=%async_computation | async-start | bytes 8388608 | tf_op jit(solution)/shard_map/all_to_all | solution.py:1433
  273.9 16.0 %collective-permute-start = (bf16[256,1024]{1,0:T(8,128)(2,1)}, bf16[256,1024]{1,0:T(8,128)(2,1)S(1)}, u32[]{:S(2)}, u32[]{:S(2)}) collective-permute-start(bf16[256,1024]{1,0:T(8,128)(2,1)} %get-tuple-element.76), channel_id=1, source_target_pairs={{0,2},{1,3},{2,4},{3,5},{4,6},{5,7},{6,0},{7,1},{8,10},{9,11},{10,... | collective-permute-start | bytes 1572872 | tf_op jit(solution)/shard_map/ppermute | solution.py:1483
  275.1 110.8 %all-to-all-start.1 = ((bf16[8,256,1024]{2,1,0:T(8,128)(2,1)}), bf16[8,256,1024]{2,1,0:T(8,128)(2,1)}, u32[]{:S(2)}, u32[]{:S(2)}) async-start(bf16[8,256,1024]{2,1,0:T(8,128)(2,1)} %bitcast.58), calls=%async_computation.1 | async-start | bytes 8388608 | tf_op jit(solution)/shard_map/all_to_all | solution.py:1467
  279.6 106.2 %collective-permute-start.1 = (bf16[256,1024]{1,0:T(8,128)(2,1)}, bf16[256,1024]{1,0:T(8,128)(2,1)}, u32[]{:S(2)}, u32[]{:S(2)}) collective-permute-start(bf16[256,1024]{1,0:T(8,128)(2,1)} %get-tuple-element.77), channel_id=1, source_target_pairs={{0,4},{1,5},{2,6},{3,7},{4,0},{5,1},{6,2},{7,3},{8,12},{9,13},{10,... | collective-permute-start | bytes 1572872 | tf_op jit(solution)/shard_map/ppermute | solution.py:1483
  281.5 104.3 %collective-permute-start.2 = (bf16[256,1024]{1,0:T(8,128)(2,1)}, bf16[256,1024]{1,0:T(8,128)(2,1)}, u32[]{:S(2)}, u32[]{:S(2)}) collective-permute-start(bf16[256,1024]{1,0:T(8,128)(2,1)} %get-tuple-element.78), channel_id=1, source_target_pairs={{0,6},{1,7},{2,0},{3,1},{4,2},{5,3},{6,4},{7,5},{8,14},{9,15},{10,... | collective-permute-start | bytes 1572872 | tf_op jit(solution)/shard_map/ppermute | solution.py:1483
  283.0 102.9 %collective-permute-start.3 = (bf16[256,1024]{1,0:T(8,128)(2,1)}, bf16[256,1024]{1,0:T(8,128)(2,1)}, u32[]{:S(2)}, u32[]{:S(2)}) collective-permute-start(bf16[256,1024]{1,0:T(8,128)(2,1)} %get-tuple-element.81), channel_id=1, source_target_pairs={{0,2},{1,3},{2,4},{3,5},{4,6},{5,7},{6,0},{7,1},{8,10},{9,11},{10,... | collective-permute-start | bytes 1572872 | tf_op jit(solution)/shard_map/ppermute | solution.py:1483
  283.6 102.3 %collective-permute-start.4 = (bf16[256,1024]{1,0:T(8,128)(2,1)}, bf16[256,1024]{1,0:T(8,128)(2,1)}, u32[]{:S(2)}, u32[]{:S(2)}) collective-permute-start(bf16[256,1024]{1,0:T(8,128)(2,1)} %get-tuple-element.82), channel_id=1, source_target_pairs={{0,4},{1,5},{2,6},{3,7},{4,0},{5,1},{6,2},{7,3},{8,12},{9,13},{10,... | collective-permute-start | bytes 1572872 | tf_op jit(solution)/shard_map/ppermute | solution.py:1483
  289.8 96.0 %copy-start.2 = (bf16[256,1024]{1,0:T(8,128)(2,1)}, bf16[256,1024]{1,0:T(8,128)(2,1)S(1)}, u32[]{:S(2)}) copy-start(bf16[256,1024]{1,0:T(8,128)(2,1)S(1)} %collective-permute-done.early_1_) | copy-start | bytes 1572868
  289.8 96.0 %collective-permute-start.5 = (bf16[256,1024]{1,0:T(8,128)(2,1)}, bf16[256,1024]{1,0:T(8,128)(2,1)}, u32[]{:S(2)}, u32[]{:S(2)}) collective-permute-start(bf16[256,1024]{1,0:T(8,128)(2,1)} %get-tuple-element.83), channel_id=1, source_target_pairs={{0,6},{1,7},{2,0},{3,1},{4,2},{5,3},{6,4},{7,5},{8,14},{9,15},{10,... | collective-permute-start | bytes 1572872 | tf_op jit(solution)/shard_map/ppermute | solution.py:1483
  506.1 4.8 copy-start
  510.9 2.0 copy-start.1
Sparse Core Ops, SparseCore 0:
  126.1 61.0 all-gather.1

commit v3 on v2

--- a/solution.py
+++ b/solution.py
@@ -759,7 +759,7 @@
 
 
 def start_kernel(
-    n, source_ref, tokens, grads, shards, small, tok, win, smalls, sent_grad, rows_in, sent, w_held, s_held, here, w_send, w_recv, t_send, t_recv, f_send, f_recv, s_send, s_recv
+    n, source_ref, tokens, grads, shards, small, tok, win, smalls, sent_grad, rows_in, sent, given, w_held, s_held, here, w_send, w_recv, t_send, t_recv, f_send, f_recv, s_send, s_recv
 ):
     me = lax.axis_index("fsdp")
     core = lax.rem(me, 2)
@@ -773,7 +773,7 @@
     for copy in loads:
         copy.start()
 
-    def place_rows(index):
+    def place_rows(index, sent=sent):
         chosen = source_ref[index]
         step = 32
 
@@ -832,20 +832,20 @@
         ).wait_recv()
         if away:
             passed.append(forward(index, block, owner))
+    more.wait()
+
+    @pl.loop(0, n)
+    def _(index):
+        place_rows(index, given)
+
+    back = pltpu.make_async_copy(given, sent_grad, here.at[4])
+    back.start()
     for copy in passed:
         copy.wait()
     for copy in pending:
         copy.wait_send()
     for copy in local:
         copy.wait()
-    more.wait()
-
-    @pl.loop(0, n)
-    def _(index):
-        place_rows(index)
-
-    back = pltpu.make_async_copy(sent, sent_grad, here.at[4])
-    back.start()
     for index, (away, turn) in enumerate(peers_of(n)):
         owner = sender_at(n, me, away, turn)
         checks = [(win.at[rows_at(owner, rows)], w_send, w_recv), (smalls.at[owner], s_send, s_recv)]
@@ -873,7 +873,8 @@
         in_specs=[pl.BlockSpec(memory_space=pltpu.SMEM)] + [anywhere] * 4,
         out_specs=[anywhere] * 4,
         scratch_shapes=[
-            pltpu.VMEM(tokens.shape, BF16), pltpu.VMEM(tokens.shape, BF16), pltpu.VMEM((rows, wide), BF16), pltpu.VMEM(small.shape, BF16),
+            pltpu.VMEM(tokens.shape, BF16), pltpu.VMEM(tokens.shape, BF16), pltpu.VMEM(tokens.shape, BF16),
+            pltpu.VMEM((rows, wide), BF16), pltpu.VMEM(small.shape, BF16),
         ]
         + [pltpu.SemaphoreType.DMA((5,))] + [pltpu.SemaphoreType.DMA((count,))] * 8,
         compiler_params=pltpu.CompilerParams(
@@ -1014,11 +1015,10 @@
     n, planes, cuts, groups, length_ref, place_ref, kept_ref, gn, tok, gain_ref, early, dwin, o_early,
     sums, base, base_grad, branch,
     output, token_grad, w_ref, o_ref, sums_ref,
-    gn_mine, gn_theirs, hidden, grad, dgain, w_own, w_in, o_own, o_in, w_give, w_pair, w_chip, z_in, oz_in, z_out,
-    oz_out, w_all, o_all, s_own, s_in, d_in, s_tot, s_up, back, out_buf, grad_buf, part,
+    gn_mine, gn_theirs, hidden, grad, dgain, w_own, w_in, o_own, o_in, w_give, w_pair, w_chip, w_above, w_half, w_cross,
+    w_all, o_above, o_half, o_cross, o_all, s_own, s_in, d_in, s_tot, s_above, s_half, s_cross, s_all, back, out_buf, grad_buf, part,
     here, g_send, g_recv, b_send, b_recv, w_send, w_recv, o_send, o_recv, p_send, p_recv,
-    z_send, z_recv, oz_send, oz_recv, y_send, y_recv, oy_send, oy_recv, s_send, s_recv, d_send, d_recv,
-    u_send, u_recv,
+    s_send, s_recv, d_send, d_recv, a_send, a_recv, c_send, c_recv, f_send, f_recv,
 ):
     me = lax.axis_index("fsdp")
     level = lax.axis_index("rep")
@@ -1031,7 +1031,9 @@
     chip_rows = w_own.shape[0]
     rows = chip_rows // 2
     outs = o_own.shape[0]
-    zrows, orows = rows // planes, outs // planes
+    middle = (level > 0) & (level < planes - 1)
+    inward = jnp.where(level == 0, 1, planes - 2)
+    outward = jnp.where(level == 1, 0, planes - 1)
     others = n // 2 - 1
     tile = 16
     barrier = pltpu.get_barrier_semaphore()
@@ -1056,8 +1058,61 @@
         copy.start()
         pending.append(copy)
 
-    def above(up):
-        return lax.rem(level + up, planes)
+    chain = []
+
+    def chain_up(k, own, above, half, cross, out, add):
+        chain.append((k, own, above, half, cross, out, add))
+
+        @pl.when(jnp.logical_not(middle))
+        def _():
+            remote(own, above, a_send.at[k], a_recv.at[k], {"rep": inward}).start()
+
+    def chain_cross(k):
+        _, own, above, half, cross, _, add = next(item for item in chain if item[0] == k)
+
+        @pl.when(middle)
+        def _():
+            arrived(above, a_send.at[k], a_recv.at[k])
+            add(half, own, above)
+            remote(half, cross, c_send.at[k], c_recv.at[k], {"rep": planes - 1 - level}).start()
+
+    def chain_out(k):
+        _, _, _, half, cross, out, add = next(item for item in chain if item[0] == k)
+
+        @pl.when(middle)
+        def _():
+            arrived(cross, c_send.at[k], c_recv.at[k])
+            add(out, half, cross)
+            remote(out, out, f_send.at[k], f_recv.at[k], {"rep": outward}).start()
+
+    def chain_end(k):
+        _, own, above, half, cross, out, _ = next(item for item in chain if item[0] == k)
+
+        @pl.when(middle)
+        def _():
+            remote(half, cross, c_send.at[k], c_recv.at[k], {"rep": planes - 1 - level}).wait_send()
+            remote(out, out, f_send.at[k], f_recv.at[k], {"rep": outward}).wait_send()
+
+        @pl.when(jnp.logical_not(middle))
+        def _():
+            remote(own, above, a_send.at[k], a_recv.at[k], {"rep": inward}).wait_send()
+            arrived(out, f_send.at[k], f_recv.at[k])
+
+    def add_wide(out, x, y):
+        @pl.loop(0, rows // 16)
+        def _(i):
+            at = pl.ds(pl.multiple_of(i * 16, 16), 16)
+            for q in range(2):
+                out[q, at, :] = (x[q, at, :].astype(F32) + y[q, at, :].astype(F32)).astype(BF16)
+
+    def add_flat(out, x, y):
+        @pl.loop(0, outs // 16)
+        def _(i):
+            at = pl.ds(pl.multiple_of(i * 16, 16), 16)
+            out[at, :] = (x[at, :].astype(F32) + y[at, :].astype(F32)).astype(BF16)
+
+    def add_small(out, x, y):
+        out[...] = x[...] + y[...]
 
     loads = [
         pltpu.make_async_copy(early[0], w_own.at[:, pl.ds(0, ahead)], here.at[0]),
@@ -1154,28 +1209,10 @@
         cols = cuts[c]
         arrived(w_pair.at[:, cols], p_send.at[c], p_recv.at[c])
         w_chip[1 - core, :, cols] = w_pair[:, cols]
-        for up in range(1, planes):
-            k = c * (planes - 1) + up - 1
-            push(
-                w_chip.at[:, rows_at(above(up), zrows), cols], z_in.at[up - 1, :, :, cols],
-                z_send.at[k], z_recv.at[k], {"rep": above(up)},
-            )
-
-    def stage_total(c):
-        cols = cuts[c]
-        for up in range(1, planes):
-            k = c * (planes - 1) + up - 1
-            arrived(z_in.at[up - 1, :, :, cols], z_send.at[k], z_recv.at[k])
-        at = rows_at(level, zrows)
-        for q in range(2):
-            total = w_chip[q, at, cols].astype(F32)
-            for k in range(planes - 1):
-                total = total + z_in[k, q, :, cols].astype(F32)
-            z_out[q, :, cols] = total.astype(BF16)
-            w_all[q, at, cols] = total.astype(BF16)
-        for up in range(1, planes):
-            k = c * (planes - 1) + up - 1
-            push(z_out.at[:, :, cols], w_all.at[:, at, cols], y_send.at[k], y_recv.at[k], {"rep": above(up)})
+        chain_up(
+            c, w_chip.at[:, :, cols], w_above.at[:, :, cols], w_half.at[:, :, cols], w_cross.at[:, :, cols],
+            w_all.at[:, :, cols], add_wide,
+        )
 
     def finish_rows(buf, pieces, s):
         kept = kept_ref[s]
@@ -1197,11 +1234,8 @@
         at = pl.ds(pl.multiple_of(i * tile, tile), tile)
         o_own[at, :] = add_up(o_own, o_in, at, slice(None))
 
-    for up in range(1, planes):
-        push(
-            o_own.at[rows_at(above(up), orows)], oz_in.at[up - 1], oz_send.at[up - 1], oz_recv.at[up - 1],
-            {"rep": above(up)},
-        )
+    count = len(cuts)
+    chain_up(count, o_own, o_above, o_half, o_cross, o_all, add_flat)
     stage_up(0)
     for copy in loads[3:6]:
         copy.wait()
@@ -1214,6 +1248,8 @@
             peer = peer_at(n, me, away, turn)
             cols = pl.ds(pl.multiple_of(peer * seg, seg), seg)
             push(dgain.at[:, cols], d_in.at[index - 1], d_send.at[index], d_recv.at[index], {"fsdp": peer})
+    chain_cross(count)
+    chain_cross(0)
     s_tot[core] = s_own[...]
     s_tot[1 - core] = jnp.zeros_like(s_own)
     for index, (away, turn) in enumerate(everyone):
@@ -1226,9 +1262,7 @@
     for index in range(n - 1):
         mine = mine + d_in[index]
     s_tot[0, CONV + 3 : CONV + 4, 0:seg] = mine[0:1]
-    for up in range(1, planes):
-        push(s_tot, s_up.at[up - 1], u_send.at[up - 1], u_recv.at[up - 1], {"rep": above(up)})
-    count = len(cuts)
+    chain_up(count + 1, s_tot, s_above, s_half, s_cross, s_all, add_small)
     waiting = list(range(1, n))
     for c in range(1, count):
         stage_sum(c)
@@ -1236,37 +1270,26 @@
             give_back(index)
         del waiting[:2]
         stage_up(c)
-        stage_total(c - 1)
         if c == 1:
-            for i in range(planes - 1):
-                arrived(oz_in.at[i], oz_send.at[i], oz_recv.at[i])
-            at = rows_at(level, orows)
-            total = o_own[at, :].astype(F32)
-            for k in range(planes - 1):
-                total = total + oz_in[k].astype(F32)
-            oz_out[...] = total.astype(BF16)
-            o_all[at, :] = total.astype(BF16)
-            for up in range(1, planes):
-                push(oz_out, o_all.at[at], oy_send.at[up - 1], oy_recv.at[up - 1], {"rep": above(up)})
+            chain_out(count)
+            chain_out(0)
+            chain_cross(count + 1)
+        else:
+            chain_cross(c - 1)
+            chain_out(count + 1 if c == 2 else c - 2)
     for copy in loads[6:9]:
         copy.wait()
     for s in range(n):
         finish_rows(out_buf, part, s)
     stores = [pltpu.make_async_copy(out_buf, output, here.at[6])]
     stores[0].start()
-    stage_total(count - 1)
-
-    for i in range(planes - 1):
-        arrived(s_up.at[i], u_send.at[i], u_recv.at[i])
-    total = s_tot[...]
-    for k in range(planes - 1):
-        total = total + s_up[k]
-    sums_ref[...] = total
-    for c, cols in enumerate(cuts):
-        for up in range(1, planes):
-            below = lax.rem(level + planes - up, planes)
-            k = c * (planes - 1) + up - 1
-            arrived(w_all.at[:, rows_at(below, zrows), cols], y_send.at[k], y_recv.at[k])
+    chain_cross(count - 1)
+    if count > 2:
+        chain_out(count - 2)
+    chain_out(count - 1)
+    for k in range(count + 2):
+        chain_end(k)
+    sums_ref[...] = s_all[...]
     inner, group, heads = groups
     for g in range(2 * inner // group):
         q, at = g % 2, g // 2 * group
@@ -1282,9 +1305,6 @@
     size = group // HEADDIM
     pieces = [tails[g % 2][:, g // 2 * size : (g // 2 + 1) * size] for g in range(2 * inner // group)]
     w_ref[:, 4 * inner + 2 * STATE :] = jnp.concatenate(pieces, axis=1)
-    for up in range(1, planes):
-        below = lax.rem(level + planes - up, planes)
-        arrived(o_all.at[rows_at(below, orows)], oy_send.at[up - 1], oy_recv.at[up - 1])
     o_ref[...] = o_all[...].astype(F32)
     for index, (away, turn) in enumerate(everyone):
         if index:
@@ -1322,7 +1342,6 @@
     vmem = pl.BlockSpec(memory_space=pltpu.VMEM)
     smem = pl.BlockSpec(memory_space=pltpu.SMEM)
     dma = pltpu.SemaphoreType.DMA
-    up = planes - 1
     return pl.pallas_call(
         functools.partial(finish_kernel, n, planes, cuts, (inner, group, heads)),
         out_shape=[
@@ -1341,19 +1360,21 @@
             pltpu.VMEM((chip_rows, wide), BF16), pltpu.VMEM((others, chip_rows, wide), BF16),
             pltpu.VMEM((outs, width), BF16), pltpu.VMEM((others, outs, width), BF16),
             pltpu.VMEM((rows, wide), BF16), pltpu.VMEM((rows, wide), BF16), pltpu.VMEM((2, rows, wide), BF16),
-            pltpu.VMEM((up, 2, rows // planes, wide), BF16), pltpu.VMEM((up, outs // planes, width), BF16),
-            pltpu.VMEM((2, rows // planes, wide), BF16), pltpu.VMEM((outs // planes, width), BF16),
-            pltpu.VMEM((2, rows, wide), BF16), pltpu.VMEM((outs, width), BF16),
+            pltpu.VMEM((2, rows, wide), BF16), pltpu.VMEM((2, rows, wide), BF16), pltpu.VMEM((2, rows, wide), BF16),
+            pltpu.VMEM((2, rows, wide), BF16),
+            pltpu.VMEM((outs, width), BF16), pltpu.VMEM((outs, width), BF16), pltpu.VMEM((outs, width), BF16),
+            pltpu.VMEM((outs, width), BF16),
             pltpu.VMEM(sums.shape, F32), pltpu.VMEM((n - 1,) + sums.shape, F32),
             pltpu.VMEM((n - 1, 8, LANES), F32), pltpu.VMEM((2,) + sums.shape, F32),
-            pltpu.VMEM((up, 2) + sums.shape, F32),
+            pltpu.VMEM((2,) + sums.shape, F32), pltpu.VMEM((2,) + sums.shape, F32),
+            pltpu.VMEM((2,) + sums.shape, F32), pltpu.VMEM((2,) + sums.shape, F32),
             pltpu.VMEM((n, span, width), BF16), pltpu.VMEM((n, span, width), BF16),
             pltpu.VMEM((n, span, width), BF16), pltpu.VMEM((n, span, width), BF16),
             dma((9 + 2 * others,)), dma((n,)), dma((n,)), dma((n,)), dma((n,)),
             dma((pieces * others,)), dma((pieces * others,)), dma((others,)), dma((others,)),
-            dma((pieces,)), dma((pieces,)), dma((pieces * up,)), dma((pieces * up,)), dma((up,)), dma((up,)),
-            dma((pieces * up,)), dma((pieces * up,)), dma((up,)), dma((up,)),
-            dma((n,)), dma((n,)), dma((n,)), dma((n,)), dma((up,)), dma((up,)),
+            dma((pieces,)), dma((pieces,)), dma((n,)), dma((n,)), dma((n,)), dma((n,)),
+            dma((pieces + 2,)), dma((pieces + 2,)), dma((pieces + 2,)), dma((pieces + 2,)),
+            dma((pieces + 2,)), dma((pieces + 2,)),
         ],
         compiler_params=pltpu.CompilerParams(
             collective_id=1, has_side_effects=True, vmem_limit_bytes=60 * 1024 * 1024
@@ -1470,7 +1491,7 @@
     branch = restore(branch)
     parts = n // 2
     planes = lax.axis_size("rep")
-    fused = aligned and rows % (16 * planes) == 0 and out_weight.shape[0] % (16 * planes) == 0
+    fused = aligned and planes == 4 and rows % (16 * planes) == 0 and out_weight.shape[0] % (16 * planes) == 0
     chip = (me // 2 if fused else me * 0).reshape(1)
     dy, gp, dog, *early = gate_call(
         grid_steps, chip_blocks, chip_lens, chip, parts, tok, cot, gain, win, gm, og, gate, y, rv

time: 520 us -> 517 us (level)
  Pallas kernels: 439 us -> 419 us
  starting transfers between devices: 14.3 us -> 23.5 us
    pallas_call x1, Pallas kernels: 96 us -> 87.5 us  [bwd_call(): pl.pallas_call(functools.partial(bwd_kernel, inner, heads), grid_spec=gri...]
    all_to_all x1, starting transfers between devices: 4.55 us -> 11.1 us  [restore(): lax.all_to_all(part.reshape(n, span, width), 'fsdp', split_axis=0, concat...]
  transfers between devices with their start and end apart: 9 -> 9, of which waited for: 2 -> 2; matrix products, arithmetic and copies ran while one was open for 1% -> 1% of each run, Pallas kernels for 29% -> 27%
where the time goes in v3:
time: 517 us; the launch traced here: 514 us
  Pallas kernels  419 us (81%)
  local copies, waits for them, and re-layouts  29.6 us (6%)
  starting transfers between devices  23.5 us (5%)
  waiting for transfers between devices  20.7 us (4%)
  between operations  14.5 us (3%)
  other arithmetic  6.01 us (1%)
    pallas_call x1, Pallas kernels, finish_call(): pl.pallas_call(functools.partial(finish_kernel, n, planes, cuts, (inner,...  110 us
    pallas_call x1, Pallas kernels, start_call(): pl.pallas_call(functools.partial(start_kernel, n), out_shape=[jax.ShapeDt...  105 us
    pallas_call x1, Pallas kernels, bwd_call(): pl.pallas_call(functools.partial(bwd_kernel, inner, heads), grid_spec=gri...  87.5 us
    pallas_call x1, Pallas kernels, fwd_call(): pl.pallas_call(functools.partial(fwd_kernel, inner, heads), grid_spec=gri...  43.6 us
    pallas_call x1, Pallas kernels, gate_call(): pl.pallas_call(functools.partial(gate_kernel, parts), grid_spec=pltpu.Pre...  35.7 us
    pallas_call x1, Pallas kernels, mid_call(): pl.pallas_call(mid_kernel, grid_spec=pltpu.PrefetchScalarGridSpec(num_sca...  17.9 us
    all_to_all x1, waiting for transfers between devices, body(): lax.all_to_all(sent_grad, 'fsdp', split_axis=0, concat_axis=0, tiled=True)  16.3 us
    unnamed x23, local copies, waits for them, and re-layouts  11.5 us
  transfers between devices with their start and end apart: 9, of which 2 were waited for; matrix products, arithmetic and copies ran while one was open for 1% of the time, Pallas kernels for 27%

profile of v3, /device:TPU:0, one launch (start us, length us, event | category | flops | bytes accessed | tf_op | source)
XLA Modules:
  0.0 513.7 jit_solution(6313914678008937482)
XLA Ops:
  7.2 0.7 slice.131
  7.9 0.8 slice.130
  8.8 1.3 fusion.9
  10.0 0.9 select_reduce_fusion.2
  11.1 0.5 copy-done.4
  11.6 0.6 select_reduce_fusion
  12.2 0.8 reshape.121
  13.0 2.1 concatenate.39
  15.1 0.6 pad_bitcast_fusion.small
  16.8 0.3 concatenate.38
  17.1 0.3 concatenate.37
  17.3 1.2 pad_maximum_fusion.shards
  18.5 105.3 %start.1 = (bf16[2,2048,1024]{2,1,0:T(8,128)(2,1)}, bf16[1024,2432]{1,0:T(8,128)(2,1)}, bf16[8,16,128]{2,1,0:T(8,128)(2,1)}, bf16[8,256,1024]{2,1,0:T(8,128)(2,1)}) custom-call(s32[8]{0:T(128)} %get-tuple-element.130.source_ref, bf16[8,256,1024]{2,1,0:T(8,128)(2,1)} %bitcast.54, bf16[8,256,1024]{2,1,0:T(8,128)(2,1)} %bitcast.56, ...), custom_call_target="tpu_custom_call" | custom-call | tf_op jit(solution)/shard_map/start/pallas_call | solution.py:865
  123.9 4.7 all-to-all-start
  129.2 0.6 slice.174
  130.8 0.6 concatenate.42.hp_ref
  131.7 0.7 broadcast_in_dim.59.dwide_ref
  132.3 0.6 and_select_fusion
  132.9 0.6 fusion.6.og_ref
  133.6 0.6 fusion.4.cb_ref
  134.2 0.6 pad_maximum_fusion.1.cw_ref
  134.8 43.6 %layer_forward.1 = (f32[2,2048,1024]{2,1,0:T(8,128)}, f32[2,2048,1280]{2,1,0:T(8,128)}, f32[2,2048,128]{2,1,0:T(8,128)}, f32[2,2048,1024]{2,1,0:T(8,128)}, f32[2...) custom-call(s32[2]{0:T(128)} %get-tuple-element.132.nb_ref, ...), custom_call_target="tpu_custom_call" | custom-call | flops 14562623488 | bytes 62914560 | tf_op jit(solution)/shard_map/layer_forward/pallas_call | solution.py:269
  178.3 16.3 %all-to-all-done = bf16[8,256,1024]{2,1,0:T(8,128)(2,1)} async-done(((bf16[8,256,1024]{2,1,0:T(8,128)(2,1)}), bf16[8,256,1024]{2,1,0:T(8,128)(2,1)}, u32[]{:S(2)}, u32[]{:S(2)}) %all-to-all-start) | async-done | bytes 4194336 | tf_op jit(solution)/shard_map/all_to_all | solution.py:1454
  194.6 8.5 %pair.1.cot_ref = bf16[2,2048,1024]{2,1,0:T(8,128)(2,1)} custom-call(bf16[2048,1024]{1,0:T(8,128)(2,1)} %bitcast.25.mine), custom_call_target="tpu_custom_call" | custom-call | tf_op jit(solution)/shard_map/pair/pallas_call | solution.py:998
  203.1 17.9 %layer_middle.1 = (f32[2,2048,1024]{2,1,0:T(8,128)}, f32[128,256]{1,0:T(8,128)}, bf16[2,2048,1024]{2,1,0:T(8,128)(2,1)}) custom-call(s32[2]{0:T(128)} %get-tuple-element.132.nb_ref, s32[2]{0:T(128)} %get-tuple-element.133.len_ref, bf16[2,2048,1024]{2,1,0:T(8,128)(2,1)} %pair.1.cot_ref, bf16[2,2048,1024]{2,1,0:T(8,128)(2,1)} %get-tuple-element.59.sc_ref, ...), custom_call_target="tpu_custom_call" | custom-call | flops 10000000000 | bytes 31457280 | tf_op jit(solution)/shard_map/layer_middle/pallas_call | solution.py:316
  221.0 10.7 %exchange.1 = (bf16[2048,1024]{1,0:T(8,128)(2,1)}, f32[128,256]{1,0:T(8,128)}) custom-call(bf16[2,2048,1024]{2,1,0:T(8,128)(2,1)} %get-tuple-element.64.bp, f32[128,256]{1,0:T(8,128)} %get-tuple-element.65.ss_ref, f32[128,256]{1,0:T(8,128)} %get-tuple-element.66.v_ref), custom_call_target="tpu_custom_call" | custom-call | tf_op jit(solution)/shard_map/exchange/pallas_call | solution.py:944
  231.7 35.7 %layer_gate.1 = (f32[2,2048,1024]{2,1,0:T(8,128)}, bf16[2,2048,1024]{2,1,0:T(8,128)(2,1)}, f32[8,1024]{1,0:T(8,128)}, bf16[256,1024]{1,0:T(8,128)(2,1)}, bf16[25...) custom-call(s32[2]{0:T(128)} %get-tuple-element.132.nb_ref, ...), custom_call_target="tpu_custom_call" | custom-call | flops 20000000000 | bytes 62914560 | tf_op jit(solution)/shard_map/layer_gate/pallas_call | solution.py:415
  267.6 0.6 dynamic_slice.27.length_ref
  268.1 0.5 subtract_clamp_fusion.kept_ref
  268.7 11.1 %all-to-all-start.1 = ((bf16[8,256,1024]{2,1,0:T(8,128)(2,1)}), bf16[8,256,1024]{2,1,0:T(8,128)(2,1)}, u32[]{:S(2)}, u32[]{:S(2)}) async-start(bf16[8,256,1024]{2,1,0:T(8,128)(2,1)} %bitcast.58), calls=%async_computation.1 | async-start | bytes 8388608 | tf_op jit(solution)/shard_map/all_to_all | solution.py:1488
  279.8 3.3 collective-permute-start.1
  283.3 1.9 collective-permute-start.3
  285.4 4.4 collective-permute-done.early_1_
  289.8 2.0 collective-permute-start.5
  291.8 87.5 %layer_backward.1 = (bf16[2,2048,1024]{2,1,0:T(8,128)(2,1)}, bf16[1024,1408]{1,0:T(8,128)(2,1)}, f32[8,1280]{1,0:T(8,128)}) custom-call(s32[2]{0:T(128)} %get-tuple-element.132.nb_ref, bf16[2,2048,1024]{2,1,0:T(8,128)(2,1)} %get-tuple-element.53.tok_ref.tok, f32[1,1024]{1,0:T(1,128)} %bitcast.82, bf16[1024,2432]{1,0:T(8,128)(2,1)} %get-tuple-element.55.win_ref.wgate_ref, ...), custom_call_target="tpu_custom_call" | custom-call | flops 99999997952 | bytes 104857600 | tf_op jit(solution)/shard_map/layer_backward/pallas_call | solution.py:683
  379.4 110.1 %finish.1 = (bf16[8,256,1024]{2,1,0:T(8,128)(2,1)}, bf16[8,256,1024]{2,1,0:T(8,128)(2,1)}, f32[128,4384]{1,0:T(8,128)}, f32[256,1024]{1,0:T(8,128)}, f32[2,8,1280]{2,1,0:T(8,128)}) custom-call(s32[1]{0:T(128)} %dynamic_slice.27.length_ref, s32[8]{0:T(128)} %copy-done.4, s32[8]{0:T(128)} %subtract_clamp_fusion.kept_ref, ...), custom_call_target="tpu_custom_call" | custom-call | tf_op jit(solution)/shard_map/finish/pallas_call | solution.py:1345
  489.5 1.2 slice_bitcast_fusion.2
  490.7 0.8 slice_bitcast_fusion.1
  491.8 0.6 slice_reduce_fusion.1
  492.4 0.6 slice.193
  493.3 0.6 squeeze_reshape.9
  494.0 0.6 squeeze_reshape.10
  494.7 0.6 squeeze_reshape.11
  495.4 3.0 copy.78
  498.4 0.6 dynamic_slice.33
  499.0 4.8 copy.97
  503.8 2.0 copy.98
  505.9 1.0 copy.99
  (99 shorter events, 4.3 us)
Async XLA Ops:
  7.2 196.0 %all-gather.2.cloned.1.call-start = ((), (), s32[]{:S(2)}) async-start(), calls=%async_computation.2 | async-start | bytes 2621440 | tf_op jit(solution)/shard_map/all_gather | solution.py:1456
  11.1 0.5 copy-start.4
  123.9 4.8 copy-start.3
  123.9 6.0 %copy-start.7 = (f32[32]{0:T(128)S(1)}, f32[32]{0:T(128)}, u32[]{:S(2)}) copy-start(f32[32]{0:T(128)} %param.22) | copy-start | bytes 388
  123.9 6.1 %copy-start.5 = (f32[32]{0:T(128)S(1)}, f32[32]{0:T(128)}, u32[]{:S(2)}) copy-start(f32[32]{0:T(128)} %param.21) | copy-start | bytes 388
  123.9 6.1 %copy-start.6 = (f32[32]{0:T(128)S(1)}, f32[32]{0:T(128)}, u32[]{:S(2)}) copy-start(f32[32]{0:T(128)} %param.23) | copy-start | bytes 388
  123.9 70.7 %all-to-all-start = ((bf16[8,256,1024]{2,1,0:T(8,128)(2,1)}), bf16[8,256,1024]{2,1,0:T(8,128)(2,1)}, u32[]{:S(2)}, u32[]{:S(2)}) async-start(bf16[8,256,1024]{2,1,0:T(8,128)(2,1)} %get-tuple-element.56), calls=%async_computation | async-start | bytes 8388608 | tf_op jit(solution)/shard_map/all_to_all | solution.py:1454
  267.5 22.3 %collective-permute-start = (bf16[256,1024]{1,0:T(8,128)(2,1)}, bf16[256,1024]{1,0:T(8,128)(2,1)S(1)}, u32[]{:S(2)}, u32[]{:S(2)}) collective-permute-start(bf16[256,1024]{1,0:T(8,128)(2,1)} %get-tuple-element.76), channel_id=1, source_target_pairs={{0,2},{1,3},{2,4},{3,5},{4,6},{5,7},{6,0},{7,1},{8,10},{9,11},{10,... | collective-permute-start | bytes 1572872 | tf_op jit(solution)/shard_map/ppermute | solution.py:1504
  268.7 110.7 %all-to-all-start.1 = ((bf16[8,256,1024]{2,1,0:T(8,128)(2,1)}), bf16[8,256,1024]{2,1,0:T(8,128)(2,1)}, u32[]{:S(2)}, u32[]{:S(2)}) async-start(bf16[8,256,1024]{2,1,0:T(8,128)(2,1)} %bitcast.58), calls=%async_computation.1 | async-start | bytes 8388608 | tf_op jit(solution)/shard_map/all_to_all | solution.py:1488
  279.8 99.5 %collective-permute-start.1 = (bf16[256,1024]{1,0:T(8,128)(2,1)}, bf16[256,1024]{1,0:T(8,128)(2,1)}, u32[]{:S(2)}, u32[]{:S(2)}) collective-permute-start(bf16[256,1024]{1,0:T(8,128)(2,1)} %get-tuple-element.77), channel_id=1, source_target_pairs={{0,4},{1,5},{2,6},{3,7},{4,0},{5,1},{6,2},{7,3},{8,12},{9,13},{10,... | collective-permute-start | bytes 1572872 | tf_op jit(solution)/shard_map/ppermute | solution.py:1504
  283.1 96.2 %collective-permute-start.2 = (bf16[256,1024]{1,0:T(8,128)(2,1)}, bf16[256,1024]{1,0:T(8,128)(2,1)}, u32[]{:S(2)}, u32[]{:S(2)}) collective-permute-start(bf16[256,1024]{1,0:T(8,128)(2,1)} %get-tuple-element.78), channel_id=1, source_target_pairs={{0,6},{1,7},{2,0},{3,1},{4,2},{5,3},{6,4},{7,5},{8,14},{9,15},{10,... | collective-permute-start | bytes 1572872 | tf_op jit(solution)/shard_map/ppermute | solution.py:1504
  283.3 96.1 %collective-permute-start.3 = (bf16[256,1024]{1,0:T(8,128)(2,1)}, bf16[256,1024]{1,0:T(8,128)(2,1)}, u32[]{:S(2)}, u32[]{:S(2)}) collective-permute-start(bf16[256,1024]{1,0:T(8,128)(2,1)} %get-tuple-element.81), channel_id=1, source_target_pairs={{0,2},{1,3},{2,4},{3,5},{4,6},{5,7},{6,0},{7,1},{8,10},{9,11},{10,... | collective-permute-start | bytes 1572872 | tf_op jit(solution)/shard_map/ppermute | solution.py:1504
  285.1 94.2 %collective-permute-start.4 = (bf16[256,1024]{1,0:T(8,128)(2,1)}, bf16[256,1024]{1,0:T(8,128)(2,1)}, u32[]{:S(2)}, u32[]{:S(2)}) collective-permute-start(bf16[256,1024]{1,0:T(8,128)(2,1)} %get-tuple-element.82), channel_id=1, source_target_pairs={{0,4},{1,5},{2,6},{3,7},{4,0},{5,1},{6,2},{7,3},{8,12},{9,13},{10,... | collective-permute-start | bytes 1572872 | tf_op jit(solution)/shard_map/ppermute | solution.py:1504
  289.8 89.5 %copy-start.2 = (bf16[256,1024]{1,0:T(8,128)(2,1)}, bf16[256,1024]{1,0:T(8,128)(2,1)S(1)}, u32[]{:S(2)}) copy-start(bf16[256,1024]{1,0:T(8,128)(2,1)S(1)} %collective-permute-done.early_1_) | copy-start | bytes 1572868
  289.8 89.5 %collective-permute-start.5 = (bf16[256,1024]{1,0:T(8,128)(2,1)}, bf16[256,1024]{1,0:T(8,128)(2,1)}, u32[]{:S(2)}, u32[]{:S(2)}) collective-permute-start(bf16[256,1024]{1,0:T(8,128)(2,1)} %get-tuple-element.83), channel_id=1, source_target_pairs={{0,6},{1,7},{2,0},{3,1},{4,2},{5,3},{6,4},{7,5},{8,14},{9,15},{10,... | collective-permute-start | bytes 1572872 | tf_op jit(solution)/shard_map/ppermute | solution.py:1504
  499.0 4.8 copy-start
  503.8 2.0 copy-start.1
Sparse Core Ops, SparseCore 0:
  124.0 61.1 all-gather.1

commit v4 on v3

--- a/solution.py
+++ b/solution.py
@@ -1263,12 +1263,10 @@
         mine = mine + d_in[index]
     s_tot[0, CONV + 3 : CONV + 4, 0:seg] = mine[0:1]
     chain_up(count + 1, s_tot, s_above, s_half, s_cross, s_all, add_small)
-    waiting = list(range(1, n))
+    for index in range(1, n):
+        give_back(index)
     for c in range(1, count):
         stage_sum(c)
-        for index in waiting[: 2 if c < count - 1 else n]:
-            give_back(index)
-        del waiting[:2]
         stage_up(c)
         if c == 1:
             chain_out(count)

time: 517 us -> 503 us (0.973)
  starting transfers between devices: 23.5 us -> 14.5 us
    all_to_all x1, starting transfers between devices: 11.1 us -> 4.55 us  [restore(): lax.all_to_all(part.reshape(n, span, width), 'fsdp', split_axis=0, concat...]
  transfers between devices with their start and end apart: 9 -> 9, of which waited for: 2 -> 2; matrix products, arithmetic and copies ran while one was open for 1% -> 1% of each run, Pallas kernels for 27% -> 28%
where the time goes in v4:
time: 503 us
  Pallas kernels  417 us (83%)
  local copies, waits for them, and re-layouts  29.6 us (6%)
  waiting for transfers between devices  21.5 us (4%)
  starting transfers between devices  14.5 us (3%)
  between operations  14.5 us (3%)
  other arithmetic  6.01 us (1%)
    pallas_call x1, Pallas kernels, finish_call(): pl.pallas_call(functools.partial(finish_kernel, n, planes, cuts, (inner,...  108 us
    pallas_call x1, Pallas kernels, start_call(): pl.pallas_call(functools.partial(start_kernel, n), out_shape=[jax.ShapeDt...  105 us
    pallas_call x1, Pallas kernels, bwd_call(): pl.pallas_call(functools.partial(bwd_kernel, inner, heads), grid_spec=gri...  87.5 us
    pallas_call x1, Pallas kernels, fwd_call(): pl.pallas_call(functools.partial(fwd_kernel, inner, heads), grid_spec=gri...  43.6 us
    pallas_call x1, Pallas kernels, gate_call(): pl.pallas_call(functools.partial(gate_kernel, parts), grid_spec=pltpu.Pre...  35.7 us
    pallas_call x1, Pallas kernels, mid_call(): pl.pallas_call(mid_kernel, grid_spec=pltpu.PrefetchScalarGridSpec(num_sca...  17.9 us
    all_to_all x1, waiting for transfers between devices, body(): lax.all_to_all(sent_grad, 'fsdp', split_axis=0, concat_axis=0, tiled=True)  16.3 us
    unnamed x23, local copies, waits for them, and re-layouts  11.5 us
  transfers between devices with their start and end apart: 9, of which 2 were waited for; matrix products, arithmetic and copies ran while one was open for 1% of the time, Pallas kernels for 28%

profile of v4, /device:TPU:0, one launch (start us, length us, event | category | flops | bytes accessed | tf_op | source)
XLA Modules:
  0.0 502.7 jit_solution(16795625567698931759)
XLA Ops:
  7.2 0.7 slice.131
  7.9 0.8 slice.130
  8.8 1.3 fusion.9
  10.0 0.9 select_reduce_fusion.2
  11.1 0.5 copy-done.4
  11.6 0.6 select_reduce_fusion
  12.2 0.8 reshape.121
  13.0 2.1 concatenate.39
  15.1 0.6 pad_bitcast_fusion.small
  17.3 1.2 pad_maximum_fusion.shards
  18.5 105.3 %start.1 = (bf16[2,2048,1024]{2,1,0:T(8,128)(2,1)}, bf16[1024,2432]{1,0:T(8,128)(2,1)}, bf16[8,16,128]{2,1,0:T(8,128)(2,1)}, bf16[8,256,1024]{2,1,0:T(8,128)(2,1)}) custom-call(s32[8]{0:T(128)} %get-tuple-element.130.source_ref, bf16[8,256,1024]{2,1,0:T(8,128)(2,1)} %bitcast.54, bf16[8,256,1024]{2,1,0:T(8,128)(2,1)} %bitcast.56, ...), custom_call_target="tpu_custom_call" | custom-call | tf_op jit(solution)/shard_map/start/pallas_call | solution.py:865
  123.9 4.7 all-to-all-start
  129.2 0.6 slice.174
  130.8 0.6 concatenate.42.hp_ref
  131.7 0.7 broadcast_in_dim.59.dwide_ref
  132.3 0.6 and_select_fusion
  132.9 0.6 fusion.6.og_ref
  133.6 0.6 fusion.4.cb_ref
  134.2 0.6 pad_maximum_fusion.1.cw_ref
  134.8 43.6 %layer_forward.1 = (f32[2,2048,1024]{2,1,0:T(8,128)}, f32[2,2048,1280]{2,1,0:T(8,128)}, f32[2,2048,128]{2,1,0:T(8,128)}, f32[2,2048,1024]{2,1,0:T(8,128)}, f32[2...) custom-call(s32[2]{0:T(128)} %get-tuple-element.132.nb_ref, ...), custom_call_target="tpu_custom_call" | custom-call | flops 14562623488 | bytes 62914560 | tf_op jit(solution)/shard_map/layer_forward/pallas_call | solution.py:269
  178.3 16.3 %all-to-all-done = bf16[8,256,1024]{2,1,0:T(8,128)(2,1)} async-done(((bf16[8,256,1024]{2,1,0:T(8,128)(2,1)}), bf16[8,256,1024]{2,1,0:T(8,128)(2,1)}, u32[]{:S(2)}, u32[]{:S(2)}) %all-to-all-start) | async-done | bytes 4194336 | tf_op jit(solution)/shard_map/all_to_all | solution.py:1452
  194.6 8.5 %pair.1.cot_ref = bf16[2,2048,1024]{2,1,0:T(8,128)(2,1)} custom-call(bf16[2048,1024]{1,0:T(8,128)(2,1)} %bitcast.25.mine), custom_call_target="tpu_custom_call" | custom-call | tf_op jit(solution)/shard_map/pair/pallas_call | solution.py:998
  203.1 17.9 %layer_middle.1 = (f32[2,2048,1024]{2,1,0:T(8,128)}, f32[128,256]{1,0:T(8,128)}, bf16[2,2048,1024]{2,1,0:T(8,128)(2,1)}) custom-call(s32[2]{0:T(128)} %get-tuple-element.132.nb_ref, s32[2]{0:T(128)} %get-tuple-element.133.len_ref, bf16[2,2048,1024]{2,1,0:T(8,128)(2,1)} %pair.1.cot_ref, bf16[2,2048,1024]{2,1,0:T(8,128)(2,1)} %get-tuple-element.59.sc_ref, ...), custom_call_target="tpu_custom_call" | custom-call | flops 10000000000 | bytes 31457280 | tf_op jit(solution)/shard_map/layer_middle/pallas_call | solution.py:316
  221.0 10.7 %exchange.1 = (bf16[2048,1024]{1,0:T(8,128)(2,1)}, f32[128,256]{1,0:T(8,128)}) custom-call(bf16[2,2048,1024]{2,1,0:T(8,128)(2,1)} %get-tuple-element.64.bp, f32[128,256]{1,0:T(8,128)} %get-tuple-element.65.ss_ref, f32[128,256]{1,0:T(8,128)} %get-tuple-element.66.v_ref), custom_call_target="tpu_custom_call" | custom-call | tf_op jit(solution)/shard_map/exchange/pallas_call | solution.py:944
  231.7 35.7 %layer_gate.1 = (f32[2,2048,1024]{2,1,0:T(8,128)}, bf16[2,2048,1024]{2,1,0:T(8,128)(2,1)}, f32[8,1024]{1,0:T(8,128)}, bf16[256,1024]{1,0:T(8,128)(2,1)}, bf16[25...) custom-call(s32[2]{0:T(128)} %get-tuple-element.132.nb_ref, ...), custom_call_target="tpu_custom_call" | custom-call | flops 20000000000 | bytes 62914560 | tf_op jit(solution)/shard_map/layer_gate/pallas_call | solution.py:415
  267.5 0.3 collective-permute-start
  267.8 0.6 dynamic_slice.27.length_ref
  268.4 0.5 subtract_clamp_fusion.kept_ref
  268.9 4.6 all-to-all-start.1
  273.4 1.9 collective-permute-start.1
  275.4 1.4 collective-permute-start.2
  276.8 0.6 collective-permute-start.3
  277.4 0.9 collective-permute-start.4
  278.3 5.1 %collective-permute-done.early_1_ = bf16[256,1024]{1,0:T(8,128)(2,1)S(1)} collective-permute-done((bf16[256,1024]{1,0:T(8,128)(2,1)}, bf16[256,1024]{1,0:T(8,128)(2,1)S(1)}, u32[]{:S(2)}, u32[]{:S(2)}) %collective-permute-start) | collective-permute-done | bytes 524320 | tf_op jit(solution)/shard_map/ppermute | solution.py:1502
  283.4 87.5 %layer_backward.1 = (bf16[2,2048,1024]{2,1,0:T(8,128)(2,1)}, bf16[1024,1408]{1,0:T(8,128)(2,1)}, f32[8,1280]{1,0:T(8,128)}) custom-call(s32[2]{0:T(128)} %get-tuple-element.132.nb_ref, bf16[2,2048,1024]{2,1,0:T(8,128)(2,1)} %get-tuple-element.53.tok_ref.tok, f32[1,1024]{1,0:T(1,128)} %bitcast.82, bf16[1024,2432]{1,0:T(8,128)(2,1)} %get-tuple-element.55.win_ref.wgate_ref, ...), custom_call_target="tpu_custom_call" | custom-call | flops 99999997952 | bytes 104857600 | tf_op jit(solution)/shard_map/layer_backward/pallas_call | solution.py:683
  371.0 107.5 %finish.1 = (bf16[8,256,1024]{2,1,0:T(8,128)(2,1)}, bf16[8,256,1024]{2,1,0:T(8,128)(2,1)}, f32[128,4384]{1,0:T(8,128)}, f32[256,1024]{1,0:T(8,128)}, f32[2,8,1280]{2,1,0:T(8,128)}) custom-call(s32[1]{0:T(128)} %dynamic_slice.27.length_ref, s32[8]{0:T(128)} %copy-done.4, s32[8]{0:T(128)} %subtract_clamp_fusion.kept_ref, ...), custom_call_target="tpu_custom_call" | custom-call | tf_op jit(solution)/shard_map/finish/pallas_call | solution.py:1343
  478.5 1.2 slice_bitcast_fusion.2
  479.7 0.8 slice_bitcast_fusion.1
  480.8 0.6 slice_reduce_fusion.1
  481.4 0.6 slice.193
  482.4 0.6 squeeze_reshape.9
  483.1 0.6 squeeze_reshape.10
  483.8 0.6 squeeze_reshape.11
  484.4 3.0 copy.78
  487.4 0.6 dynamic_slice.33
  488.1 4.8 copy.97
  492.9 2.0 copy.98
  494.9 1.0 copy.99
  (99 shorter events, 4.4 us)
Async XLA Ops:
  7.2 196.0 %all-gather.2.cloned.1.call-start = ((), (), s32[]{:S(2)}) async-start(), calls=%async_computation.2 | async-start | bytes 2621440 | tf_op jit(solution)/shard_map/all_gather | solution.py:1454
  11.1 0.5 copy-start.4
  123.9 4.8 copy-start.3
  123.9 6.0 %copy-start.7 = (f32[32]{0:T(128)S(1)}, f32[32]{0:T(128)}, u32[]{:S(2)}) copy-start(f32[32]{0:T(128)} %param.22) | copy-start | bytes 388
  123.9 6.1 %copy-start.5 = (f32[32]{0:T(128)S(1)}, f32[32]{0:T(128)}, u32[]{:S(2)}) copy-start(f32[32]{0:T(128)} %param.21) | copy-start | bytes 388
  123.9 6.1 %copy-start.6 = (f32[32]{0:T(128)S(1)}, f32[32]{0:T(128)}, u32[]{:S(2)}) copy-start(f32[32]{0:T(128)} %param.23) | copy-start | bytes 388
  123.9 70.7 %all-to-all-start = ((bf16[8,256,1024]{2,1,0:T(8,128)(2,1)}), bf16[8,256,1024]{2,1,0:T(8,128)(2,1)}, u32[]{:S(2)}, u32[]{:S(2)}) async-start(bf16[8,256,1024]{2,1,0:T(8,128)(2,1)} %get-tuple-element.56), calls=%async_computation | async-start | bytes 8388608 | tf_op jit(solution)/shard_map/all_to_all | solution.py:1452
  267.5 16.0 %collective-permute-start = (bf16[256,1024]{1,0:T(8,128)(2,1)}, bf16[256,1024]{1,0:T(8,128)(2,1)S(1)}, u32[]{:S(2)}, u32[]{:S(2)}) collective-permute-start(bf16[256,1024]{1,0:T(8,128)(2,1)} %get-tuple-element.76), channel_id=1, source_target_pairs={{0,2},{1,3},{2,4},{3,5},{4,6},{5,7},{6,0},{7,1},{8,10},{9,11},{10,... | collective-permute-start | bytes 1572872 | tf_op jit(solution)/shard_map/ppermute | solution.py:1502
  268.9 102.1 %all-to-all-start.1 = ((bf16[8,256,1024]{2,1,0:T(8,128)(2,1)}), bf16[8,256,1024]{2,1,0:T(8,128)(2,1)}, u32[]{:S(2)}, u32[]{:S(2)}) async-start(bf16[8,256,1024]{2,1,0:T(8,128)(2,1)} %bitcast.58), calls=%async_computation.1 | async-start | bytes 8388608 | tf_op jit(solution)/shard_map/all_to_all | solution.py:1486
  273.4 97.5 %collective-permute-start.1 = (bf16[256,1024]{1,0:T(8,128)(2,1)}, bf16[256,1024]{1,0:T(8,128)(2,1)}, u32[]{:S(2)}, u32[]{:S(2)}) collective-permute-start(bf16[256,1024]{1,0:T(8,128)(2,1)} %get-tuple-element.77), channel_id=1, source_target_pairs={{0,4},{1,5},{2,6},{3,7},{4,0},{5,1},{6,2},{7,3},{8,12},{9,13},{10,... | collective-permute-start | bytes 1572872 | tf_op jit(solution)/shard_map/ppermute | solution.py:1502
  275.4 95.6 %collective-permute-start.2 = (bf16[256,1024]{1,0:T(8,128)(2,1)}, bf16[256,1024]{1,0:T(8,128)(2,1)}, u32[]{:S(2)}, u32[]{:S(2)}) collective-permute-start(bf16[256,1024]{1,0:T(8,128)(2,1)} %get-tuple-element.78), channel_id=1, source_target_pairs={{0,6},{1,7},{2,0},{3,1},{4,2},{5,3},{6,4},{7,5},{8,14},{9,15},{10,... | collective-permute-start | bytes 1572872 | tf_op jit(solution)/shard_map/ppermute | solution.py:1502
  276.8 94.2 %collective-permute-start.3 = (bf16[256,1024]{1,0:T(8,128)(2,1)}, bf16[256,1024]{1,0:T(8,128)(2,1)}, u32[]{:S(2)}, u32[]{:S(2)}) collective-permute-start(bf16[256,1024]{1,0:T(8,128)(2,1)} %get-tuple-element.81), channel_id=1, source_target_pairs={{0,2},{1,3},{2,4},{3,5},{4,6},{5,7},{6,0},{7,1},{8,10},{9,11},{10,... | collective-permute-start | bytes 1572872 | tf_op jit(solution)/shard_map/ppermute | solution.py:1502
  277.4 93.6 %collective-permute-start.4 = (bf16[256,1024]{1,0:T(8,128)(2,1)}, bf16[256,1024]{1,0:T(8,128)(2,1)}, u32[]{:S(2)}, u32[]{:S(2)}) collective-permute-start(bf16[256,1024]{1,0:T(8,128)(2,1)} %get-tuple-element.82), channel_id=1, source_target_pairs={{0,4},{1,5},{2,6},{3,7},{4,0},{5,1},{6,2},{7,3},{8,12},{9,13},{10,... | collective-permute-start | bytes 1572872 | tf_op jit(solution)/shard_map/ppermute | solution.py:1502
  283.4 87.5 %copy-start.2 = (bf16[256,1024]{1,0:T(8,128)(2,1)}, bf16[256,1024]{1,0:T(8,128)(2,1)S(1)}, u32[]{:S(2)}) copy-start(bf16[256,1024]{1,0:T(8,128)(2,1)S(1)} %collective-permute-done.early_1_) | copy-start | bytes 1572868
  283.4 87.5 %collective-permute-start.5 = (bf16[256,1024]{1,0:T(8,128)(2,1)}, bf16[256,1024]{1,0:T(8,128)(2,1)}, u32[]{:S(2)}, u32[]{:S(2)}) collective-permute-start(bf16[256,1024]{1,0:T(8,128)(2,1)} %get-tuple-element.83), channel_id=1, source_target_pairs={{0,6},{1,7},{2,0},{3,1},{4,2},{5,3},{6,4},{7,5},{8,14},{9,15},{10,... | collective-permute-start | bytes 1572872 | tf_op jit(solution)/shard_map/ppermute | solution.py:1502
  488.1 4.8 copy-start
  492.9 2.0 copy-start.1
Sparse Core Ops, SparseCore 0:
  124.0 61.1 all-gather.1
